TPU v7x, 128 devices: a whole 4x4x4 slice. The times are simulated.
128 devices in a mesh: store: 8 (over z, core), scorer: 16 (over y, x).
Axes of the slice: x: 4, y: 4, z: 4, core: 2. Of those that a mesh axis runs over, the one named last changes fastest.
Arguments:
- store_rows: bfloat16 [262144, 256], P(('store', 'scorer')), may hold values from -11 to 11
- cluster_logsize: bfloat16 [262144], P(('store', 'scorer')), may hold values from 0 to 318
- cluster_home: int32 [262144], replicated, may hold values from 0 to 262143, as said below
- cluster_ids: int32 [1024, 512], P(('store', 'scorer')), may hold values from 0 to 262143, as said below
- valid_count: int32 [1024], P(('store', 'scorer')), may hold values from 64 to 512
- candidates: bfloat16 [1024, 512, 256], P(('store', 'scorer')), may hold values from -11 to 11
- cand_count: int32 [1024], P(('store', 'scorer')), may hold values from 0 to 512, as said below
- candidate_row: int32 [1024, 512], P(('store', 'scorer')), may hold values from 0 to 32767, as said below
- query_proj: bfloat16 [256, 256], replicated, may hold values from -0.375 to 0.375
- key_proj: bfloat16 [256, 256], replicated, may hold values from -0.375 to 0.375
- value_proj: bfloat16 [256, 256], replicated, may hold values from -0.375 to 0.375
- out_proj: bfloat16 [256, 256], replicated, may hold values from -0.375 to 0.375
- mlp_first: bfloat16 [512, 512], replicated, may hold values from -0.25 to 0.25
- bias_first: float32 [512], replicated, may hold values from -3 to 3
- mlp_second: bfloat16 [512, 256], replicated, may hold values from -0.25 to 0.25
- bias_second: float32 [256], replicated, may hold values from -3 to 3
- score_proj: bfloat16 [256], replicated, may hold values from -0.375 to 0.375
Outputs:
- span_scores: float32 [262144], P(('store', 'scorer'))
Inputs may be any that keep to these rules, and one draw needn't show every extreme that they name: A permutation: cluster c is row cluster_home[c] of store_rows. `cluster_ids`: of the 4096 entries of one device's requests, exactly 32 name clusters whose rows lie on each device's rows of store_rows, valid slots or not. `cand_count`: the counts of the 16 devices of one store group sum to 32768; in every group one device has all its requests full. `candidate_row`: the valid candidates of a store group fill each of its 32768 rows once; rows c * 2048 to (c + 1) * 2048 - 1 form span c, held by the group's device of scorer index c. One device has at most 256 valid candidates in one span, and in every group one device has exactly 256 in each span. Padded slots hold 0.
All inputs are finite; a program needn't handle non-finite values.
Results may differ from a plain program's by a relative error of at most 0.0065.
Values may be sent and summed in bfloat16 or wider, within the bound.
A program may use at most 128 MiB of HBM per device.

v0:
```python
import math

import jax
import jax.numpy as jnp
from jax import lax
from jax.sharding import PartitionSpec as P

HEADS = 4


def attend(cand_block, key_rows, key_sizes, key_count, query_proj, key_proj, value_proj, out_proj):
    batch_size, cand_slots, row_width = cand_block.shape
    cluster_slots = key_rows.shape[1]
    head_size = row_width // HEADS
    queries = jnp.dot(
        cand_block.reshape(-1, row_width), query_proj, preferred_element_type=jnp.float32
    ).astype(jnp.bfloat16)
    keys_all = jnp.dot(
        key_rows.reshape(-1, row_width), key_proj, preferred_element_type=jnp.float32
    ).astype(jnp.bfloat16)
    values_all = jnp.dot(
        key_rows.reshape(-1, row_width), value_proj, preferred_element_type=jnp.float32
    ).astype(jnp.bfloat16)
    queries = queries.reshape(batch_size, cand_slots, HEADS, head_size)
    keys_all = keys_all.reshape(batch_size, cluster_slots, HEADS, head_size)
    values_all = values_all.reshape(batch_size, cluster_slots, HEADS, head_size)
    logits = jnp.einsum("bchd,bkhd->bhck", queries, keys_all, preferred_element_type=jnp.float32)
    logits = logits * (1.0 / math.sqrt(head_size)) + key_sizes.astype(jnp.float32)[:, None, None, :]
    usable = jnp.arange(cluster_slots, dtype=jnp.int32)[None, :] < key_count[:, None]
    logits = jnp.where(usable[:, None, None, :], logits, -1e30)
    row_max = jnp.max(logits, axis=-1, keepdims=True)
    weights = jnp.exp(logits - row_max)
    probs = (weights / jnp.sum(weights, axis=-1, keepdims=True)).astype(jnp.bfloat16)
    context = jnp.einsum(
        "bhck,bkhd->bchd", probs, values_all, preferred_element_type=jnp.float32
    ).astype(jnp.bfloat16)
    context = context.reshape(batch_size * cand_slots, row_width)
    attended = jnp.dot(context, out_proj, preferred_element_type=jnp.float32).astype(jnp.bfloat16)
    return attended.reshape(batch_size, cand_slots, row_width)


def score_rows(features, mlp_first, bias_first, mlp_second, bias_second, score_proj):
    hidden_one = jnp.maximum(
        jnp.dot(features, mlp_first, preferred_element_type=jnp.float32) + bias_first, 0.0
    ).astype(jnp.bfloat16)
    hidden_two = jnp.maximum(
        jnp.dot(hidden_one, mlp_second, preferred_element_type=jnp.float32) + bias_second, 0.0
    ).astype(jnp.bfloat16)
    return jnp.dot(hidden_two, score_proj, preferred_element_type=jnp.float32)


def select_rows(wanted, table_rows, table_sizes):
    table_count = table_rows.shape[0]
    selector = (wanted[:, None] == jnp.arange(table_count, dtype=jnp.int32)[None, :]).astype(
        jnp.bfloat16
    )
    picked_rows = jnp.dot(selector, table_rows, preferred_element_type=jnp.float32).astype(
        jnp.bfloat16
    )
    picked_sizes = jnp.dot(selector, table_sizes[:, None], preferred_element_type=jnp.float32)[
        :, 0
    ].astype(jnp.bfloat16)
    return (picked_rows, picked_sizes)


def serve_lookup(wanted, store_rows, cluster_logsize):
    total = wanted.shape[0]
    piece = math.gcd(total, 1024)

    def one_piece(piece_index):
        part_ids = lax.dynamic_slice_in_dim(wanted, piece_index * piece, piece, 0)
        return select_rows(part_ids, store_rows, cluster_logsize)

    found_rows, found_sizes = lax.map(one_piece, jnp.arange(total // piece, dtype=jnp.int32))
    return (found_rows.reshape(total, store_rows.shape[1]), found_sizes.reshape(total))


def on_device(
    store_rows,
    cluster_logsize,
    cluster_home,
    cluster_ids,
    valid_count,
    candidates,
    cand_count,
    candidate_row,
    query_proj,
    key_proj,
    value_proj,
    out_proj,
    mlp_first,
    bias_first,
    mlp_second,
    bias_second,
    score_proj,
):
    device_count = lax.axis_size(("store", "scorer"))
    scorer_count = lax.axis_size("scorer")
    req_dev, cluster_slots = cluster_ids.shape
    rows_dev, row_width = store_rows.shape
    cand_slots = candidates.shape[1]
    per_pair = req_dev * cluster_slots // device_count
    slot_total = req_dev * cluster_slots
    global_row = cluster_home[cluster_ids.reshape(-1)]
    home_dev = global_row // rows_dev
    local_row = global_row - home_dev * rows_dev
    tile = math.gcd(slot_total, 128)
    tile_count = slot_total // tile
    dest_hot = (home_dev[:, None] == jnp.arange(device_count, dtype=jnp.int32)[None, :]).astype(
        jnp.bfloat16
    )
    dest_tiles = dest_hot.reshape(tile_count, tile, device_count)
    lower = (
        jnp.arange(tile, dtype=jnp.int32)[:, None] >= jnp.arange(tile, dtype=jnp.int32)[None, :]
    ).astype(jnp.bfloat16)
    within_tile = jnp.einsum("ij,bjd->bid", lower, dest_tiles, preferred_element_type=jnp.float32)
    tile_totals = within_tile[:, tile - 1, :]
    earlier = jnp.cumsum(tile_totals, axis=0) - tile_totals
    running = (within_tile + earlier[:, None, :]).reshape(slot_total, device_count)
    ranking = (jnp.sum(running * dest_hot.astype(jnp.float32), axis=1) - 1.0).astype(jnp.int32)
    send_pos = home_dev * per_pair + ranking
    asked_rows = (
        jnp.zeros((slot_total,), jnp.int32)
        .at[send_pos]
        .set(local_row)
        .reshape(device_count, per_pair)
    )
    asked_here = lax.all_to_all(
        asked_rows, ("store", "scorer"), split_axis=0, concat_axis=0, tiled=True
    )
    item_count = asked_here.shape[1]
    found_rows, found_sizes = serve_lookup(asked_here.reshape(-1), store_rows, cluster_logsize)
    got_rows = lax.all_to_all(
        found_rows.reshape(device_count, item_count, row_width),
        ("store", "scorer"),
        split_axis=0,
        concat_axis=0,
        tiled=True,
    )
    got_sizes = lax.all_to_all(
        found_sizes.reshape(device_count, item_count),
        ("store", "scorer"),
        split_axis=0,
        concat_axis=0,
        tiled=True,
    )
    arrived_rows = got_rows.reshape(slot_total, row_width)
    arrived_sizes = got_sizes.reshape(slot_total)
    block_size = math.gcd(req_dev, 2)

    def one_block(block_index):
        block_start = block_index * block_size
        cand_block = lax.dynamic_slice_in_dim(candidates, block_start, block_size, 0)
        wanted = lax.dynamic_slice_in_dim(
            send_pos, block_start * cluster_slots, block_size * cluster_slots, 0
        )
        block_rows, block_sizes = select_rows(wanted, arrived_rows, arrived_sizes)
        block_rows = block_rows.reshape(block_size, cluster_slots, row_width)
        block_sizes = block_sizes.reshape(block_size, cluster_slots)
        key_count = lax.dynamic_slice_in_dim(valid_count, block_start, block_size, 0)
        return attend(
            cand_block,
            block_rows,
            block_sizes,
            key_count,
            query_proj,
            key_proj,
            value_proj,
            out_proj,
        )

    attended = lax.map(one_block, jnp.arange(req_dev // block_size, dtype=jnp.int32)).reshape(
        req_dev, cand_slots, row_width
    )
    features = jnp.concatenate([candidates, attended], axis=-1).reshape(
        req_dev * cand_slots, 2 * row_width
    )
    span_live = req_dev * cand_slots // 2
    pair_cap = req_dev * cand_slots // scorer_count
    valid_mask = (jnp.arange(cand_slots, dtype=jnp.int32)[None, :] < cand_count[:, None]).reshape(
        -1
    )
    flat_rows = candidate_row.reshape(-1)
    target_dev = flat_rows // span_live
    span_pos = flat_rows - target_dev * span_live
    onehot = (
        (target_dev[:, None] == jnp.arange(scorer_count, dtype=jnp.int32)[None, :])
        & valid_mask[:, None]
    ).astype(jnp.int32)
    rank_span = jnp.sum(jnp.cumsum(onehot, axis=0) * onehot, axis=1) - 1
    send_slot = jnp.where(valid_mask, target_dev * pair_cap + rank_span, scorer_count * pair_cap)
    spots = (
        jnp.full((scorer_count * pair_cap,), span_live, jnp.int32)
        .at[send_slot]
        .set(span_pos, mode="drop")
    )
    spots = spots.reshape(scorer_count, pair_cap)
    cand_score = score_rows(features, mlp_first, bias_first, mlp_second, bias_second, score_proj)
    packed = (
        jnp.zeros((scorer_count * pair_cap,), jnp.float32)
        .at[send_slot]
        .set(cand_score, mode="drop")
    )
    arrived, arrived_spots = (
        lax.all_to_all(
            packed.reshape(scorer_count, pair_cap),
            "scorer",
            split_axis=0,
            concat_axis=0,
            tiled=True,
        ),
        lax.all_to_all(spots, "scorer", split_axis=0, concat_axis=0, tiled=True),
    )
    span_scores = (
        jnp.zeros((span_live,), jnp.float32)
        .at[arrived_spots.reshape(-1)]
        .set(arrived.reshape(-1), mode="drop")
    )
    return span_scores


def solution(mesh):
    in_specs = (
        P(("store", "scorer"), None),
        P(("store", "scorer")),
        P(),
        P(("store", "scorer"), None),
        P(("store", "scorer")),
        P(("store", "scorer"), None, None),
        P(("store", "scorer")),
        P(("store", "scorer"), None),
        P(),
        P(),
        P(),
        P(),
        P(),
        P(),
        P(),
        P(),
        P(),
    )
    out_specs = P(("store", "scorer"))
    return jax.shard_map(
        on_device, mesh=mesh, in_specs=in_specs, out_specs=out_specs, check_vma=False
    )
```

profile of v0, /device:TPU:0, one launch (start us, length us, event | category | flops | bytes accessed | tf_op | source)
XLA Modules:
  0.0 351.7 jit_solution(2125707313395969441)
XLA Ops:
  1.2 23.0 %gather_fusion = s32[4096]{0:T(1024)S(1)} fusion(s32[262144]{0:T(1024)S(1)} %copy-done, s32[4096]{0:T(1024)S(1)} %broadcast_clamp_fusion), kind=kCustom, calls=%fused_computation | custom fusion | bytes 49152 | tf_op jit(solution)/shard_map/gather | solution.py:104
  26.7 15.5 %scatter_custom_fusion.1 = s32[4096]{0:T(1024)S(1)} fusion(s32[4096]{0:T(1024)S(1)} %bitcast.206, s32[4096]{0:T(1024)S(1)} %get-tuple-element.247, s32[]{:T(128)} %constant.123.clone.1), kind=kCustom, calls=%fused_computation.131 | custom fusion | bytes 16388 | tf_op jit(solution)/shard_map/scatter | solution.py:125
  42.9 11.1 %all-to-all-start.1 = ((s32[128,1,32]{2,1,0:T(1,128)}), s32[128,1,32]{2,1,0:T(1,128)S(1)}, u32[]{:S(2)}, u32[]{:S(2)}) async-start(s32[128,1,32]{2,1,0:T(1,128)} %bitcast.26), calls=%async_computation.1 | async-start | bytes 131072 | tf_op jit(solution)/shard_map/all_to_all | solution.py:128
  54.3 9.2 %all-to-all-done.1 = s32[128,1,32]{2,1,0:T(1,128)S(1)} async-done(((s32[128,1,32]{2,1,0:T(1,128)}), s32[128,1,32]{2,1,0:T(1,128)S(1)}, u32[]{:S(2)}, u32[]{:S(2)}) %all-to-all-start.1) | async-done | bytes 16416 | tf_op jit(solution)/shard_map/all_to_all | solution.py:128
  65.0 21.3 %while.25 = (s32[]{:T(128)}, bf16[4,1024,256]{2,1,0:T(8,128)(2,1)}, bf16[4,1024]{1,0:T(4,128)(2,1)S(1)}, s32[4]{0:T(128)S(1)}, s32[4096]{0:T(1024)S(1)}, /*index...) while((s32[]{:T(128)}, bf16[4,1024,256]{2,1,0:T(8,128)(2,1)}, ...), condition=%wide.region_8.9_spmd, body=%wide.region_7.8_spmd.sunk | while | flops 1082393600 | bytes 1620655 | solution.py:74
  87.0 4.6 %all-to-all-start.3 = ((bf16[128,1,32]{2,1,0:T(2,128)(2,1)}), bf16[128,1,32]{2,1,0:T(2,128)(2,1)S(1)}, u32[]{:S(2)}, u32[]{:S(2)}) async-start(bf16[128,1,32]{2,1,0:T(2,128)(2,1)} %all_to_all.39), calls=%async_computation.3 | async-start | bytes 131072 | tf_op jit(solution)/shard_map/all_to_all | solution.py:140
  91.7 9.4 %all-to-all-done.3 = bf16[128,1,32]{2,1,0:T(2,128)(2,1)S(1)} async-done(((bf16[128,1,32]{2,1,0:T(2,128)(2,1)}), bf16[128,1,32]{2,1,0:T(2,128)(2,1)S(1)}, u32[]{:S(2)}, u32[]{:S(2)}) %all-to-all-start.3) | async-done | bytes 8224 | tf_op jit(solution)/shard_map/all_to_all | solution.py:140
  101.1 5.8 %all-to-all-start.2 = ((bf16[128,32,256]{2,1,0:T(8,128)(2,1)}), bf16[128,32,256]{2,1,0:T(8,128)(2,1)}, u32[]{:S(2)}, u32[]{:S(2)}) async-start(bf16[128,32,256]{2,1,0:T(8,128)(2,1)} %bitcast.27), calls=%async_computation.2 | async-start | bytes 4194304 | tf_op jit(solution)/shard_map/all_to_all | solution.py:133
  106.9 4.6 %reduce-window.6 = s32[16,32,128]{2,1,0:T(8,128)S(1)} reduce-window(s32[16,32,128]{2,1,0:T(8,128)S(1)} %fusion.44, s32[]{:T(128)} %constant.123.clone.1), window={size=1x1x128 pad=0_0x0_0x127_0}, to_apply=%region_0.1 | reduce-window | flops 8323072 | bytes 524292 | tf_op jit(solution)/shard_map/reduce-window
  112.9 16.1 %scatter_custom_fusion = s32[4096]{0:T(1024)} fusion(s32[4096]{0:T(1024)S(1)} %bitcast.210, s32[4096]{0:T(1024)S(1)} %get-tuple-element.249, s32[]{:T(128)} %constant.121.clone.1), kind=kCustom, calls=%fused_computation.133 | custom fusion | bytes 16388 | tf_op jit(solution)/shard_map/scatter | solution.py:195
  129.6 6.5 %all-to-all-done.2 = bf16[128,32,256]{2,1,0:T(8,128)(2,1)} async-done(((bf16[128,32,256]{2,1,0:T(8,128)(2,1)}), bf16[128,32,256]{2,1,0:T(8,128)(2,1)}, u32[]{:S(2)}, u32[]{:S(2)}) %all-to-all-start.2) | async-done | bytes 2097184 | tf_op jit(solution)/shard_map/all_to_all | solution.py:133
  140.4 153.6 %while.26 = (s32[]{:T(128)}, bf16[4,2,512,256]{3,2,1,0:T(8,128)(2,1)}, s32[4]{0:T(128)S(1)}, s32[4096]{0:T(1024)S(1)}, bf16[4096,256]{1,0:T(8,128)(2,1)}, /*inde...) while((s32[]{:T(128)}, ...), condition=%wide.wide.region_12.13_spmd, body=%wide.wide.region_9.12_spmd.sunk | while | flops 3260549632 | bytes 55262332 | solution.py:172
  152.6 4.5 %fusion.149 = f32[2,4,512,512]{2,3,1,0:T(8,128)} fusion(bf16[2,512,4,64]{3,2,1,0:T(4,128)(2,1)S(1)} %reshape.570, bf16[2,512,4,64]{3,2,1,0:T(4,128)(2,1)S(1)} %reshape.571), kind=kOutput, calls=%fused_computation.37.clone.clone.1 | convolution fusion | flops 268435456 | bytes 9437184 | tf_op jit(solution)/shard_map/while/body/eval_jaxpr/bchd,bkhd->bhck/dot_general | solution.py:27
  161.1 10.9 %fusion.152 = (f32[2,4,512]{2,1,0:T(4,128)S(1)}, f32[2,4,512,512]{2,3,1,0:T(8,128)}) fusion(f32[2,4,512,512]{2,3,1,0:T(8,128)} %fusion.149, f32[2,512]{1,0:T(2,128)S(1)} %fusion.151, pred[2,512]{1,0:T(4,128)(4,1)S(1)} %iota_compare_fusion.32), kind=kOutput, calls=%fused_computation.139.clone.clone.1 | output fusion | flops 16777728 | bytes 16798720 | tf_op jit(solution)/shard_map/while/body/eval_jaxpr/sub | solution.py:32
  191.0 4.5 %fusion.149 = f32[2,4,512,512]{2,3,1,0:T(8,128)} fusion(bf16[2,512,4,64]{3,2,1,0:T(4,128)(2,1)S(1)} %reshape.570, bf16[2,512,4,64]{3,2,1,0:T(4,128)(2,1)S(1)} %reshape.571), kind=kOutput, calls=%fused_computation.37.clone.clone.1 | convolution fusion | flops 268435456 | bytes 9437184 | tf_op jit(solution)/shard_map/while/body/eval_jaxpr/bchd,bkhd->bhck/dot_general | solution.py:27
  199.5 10.9 %fusion.152 = (f32[2,4,512]{2,1,0:T(4,128)S(1)}, f32[2,4,512,512]{2,3,1,0:T(8,128)}) fusion(f32[2,4,512,512]{2,3,1,0:T(8,128)} %fusion.149, f32[2,512]{1,0:T(2,128)S(1)} %fusion.151, pred[2,512]{1,0:T(4,128)(4,1)S(1)} %iota_compare_fusion.32), kind=kOutput, calls=%fused_computation.139.clone.clone.1 | output fusion | flops 16777728 | bytes 16798720 | tf_op jit(solution)/shard_map/while/body/eval_jaxpr/sub | solution.py:32
  229.3 4.5 %fusion.149 = f32[2,4,512,512]{2,3,1,0:T(8,128)} fusion(bf16[2,512,4,64]{3,2,1,0:T(4,128)(2,1)S(1)} %reshape.570, bf16[2,512,4,64]{3,2,1,0:T(4,128)(2,1)S(1)} %reshape.571), kind=kOutput, calls=%fused_computation.37.clone.clone.1 | convolution fusion | flops 268435456 | bytes 9437184 | tf_op jit(solution)/shard_map/while/body/eval_jaxpr/bchd,bkhd->bhck/dot_general | solution.py:27
  237.8 10.9 %fusion.152 = (f32[2,4,512]{2,1,0:T(4,128)S(1)}, f32[2,4,512,512]{2,3,1,0:T(8,128)}) fusion(f32[2,4,512,512]{2,3,1,0:T(8,128)} %fusion.149, f32[2,512]{1,0:T(2,128)S(1)} %fusion.151, pred[2,512]{1,0:T(4,128)(4,1)S(1)} %iota_compare_fusion.32), kind=kOutput, calls=%fused_computation.139.clone.clone.1 | output fusion | flops 16777728 | bytes 16798720 | tf_op jit(solution)/shard_map/while/body/eval_jaxpr/sub | solution.py:32
  276.2 10.9 %fusion.152 = (f32[2,4,512]{2,1,0:T(4,128)S(1)}, f32[2,4,512,512]{2,3,1,0:T(8,128)}) fusion(f32[2,4,512,512]{2,3,1,0:T(8,128)} %fusion.149, f32[2,512]{1,0:T(2,128)S(1)} %fusion.151, pred[2,512]{1,0:T(4,128)(4,1)S(1)} %iota_compare_fusion.32), kind=kOutput, calls=%fused_computation.139.clone.clone.1 | output fusion | flops 16777728 | bytes 16798720 | tf_op jit(solution)/shard_map/while/body/eval_jaxpr/sub | solution.py:32
  294.0 6.6 %maximum_convert_fusion = bf16[4096,512]{1,0:T(8,128)(2,1)} fusion(bf16[512,512]{1,0:T(8,128)(2,1)} %param.33, bf16[4096,256]{1,0:T(8,128)(2,1)} %bitcast.31, bf16[4096,256]{1,0:T(8,128)(2,1)} %bitcast.188, f32[512]{0:T(512)S(1)} %copy-done.16), kind=kOutput, calls=%fused_computation.48 | convolution fusion | flops 2162163712 | bytes 8914944 | tf_op jit(solution)/shard_map/dot_general | solution.py:44
  304.7 16.2 %scatter_custom_fusion.2 = f32[4096]{0:T(1024)} fusion(s32[4096]{0:T(1024)} %bitcast.211, f32[4096]{0:T(1024)S(1)} %bitcast.212, f32[]{:T(128)} %constant.120.clone.1), kind=kCustom, calls=%fused_computation.127 | custom fusion | bytes 16896 | tf_op jit(solution)/shard_map/scatter | solution.py:202
  320.9 7.1 %all-to-all-start.4 = ((f32[16,1,256]{2,1,0:T(1,128)}), f32[16,1,256]{2,1,0:T(1,128)S(1)}, u32[]{:S(2)}, u32[]{:S(2)}) async-start(f32[16,1,256]{2,1,0:T(1,128)} %bitcast.33), calls=%async_computation.4 | async-start | bytes 32768 | tf_op jit(solution)/shard_map/all_to_all | solution.py:205
  328.7 6.8 %all-to-all-done.4 = f32[16,1,256]{2,1,0:T(1,128)S(1)} async-done(((f32[16,1,256]{2,1,0:T(1,128)}), f32[16,1,256]{2,1,0:T(1,128)S(1)}, u32[]{:S(2)}, u32[]{:S(2)}) %all-to-all-start.4) | async-done | bytes 16416 | tf_op jit(solution)/shard_map/all_to_all | solution.py:205
  335.6 16.1 %scatter_custom_fusion.3 = f32[2048]{0:T(1024)} fusion(s32[4096]{0:T(1024)S(1)} %bitcast.209, f32[4096]{0:T(1024)S(1)} %bitcast.208, f32[]{:T(128)} %constant.120.clone.1), kind=kCustom, calls=%fused_computation.135 | custom fusion | bytes 8196 | tf_op jit(solution)/shard_map/scatter | solution.py:217
  (246 shorter events, 126.9 us)
Async XLA Ops:
  24.3 29.8 %copy-start.7 = (s32[8,512]{1,0:T(8,128)S(1)}, s32[8,512]{1,0:T(8,128)}, u32[]{:S(2)}) copy-start(s32[8,512]{1,0:T(8,128)} %param.28) | copy-start | bytes 49156
  24.3 29.8 %copy-start.13 = (s32[8]{0:T(128)S(1)}, s32[8]{0:T(128)}, u32[]{:S(2)}) copy-start(s32[8]{0:T(128)} %param.27) | copy-start | bytes 100
  24.3 40.6 %copy-start.9 = (bf16[2048]{0:T(1024)(128)(2,1)S(1)}, bf16[2048]{0:T(1024)(128)(2,1)}, u32[]{:S(2)}) copy-start(bf16[2048]{0:T(1024)(128)(2,1)} %param.22) | copy-start | bytes 12292
  24.3 40.6 %copy-start.14 = (bf16[2048,256]{1,0:T(8,128)(2,1)S(1)}, bf16[2048,256]{1,0:T(8,128)(2,1)}, u32[]{:S(2)}) copy-start(bf16[2048,256]{1,0:T(8,128)(2,1)} %param.21) | copy-start | bytes 3145732
  42.9 20.6 %all-to-all-start.1 = ((s32[128,1,32]{2,1,0:T(1,128)}), s32[128,1,32]{2,1,0:T(1,128)S(1)}, u32[]{:S(2)}, u32[]{:S(2)}) async-start(s32[128,1,32]{2,1,0:T(1,128)} %bitcast.26), calls=%async_computation.1 | async-start | bytes 131072 | tf_op jit(solution)/shard_map/all_to_all | solution.py:128
  86.2 20.7 %copy-start.18 = (bf16[256]{0:T(256)(128)(2,1)S(1)}, bf16[256]{0:T(256)(128)(2,1)}, u32[]{:S(2)}) copy-start(bf16[256]{0:T(256)(128)(2,1)} %param.37) | copy-start | bytes 1540
  86.2 54.1 %copy-start.3 = (bf16[256,256]{1,0:T(8,128)(2,1)S(1)}, bf16[256,256]{1,0:T(8,128)(2,1)}, u32[]{:S(2)}) copy-start(bf16[256,256]{1,0:T(8,128)(2,1)} %param.31) | copy-start | bytes 393220
  86.3 54.1 %copy-start.4 = (bf16[256,256]{1,0:T(8,128)(2,1)S(1)}, bf16[256,256]{1,0:T(8,128)(2,1)}, u32[]{:S(2)}) copy-start(bf16[256,256]{1,0:T(8,128)(2,1)} %param.29) | copy-start | bytes 393220
  86.3 54.1 %copy-start.5 = (bf16[256,256]{1,0:T(8,128)(2,1)S(1)}, bf16[256,256]{1,0:T(8,128)(2,1)}, u32[]{:S(2)}) copy-start(bf16[256,256]{1,0:T(8,128)(2,1)} %param.30) | copy-start | bytes 393220
  86.3 54.0 %copy-start.19 = (s32[8]{0:T(128)S(1)}, s32[8]{0:T(128)}, u32[]{:S(2)}) copy-start(s32[8]{0:T(128)} %param.25) | copy-start | bytes 100
  87.0 14.1 %all-to-all-start.3 = ((bf16[128,1,32]{2,1,0:T(2,128)(2,1)}), bf16[128,1,32]{2,1,0:T(2,128)(2,1)S(1)}, u32[]{:S(2)}, u32[]{:S(2)}) async-start(bf16[128,1,32]{2,1,0:T(2,128)(2,1)} %all_to_all.39), calls=%async_computation.3 | async-start | bytes 131072 | tf_op jit(solution)/shard_map/all_to_all | solution.py:140
  101.1 35.1 %all-to-all-start.2 = ((bf16[128,32,256]{2,1,0:T(8,128)(2,1)}), bf16[128,32,256]{2,1,0:T(8,128)(2,1)}, u32[]{:S(2)}, u32[]{:S(2)}) async-start(bf16[128,32,256]{2,1,0:T(8,128)(2,1)} %bitcast.27), calls=%async_computation.2 | async-start | bytes 4194304 | tf_op jit(solution)/shard_map/all_to_all | solution.py:133
  112.9 27.5 %copy-start.12 = (s32[4096,1]{0,1:T(1,128)}, s32[4096,1]{0,1:T(1,128)S(1)}, u32[]{:S(2)}) copy-start(s32[4096,1]{0,1:T(1,128)S(1)} %compare_select_fusion.3) | copy-start | bytes 49156
  129.0 11.3 %copy-start.8 = (bf16[128,1,32]{2,0,1:T(8,128)(2,1)}, bf16[128,1,32]{2,0,1:T(8,128)(2,1)S(1)}, u32[]{:S(2)}) copy-start(bf16[128,1,32]{2,0,1:T(8,128)(2,1)S(1)} %copy.79) | copy-start | bytes 24580
  136.1 184.8 %all-to-all-start = ((s32[16,1,256]{2,1,0:T(1,128)}), s32[16,1,256]{2,1,0:T(1,128)}, u32[]{:S(2)}, u32[]{:S(2)}) async-start(s32[16,1,256]{2,1,0:T(1,128)} %bitcast.13), calls=%async_computation | async-start | bytes 32768 | tf_op jit(solution)/shard_map/all_to_all | solution.py:212
  140.3 153.6 %copy-start.16 = (f32[512]{0:T(512)S(1)}, f32[512]{0:T(512)}, u32[]{:S(2)}) copy-start(f32[512]{0:T(512)} %param.34) | copy-start | bytes 6148
  140.6 5.7 %copy-start.10 = (s32[4096]{0:T(1024)}, s32[4096]{0:T(1024)S(1)}, u32[]{:S(2)}) copy-start(s32[4096]{0:T(1024)S(1)} %get-tuple-element.503) | copy-start | bytes 49156 | tf_op jit(solution)/shard_map/while
  161.1 10.9 %copy-start.2 = (bf16[1024,256]{1,0:T(8,128)(2,1)S(1)}, bf16[1024,256]{1,0:T(8,128)(2,1)}, u32[]{:S(2)}) copy-start(bf16[1024,256]{1,0:T(8,128)(2,1)} %copy-done.1) | copy-start | bytes 1572868 | tf_op jit(solution)/shard_map/while
  199.5 10.9 %copy-start.2 = (bf16[1024,256]{1,0:T(8,128)(2,1)S(1)}, bf16[1024,256]{1,0:T(8,128)(2,1)}, u32[]{:S(2)}) copy-start(bf16[1024,256]{1,0:T(8,128)(2,1)} %copy-done.1) | copy-start | bytes 1572868 | tf_op jit(solution)/shard_map/while
  237.8 10.9 %copy-start.2 = (bf16[1024,256]{1,0:T(8,128)(2,1)S(1)}, bf16[1024,256]{1,0:T(8,128)(2,1)}, u32[]{:S(2)}) copy-start(bf16[1024,256]{1,0:T(8,128)(2,1)} %copy-done.1) | copy-start | bytes 1572868 | tf_op jit(solution)/shard_map/while
  276.2 10.9 %copy-start.2 = (bf16[1024,256]{1,0:T(8,128)(2,1)S(1)}, bf16[1024,256]{1,0:T(8,128)(2,1)}, u32[]{:S(2)}) copy-start(bf16[1024,256]{1,0:T(8,128)(2,1)} %copy-done.1) | copy-start | bytes 1572868 | tf_op jit(solution)/shard_map/while
  294.0 6.7 %copy-start.15 = (bf16[512,256]{1,0:T(8,128)(2,1)S(1)}, bf16[512,256]{1,0:T(8,128)(2,1)}, u32[]{:S(2)}) copy-start(bf16[512,256]{1,0:T(8,128)(2,1)} %param.35) | copy-start | bytes 786436
  294.0 6.7 %copy-start.17 = (f32[256]{0:T(256)S(1)}, f32[256]{0:T(256)}, u32[]{:S(2)}) copy-start(f32[256]{0:T(256)} %param.36) | copy-start | bytes 3076
  320.9 14.7 %all-to-all-start.4 = ((f32[16,1,256]{2,1,0:T(1,128)}), f32[16,1,256]{2,1,0:T(1,128)S(1)}, u32[]{:S(2)}, u32[]{:S(2)}) async-start(f32[16,1,256]{2,1,0:T(1,128)} %bitcast.33), calls=%async_computation.4 | async-start | bytes 32768 | tf_op jit(solution)/shard_map/all_to_all | solution.py:205
  (24 other events, 78.8 us)
where the time goes:
time: 353 us; the launch traced here: 352 us
  local copies, waits for them, and re-layouts  122 us (35%)
  matrix products  104 us (29%)
  other arithmetic  52.5 us (15%)
  starting transfers between devices  32.7 us (9%)
  waiting for transfers between devices  31.9 us (9%)
  loops' own time  8.44 us (2%)
    sub x4, other arithmetic, attend(): weights = jnp.exp(logits - row_max)  43.6 us
    dot_general x8, matrix products, select_rows(): jnp.dot(selector, table_rows, preferred_element_type=jnp.float32)  26.8 us
    gather x1, local copies, waits for them, and re-layouts, on_device(): global_row = cluster_home[cluster_ids.reshape(-1)]  23 us
    dot_general x8, matrix products, select_rows(): jnp.dot(selector, table_sizes[:, None], preferred_element_type=jnp.float32)  21.9 us
    dot_general x4, matrix products, attend(): jnp.einsum('bchd,bkhd->bhck', queries, keys_all, preferred_element_type=j...  17.9 us
    dot_general x4, matrix products, attend(): jnp.einsum('bhck,bkhd->bchd', probs, values_all, preferred_element_type=j...  17.2 us
    scatter x1, local copies, waits for them, and re-layouts, on_device(): packed = jnp.zeros((scorer_count * pair_cap,), jnp.float32).at[send_slot]...  16.2 us
    scatter x1, local copies, waits for them, and re-layouts, on_device(): spots = jnp.full((scorer_count * pair_cap,), span_live, jnp.int32).at[sen...  16.1 us
  transfers between devices with their start and end apart: 5, of which 4 were waited for; matrix products, arithmetic and copies ran while one was open for 55% of the time, Pallas kernels for 0%

commit v1 on v0

v1 whole, which is shorter than its diff:
```python
import functools

import jax
import jax.numpy as jnp
from jax import lax
from jax.experimental import pallas as pl
from jax.experimental.pallas import tpu as pltpu
from jax.sharding import PartitionSpec as P

HEADS = 4
AXES = ("store", "scorer")
LANES = 128
NT = (((1,), (1,)), ((), ()))
TN = (((0,), (0,)), ((), ()))
BF = jnp.bfloat16
F32 = jnp.float32
VMEM_LIMIT = 48 * 1024 * 1024


def lane_pick(rows, lane_index):
    return jnp.take_along_axis(rows, lane_index, axis=1)


def column_of(row):
    return jnp.broadcast_to(row, (LANES, LANES)).T


def route_kernel(rows_dev, per_pair, ids_smem, ids_ref, table_ref, ask_ref, pos_ref, home_ref, rows_scr):
    tiles = ids_ref.shape[0]
    shift_rows = rows_dev.bit_length() - 1

    def fetch(t, carry):
        for u in range(LANES):
            c = ids_smem[t, u]
            rows_scr[pl.ds(t * LANES + u, 1), :] = table_ref[
                pl.ds(lax.shift_right_logical(c, 7), 1), :
            ]
        return carry

    lax.fori_loop(0, tiles, fetch, 0)
    lane = lax.broadcasted_iota(jnp.int32, (LANES, LANES), 1)
    sub = lax.broadcasted_iota(jnp.int32, (LANES, LANES), 0)
    lower = jnp.where(sub >= lane, 1.0, 0.0).astype(BF)
    ones = jnp.ones((LANES, LANES), BF)
    base = jnp.zeros((1, LANES), F32)
    acc = jnp.zeros((LANES, 2 * LANES), F32)
    for t in range(tiles):
        ids_col = column_of(ids_ref[t : t + 1, :])
        home = lane_pick(rows_scr[t * LANES : (t + 1) * LANES, :], ids_col & (LANES - 1))
        dest = lax.shift_right_logical(home, shift_rows)
        hot = dest == lane
        hot_b = jnp.where(hot, 1.0, 0.0).astype(BF)
        incl = jnp.dot(lower, hot_b, preferred_element_type=F32)
        picked = jnp.where(hot, incl + (base - 1.0), 0.0).astype(BF)
        rank = jnp.dot(picked, ones, preferred_element_type=F32).astype(jnp.int32)
        base = base + incl[LANES - 1 : LANES, :]
        low = (home & 255).astype(F32)
        high = (lax.shift_right_logical(home, 8) & ((rows_dev >> 8) - 1)).astype(F32)
        at = rank == lane
        parts = jnp.concatenate(
            [jnp.where(at, low, 0.0), jnp.where(at, high, 0.0)], axis=1
        ).astype(BF)
        acc = acc + lax.dot_general(hot_b, parts, TN, preferred_element_type=F32)
        diag = sub == lane
        pos = (dest * per_pair + rank).astype(F32)
        pos_ref[t : t + 1, :] = jnp.sum(
            jnp.where(diag, pos, 0.0), axis=0, keepdims=True
        ).astype(jnp.int32)
        home_ref[t : t + 1, :] = jnp.sum(
            jnp.where(diag, home.astype(F32), 0.0), axis=0, keepdims=True
        ).astype(jnp.int32)
    ask_ref[...] = (acc[:, :LANES] + 256.0 * acc[:, LANES:]).astype(jnp.int32)


def route(ids, table, rows_dev, per_pair):
    tiles = ids.shape[0]
    vm = pl.BlockSpec(memory_space=pltpu.VMEM)
    return pl.pallas_call(
        functools.partial(route_kernel, rows_dev, per_pair),
        out_shape=(
            jax.ShapeDtypeStruct((LANES, LANES), jnp.int32),
            jax.ShapeDtypeStruct((tiles, LANES), jnp.int32),
            jax.ShapeDtypeStruct((tiles, LANES), jnp.int32),
        ),
        in_specs=[pl.BlockSpec(memory_space=pltpu.SMEM), vm, vm],
        out_specs=(vm, vm, vm),
        scratch_shapes=[pltpu.VMEM((tiles * LANES, LANES), jnp.int32)],
        compiler_params=pltpu.CompilerParams(vmem_limit_bytes=VMEM_LIMIT),
        name="route",
    )(ids, ids, table)


def serve_kernel(per_pair, ask_smem, store_ref, out_ref, store_scr, stage):
    store_scr[...] = store_ref[...].astype(F32)
    pairs = ask_smem.shape[0]
    group = 4

    def some(g, carry):
        for q in range(group):
            for j in range(per_pair):
                row = ask_smem[g * group + q, j]
                stage[pl.ds(q * per_pair + j, 1), :] = store_scr[pl.ds(row, 1), :]
        out_ref[pl.ds(g * (group * per_pair), group * per_pair), :] = stage[...].astype(BF)
        return carry

    lax.fori_loop(0, pairs // group, some, 0)


def serve(asked, store_rows, per_pair):
    pairs = asked.shape[0]
    width = store_rows.shape[1]
    vm = pl.BlockSpec(memory_space=pltpu.VMEM)
    return pl.pallas_call(
        functools.partial(serve_kernel, per_pair),
        out_shape=jax.ShapeDtypeStruct((pairs * per_pair, width), BF),
        in_specs=[pl.BlockSpec(memory_space=pltpu.SMEM), vm],
        out_specs=vm,
        scratch_shapes=[
            pltpu.VMEM(store_rows.shape, F32),
            pltpu.VMEM((4 * per_pair, width), F32),
        ],
        compiler_params=pltpu.CompilerParams(vmem_limit_bytes=VMEM_LIMIT),
        name="serve",
    )(asked, store_rows)


def score_kernel(
    pos_smem,
    home_smem,
    valid_smem,
    count_smem,
    home_ref,
    sizes_ref,
    arrived_ref,
    cand_ref,
    row_ref,
    wq_ref,
    wk_ref,
    wv_ref,
    wo_ref,
    m1_ref,
    b1_ref,
    m2_ref,
    b2_ref,
    sp_ref,
    out_ref,
    arr_scr,
    x_scr,
    sz_scr,
    k_scr,
    v_scr,
):
    r = pl.program_id(0)
    slots, width = x_scr.shape
    cands = cand_ref.shape[1]
    per_req = slots // LANES
    head_size = width // HEADS
    step = 256

    @pl.when(r == 0)
    def _():
        arr_scr[...] = arrived_ref[...].astype(F32)
        x_scr[...] = jnp.zeros_like(x_scr)
        sz_scr[...] = jnp.zeros_like(sz_scr)
        out_ref[...] = jnp.zeros_like(out_ref)

    valid = valid_smem[r]
    count = count_smem[r]

    unroll = 32

    def fetch(b, carry):
        line = r * per_req + b // (LANES // unroll)
        col = lax.rem(b, LANES // unroll) * unroll
        for u in range(unroll):
            at = pos_smem[line, col + u]
            home = home_smem[line, col + u]
            x_scr[pl.ds(b * unroll + u, 1), :] = arr_scr[pl.ds(at, 1), :]
            sz_scr[pl.ds(b * unroll + u, 1), :] = sizes_ref[
                pl.ds(lax.shift_right_logical(home, 7), 1), :
            ]
        return carry

    lax.fori_loop(0, pl.cdiv(valid, unroll), fetch, 0)

    x = x_scr[...].astype(BF)
    keys = jnp.dot(x, wk_ref[...], preferred_element_type=F32).astype(BF).astype(F32) * 0.125
    values = jnp.dot(x, wv_ref[...], preferred_element_type=F32).astype(BF).astype(F32)
    sizes = []
    for t in range(per_req):
        home_col = column_of(home_ref[0, t : t + 1, :])
        size = lane_pick(sz_scr[t * LANES : (t + 1) * LANES, :], home_col & (LANES - 1))
        slot = lax.broadcasted_iota(jnp.int32, (LANES, LANES), 0) + t * LANES
        sizes.append(jnp.where(slot < valid, size, -1e30))
    sizes = jnp.concatenate(sizes, axis=0)
    lane = lax.broadcasted_iota(jnp.int32, (slots, LANES), 1)
    bias = jnp.where(lane == 0, sizes, 0.0).astype(BF)
    for h in range(HEADS):
        half = slice((h // 2) * LANES, (h // 2 + 1) * LANES)
        other = slice((1 - h // 2) * LANES, (2 - h // 2) * LANES)
        mine = (lane // head_size) == (h % 2)
        k_scr[h, :, half] = jnp.where(mine, keys[:, half], 0.0).astype(BF)
        k_scr[h, :, other] = bias
        v_scr[h, :, :LANES] = jnp.where(mine, values[:, half], 0.0).astype(BF)
        v_scr[h, :, LANES:] = jnp.where(mine, 1.0, 0.0).astype(BF)

    for c in range(0, cands, step):
        cand = cand_ref[0, c : c + step, :]
        query = jnp.dot(cand, wq_ref[...], preferred_element_type=F32)
        clane = lax.broadcasted_iota(jnp.int32, (step, LANES), 1)
        halves = []
        for p in range(2):
            own = query[:, p * LANES : (p + 1) * LANES].astype(BF)
            other = query[:, (1 - p) * LANES : (2 - p) * LANES]
            other = jnp.where(clane == 0, 1.0, other).astype(BF)
            parts = [own, other] if p == 0 else [other, own]
            q_p = jnp.concatenate(parts, axis=1)
            total = None
            for h in (2 * p, 2 * p + 1):
                logits = lax.dot_general(q_p, k_scr[h], NT, preferred_element_type=F32)
                top = jnp.max(logits, axis=1, keepdims=True)
                probs = jnp.exp(logits - top).astype(BF)
                part = jnp.dot(probs, v_scr[h], preferred_element_type=F32)
                total = part if total is None else total + part
            halves.append((total[:, :LANES] / total[:, LANES:]).astype(BF))
        context = jnp.concatenate(halves, axis=1)
        attended = jnp.dot(context, wo_ref[...], preferred_element_type=F32).astype(BF)
        hidden = jnp.dot(cand, m1_ref[:width, :], preferred_element_type=F32)
        hidden += jnp.dot(attended, m1_ref[width:, :], preferred_element_type=F32)
        hidden = jnp.maximum(hidden + b1_ref[...], 0.0).astype(BF)
        hidden = jnp.dot(hidden, m2_ref[...], preferred_element_type=F32)
        hidden = jnp.maximum(hidden + b2_ref[...], 0.0).astype(BF)
        score = lax.dot_general(sp_ref[...], hidden, NT, preferred_element_type=F32)[0:1, :]
        slot = lax.broadcasted_iota(jnp.int32, (1, step), 1) + c
        score = jnp.where(slot < count, score, 0.0)
        first = score.astype(BF).astype(F32)
        second = score - first
        row = row_ref[0, :, c : c + step]
        lines = out_ref.shape[0]
        at_line = lax.broadcasted_iota(jnp.int32, (lines, step), 0) == lax.shift_right_logical(row, 7)
        at_lane = lax.broadcasted_iota(jnp.int32, (LANES, step), 0) == (row & (LANES - 1))
        at_lane = jnp.where(at_lane, 1.0, 0.0).astype(BF)
        out_ref[...] += lax.dot_general(
            jnp.where(at_line, first, 0.0).astype(BF), at_lane, NT, preferred_element_type=F32
        ) + lax.dot_general(
            jnp.where(at_line, second, 0.0).astype(BF), at_lane, NT, preferred_element_type=F32
        )


def score(pos, home, valid, count, sizes, arrived, candidates, rows, weights, lines):
    reqs, cands, width = candidates.shape
    slots = pos.size // reqs
    sm = pl.BlockSpec(memory_space=pltpu.SMEM)

    def whole(a):
        return pl.BlockSpec(a.shape, lambda r, n=a.ndim: (0,) * n)

    home3 = home.reshape(reqs, slots // LANES, LANES)
    rows3 = rows.reshape(reqs, 1, cands)
    return pl.pallas_call(
        score_kernel,
        grid=(reqs,),
        out_shape=jax.ShapeDtypeStruct((lines, LANES), F32),
        in_specs=[
            sm,
            sm,
            sm,
            sm,
            pl.BlockSpec((1, slots // LANES, LANES), lambda r: (r, 0, 0)),
            whole(sizes),
            whole(arrived),
            pl.BlockSpec((1, cands, width), lambda r: (r, 0, 0)),
            pl.BlockSpec((1, 1, cands), lambda r: (r, 0, 0)),
        ]
        + [whole(w) for w in weights],
        out_specs=pl.BlockSpec((lines, LANES), lambda r: (0, 0)),
        scratch_shapes=[
            pltpu.VMEM(arrived.shape, F32),
            pltpu.VMEM((slots, width), F32),
            pltpu.VMEM((slots, LANES), F32),
            pltpu.VMEM((HEADS, slots, width), BF),
            pltpu.VMEM((HEADS, slots, width), BF),
        ],
        compiler_params=pltpu.CompilerParams(vmem_limit_bytes=VMEM_LIMIT),
        name="score",
    )(pos, home, valid, count, home3, sizes, arrived, candidates, rows3, *weights)


def on_device(
    store_rows,
    cluster_logsize,
    cluster_home,
    cluster_ids,
    valid_count,
    candidates,
    cand_count,
    candidate_row,
    query_proj,
    key_proj,
    value_proj,
    out_proj,
    mlp_first,
    bias_first,
    mlp_second,
    bias_second,
    score_proj,
):
    device_count = lax.axis_size(AXES)
    scorer_count = lax.axis_size("scorer")
    rows_dev, width = store_rows.shape
    slot_total = cluster_ids.size
    per_pair = slot_total // device_count
    reqs, cands = candidate_row.shape
    sizes = lax.all_gather(cluster_logsize, AXES, tiled=True)
    sizes = sizes.astype(F32).reshape(-1, LANES)
    ask, pos, home = route(
        cluster_ids.reshape(-1, LANES), cluster_home.reshape(-1, LANES), rows_dev, per_pair
    )
    asked = lax.all_to_all(
        ask[:device_count, :per_pair], AXES, split_axis=0, concat_axis=0, tiled=True
    )
    found = serve(asked, store_rows, per_pair)
    arrived = lax.all_to_all(
        found.reshape(device_count, per_pair, width), AXES, split_axis=0, concat_axis=0, tiled=True
    ).reshape(slot_total, width)
    weights = (
        query_proj,
        key_proj,
        value_proj,
        out_proj,
        mlp_first,
        bias_first.reshape(1, -1),
        mlp_second,
        bias_second.reshape(1, -1),
        jnp.broadcast_to(score_proj.reshape(1, -1), (16, score_proj.size)),
    )
    lines = scorer_count * (reqs * cands // 2) // LANES
    table = score(
        pos, home, valid_count, cand_count, sizes, arrived, candidates, candidate_row, weights, lines
    )
    blocks = table.reshape(scorer_count, lines // scorer_count, LANES)
    blocks = lax.all_to_all(blocks, "scorer", split_axis=0, concat_axis=0, tiled=True)
    return jnp.sum(blocks, axis=0).reshape(-1)


def solution(mesh):
    split = P(AXES)
    in_specs = (
        P(AXES, None),
        split,
        P(),
        P(AXES, None),
        split,
        P(AXES, None, None),
        split,
        P(AXES, None),
    ) + (P(),) * 9
    return jax.shard_map(
        on_device, mesh=mesh, in_specs=in_specs, out_specs=split, check_vma=False
    )
```

time: 353 us -> 197 us (0.56)
  local copies, waits for them, and re-layouts: 122 us -> 13.7 us
  matrix products: 104 us -> 0 us
  blocking collectives: 0 us -> 104 us
  Pallas kernels: 0 us -> 72.6 us
  other arithmetic: 52.5 us -> 0.69 us
  waiting for transfers between devices: 31.9 us -> 0.01 us
  starting transfers between devices: 32.7 us -> 4.78 us
  loops' own time: 8.44 us -> 0 us
    dot_general x43 -> x0, matrix products: 104 us -> none  [the longest x8 26.8 us: select_rows(): jnp.dot(selector, table_rows, preferred_element_type=jnp.float32)]
    pallas_call x0 -> x3, Pallas kernels: none -> 72.6 us  [the longest x1 52.5 us: score(): pl.pallas_call(score_kernel, grid=(reqs,), out_shape=jax.ShapeDtypeStruct...]
    all_gather x0 -> x1, blocking collectives: none -> 71.5 us  [on_device(): sizes = lax.all_gather(cluster_logsize, AXES, tiled=True)]
    scatter x4 -> x0, local copies, waits for them, and re-layouts: 63.9 us -> none  [the longest x1 16.2 us: on_device(): packed = jnp.zeros((scorer_count * pair_cap,), jnp.float32).at[send_slot]...]
    sub x7 -> x0, other arithmetic: 43.7 us -> none  [the longest x4 43.6 us: attend(): weights = jnp.exp(logits - row_max)]
    all_to_all x0 -> x2, blocking collectives: none -> 32.8 us  [the longest x1 20.4 us: on_device(): lax.all_to_all(ask[:device_count, :per_pair], AXES, split_axis=0, concat_...]
    all_to_all x5 -> x1, waiting for transfers between devices: 31.9 us -> 0.01 us  [on_device(): lax.all_to_all(found.reshape(device_count, per_pair, width), AXES, split_...]
    all_to_all x5 -> x1, starting transfers between devices: 32.7 us -> 4.78 us  [on_device(): lax.all_to_all(found.reshape(device_count, per_pair, width), AXES, split_...]
  transfers between devices with their start and end apart: 5 -> 1, of which waited for: 4 -> 0; matrix products, arithmetic and copies ran while one was open for 55% -> 0% of each run, Pallas kernels for 0% -> 0%
where the time goes in v1:
time: 197 us; the launch traced here: 196 us
  blocking collectives  104 us (53%)
  Pallas kernels  72.6 us (37%)
  local copies, waits for them, and re-layouts  13.7 us (7%)
  starting transfers between devices  4.78 us (2%)
    all_gather x1, blocking collectives, on_device(): sizes = lax.all_gather(cluster_logsize, AXES, tiled=True)  71.5 us
    pallas_call x1, Pallas kernels, score(): pl.pallas_call(score_kernel, grid=(reqs,), out_shape=jax.ShapeDtypeStruct...  52.5 us
    all_to_all x1, blocking collectives, on_device(): lax.all_to_all(ask[:device_count, :per_pair], AXES, split_axis=0, concat_...  20.4 us
    all_to_all x1, blocking collectives, on_device(): lax.all_to_all(blocks, 'scorer', split_axis=0, concat_axis=0, tiled=True)  12.3 us
    unnamed x36, local copies, waits for them, and re-layouts  11.7 us
    pallas_call x1, Pallas kernels, route(): pl.pallas_call(functools.partial(route_kernel, rows_dev, per_pair), out_s...  10.5 us
    pallas_call x1, Pallas kernels, serve(): pl.pallas_call(functools.partial(serve_kernel, per_pair), out_shape=jax.S...  9.55 us
    all_to_all x1, starting transfers between devices, on_device(): lax.all_to_all(found.reshape(device_count, per_pair, width), AXES, split_...  4.78 us
  transfers between devices with their start and end apart: 1, of which 0 were waited for; matrix products, arithmetic and copies ran while one was open for 0% of the time, Pallas kernels for 0%

profile of v1, /device:TPU:0, one launch (start us, length us, event | category | flops | bytes accessed | tf_op | source)
XLA Modules:
  0.0 196.1 jit_solution(7238375526664821299)
XLA Ops:
  0.0 0.7 reshape.39.ids_smem.ids_ref
  0.7 1.2 copy-done.2
  1.9 10.5 %route.1 = (s32[128,128]{1,0:T(8,128)S(1)}, s32[32,128]{1,0:T(8,128)S(1)}, s32[32,128]{1,0:T(8,128)S(1)}) custom-call(s32[32,128]{1,0:T(8,128)S(1)} %reshape.39.ids_smem.ids_ref, s32[32,128]{1,0:T(8,128)S(1)} %reshape.39.ids_smem.ids_ref, s32[2048,128]{1,0:T(8,128)S(1)} %bitcast.18), custom_call_target="tpu_custom_call" | custom-call | tf_op jit(solution)/shard_map/route/pallas_call | solution.py:78
  12.5 20.4 %all_to_all.21 = s32[128,1,32]{2,1,0:T(1,128)S(1)} all-to-all(s32[128,1,32]{2,1,0:T(1,128)S(1)} %bitcast.22), channel_id=1, replica_groups=mesh['store'=8,'scorer'=16] {'store','scorer'}, dimensions={0} | all-to-all | bytes 32768 | tf_op jit(solution)/shard_map/all_to_all | solution.py:319
  32.9 1.2 copy-done.1
  34.2 9.5 %serve.1 = bf16[4096,256]{1,0:T(8,128)(2,1)S(1)} custom-call(s32[128,32]{1,0:T(8,128)S(1)} %bitcast.20, bf16[2048,256]{1,0:T(8,128)(2,1)S(1)} %copy-done.1), custom_call_target="tpu_custom_call" | custom-call | tf_op jit(solution)/shard_map/serve/pallas_call | solution.py:113
  43.7 1.3 copy-done
  45.0 4.8 %all-to-all-start.1 = ((bf16[128,32,256]{2,1,0:T(8,128)(2,1)}), bf16[128,32,256]{2,1,0:T(8,128)(2,1)S(1)}, u32[]{:S(2)}, u32[]{:S(2)}) async-start(bf16[128,32,256]{2,1,0:T(8,128)(2,1)} %bitcast.17), calls=%async_computation.1 | async-start | bytes 4194304 | tf_op jit(solution)/shard_map/all_to_all | solution.py:323
  49.9 0.6 reshape.46.row_ref
  50.5 71.5 %all_gather.3 = bf16[262144]{0:T(1024)(128)(2,1)S(1)} all-gather(bf16[2048]{0:T(1024)(128)(2,1)S(1)} %copy-done.17), channel_id=1, replica_groups=mesh['store'=8,'scorer'=16] {'store','scorer'}, dimensions={0}, use_global_device_ids=true | all-gather | bytes 528384 | tf_op jit(solution)/shard_map/all_gather | solution.py:314
  122.1 0.7 broadcast_in_dim.2.sp_ref
  122.8 1.0 copy-done.3
  123.8 0.9 copy-done.6
  124.7 0.9 copy-done.7
  125.6 0.9 copy-done.8
  126.5 0.7 copy-done.9
  127.2 0.7 copy-done.11
  127.9 0.7 copy-done.12
  128.6 0.7 copy-done.13
  129.3 0.7 copy-done.14
  130.0 0.7 copy-done.15
  130.6 52.5 %score.1 = f32[256,128]{1,0:T(8,128)S(1)} custom-call(s32[32,128]{1,0:T(8,128)S(1)} %copy-done.11, s32[32,128]{1,0:T(8,128)S(1)} %get-tuple-element.9.home_smem, s32[8]{0:T(128)S(1)} %copy-done.14, s32[8]{0:T(128)S(1)} %copy-done.15, s32[8,4,128]{2,1,0:T(4,128)S(1)} %bitcast.21, f32[2048,128]{1,0:T(8,128)S(1)} %bitcast_convert_fusion.sizes_ref, ...), custom_call_target="tpu_custom_call" | custom-call | tf_op jit(solution)/shard_map/score/pallas_call | solution.py:260
  183.1 12.3 %all_to_all.22 = f32[16,16,128]{2,1,0:T(8,128)S(1)} all-to-all(f32[16,16,128]{2,1,0:T(8,128)S(1)} %bitcast.19), channel_id=1, replica_groups=mesh['store'=8,'scorer'=16] {'scorer'}, dimensions={0} | all-to-all | bytes 262144 | tf_op jit(solution)/shard_map/all_to_all | solution.py:342
  195.5 0.6 reduce_sum.9
  (25 shorter events, 0.1 us)
Async XLA Ops:
  0.7 1.2 copy-start.2
  12.5 32.6 %copy-start.10 = (s32[32,128]{1,0:T(8,128)}, s32[32,128]{1,0:T(8,128)S(1)}, u32[]{:S(2)}) copy-start(s32[32,128]{1,0:T(8,128)S(1)} %get-tuple-element.8.pos_smem) | copy-start | bytes 49156
  32.9 1.2 copy-start.1
  43.7 1.3 copy-start
  45.0 4.8 %copy-start.16 = (s32[8,512]{1,0:T(8,128)S(1)}, s32[8,512]{1,0:T(8,128)}, u32[]{:S(2)}) copy-start(s32[8,512]{1,0:T(8,128)} %param.24) | copy-start | bytes 49156
  45.0 5.4 %copy-start.17 = (bf16[2048]{0:T(1024)(128)(2,1)S(1)}, bf16[2048]{0:T(1024)(128)(2,1)}, u32[]{:S(2)}) copy-start(bf16[2048]{0:T(1024)(128)(2,1)} %param.18) | copy-start | bytes 12292
  45.0 77.0 %all-to-all-start.1 = ((bf16[128,32,256]{2,1,0:T(8,128)(2,1)}), bf16[128,32,256]{2,1,0:T(8,128)(2,1)S(1)}, u32[]{:S(2)}, u32[]{:S(2)}) async-start(bf16[128,32,256]{2,1,0:T(8,128)(2,1)} %bitcast.17), calls=%async_computation.1 | async-start | bytes 4194304 | tf_op jit(solution)/shard_map/all_to_all | solution.py:323
  49.8 72.9 %copy-start.4 = (bf16[512,256]{1,0:T(8,128)(2,1)S(1)}, bf16[512,256]{1,0:T(8,128)(2,1)}, u32[]{:S(2)}) copy-start(bf16[512,256]{1,0:T(8,128)(2,1)} %m2_ref.1) | copy-start | bytes 786436
  49.9 72.9 %copy-start.5 = (bf16[256,256]{1,0:T(8,128)(2,1)S(1)}, bf16[256,256]{1,0:T(8,128)(2,1)}, u32[]{:S(2)}) copy-start(bf16[256,256]{1,0:T(8,128)(2,1)} %wq_ref.1) | copy-start | bytes 393220
  122.7 1.0 copy-start.3
  123.8 0.9 copy-start.6
  124.7 0.9 copy-start.7
  125.6 0.9 copy-start.8
  126.5 0.7 copy-start.9
  127.2 0.7 copy-start.11
  127.9 0.7 copy-start.12
  128.6 0.7 copy-start.13
  129.3 0.7 copy-start.14
  130.0 0.7 copy-start.15

commit v2 on v1

--- a/solution.py
+++ b/solution.py
@@ -15,6 +15,7 @@
 BF = jnp.bfloat16
 F32 = jnp.float32
 VMEM_LIMIT = 48 * 1024 * 1024
+MESH = pl.DeviceIdType.MESH
 
 
 def lane_pick(rows, lane_index):
@@ -25,7 +26,7 @@
     return jnp.broadcast_to(row, (LANES, LANES)).T
 
 
-def route_kernel(rows_dev, per_pair, ids_smem, ids_ref, table_ref, ask_ref, pos_ref, home_ref, rows_scr):
+def route_kernel(rows_dev, per_pair, ids_smem, ids_ref, table_ref, ask_ref, pos_ref, rows_scr):
     tiles = ids_ref.shape[0]
     shift_rows = rows_dev.bit_length() - 1
 
@@ -66,9 +67,6 @@
         pos_ref[t : t + 1, :] = jnp.sum(
             jnp.where(diag, pos, 0.0), axis=0, keepdims=True
         ).astype(jnp.int32)
-        home_ref[t : t + 1, :] = jnp.sum(
-            jnp.where(diag, home.astype(F32), 0.0), axis=0, keepdims=True
-        ).astype(jnp.int32)
     ask_ref[...] = (acc[:, :LANES] + 256.0 * acc[:, LANES:]).astype(jnp.int32)
 
 
@@ -80,56 +78,215 @@
         out_shape=(
             jax.ShapeDtypeStruct((LANES, LANES), jnp.int32),
             jax.ShapeDtypeStruct((tiles, LANES), jnp.int32),
-            jax.ShapeDtypeStruct((tiles, LANES), jnp.int32),
         ),
         in_specs=[pl.BlockSpec(memory_space=pltpu.SMEM), vm, vm],
-        out_specs=(vm, vm, vm),
+        out_specs=(vm, vm),
         scratch_shapes=[pltpu.VMEM((tiles * LANES, LANES), jnp.int32)],
         compiler_params=pltpu.CompilerParams(vmem_limit_bytes=VMEM_LIMIT),
         name="route",
     )(ids, ids, table)
 
 
-def serve_kernel(per_pair, ask_smem, store_ref, out_ref, store_scr, stage):
+def peer_of(step, stores, scorers):
+    store = lax.rem(lax.axis_index("store") + step // scorers, stores)
+    scorer = lax.rem(lax.axis_index("scorer") + lax.rem(step, scorers), scorers)
+    return store, scorer
+
+
+def exchange_kernel(
+    stores,
+    scorers,
+    per_pair,
+    ask_ref,
+    store_ref,
+    sizes_ref,
+    rows_out,
+    sizes_out,
+    ask_in,
+    ask_smem,
+    store_scr,
+    size_scr,
+    stage,
+    size_stage,
+    rows_send,
+    sizes_send,
+    send_sems,
+    recv_sems,
+    local_sem,
+):
+    pairs = stores * scorers
+    me = lax.axis_index("store") * scorers + lax.axis_index("scorer")
+    barrier = pltpu.get_barrier_semaphore()
+
+    def greet(i, carry):
+        pl.semaphore_signal(barrier, inc=1, device_id=peer_of(i, stores, scorers), device_id_type=MESH)
+        return carry
+
+    lax.fori_loop(1, pairs, greet, 0)
     store_scr[...] = store_ref[...].astype(F32)
-    pairs = ask_smem.shape[0]
-    group = 4
-
-    def some(g, carry):
-        for q in range(group):
-            for j in range(per_pair):
-                row = ask_smem[g * group + q, j]
-                stage[pl.ds(q * per_pair + j, 1), :] = store_scr[pl.ds(row, 1), :]
-        out_ref[pl.ds(g * (group * per_pair), group * per_pair), :] = stage[...].astype(BF)
-        return carry
-
-    lax.fori_loop(0, pairs // group, some, 0)
-
-
-def serve(asked, store_rows, per_pair):
-    pairs = asked.shape[0]
+    for t in range(sizes_ref.shape[0]):
+        size_scr[t * LANES : (t + 1) * LANES, :] = column_of(sizes_ref[t : t + 1, :])
+    pl.semaphore_wait(barrier, pairs - 1)
+
+    def ask(i, carry):
+        store, scorer = peer_of(i, stores, scorers)
+        pltpu.make_async_remote_copy(
+            src_ref=ask_ref.at[store * scorers + scorer],
+            dst_ref=ask_in.at[me],
+            send_sem=send_sems.at[0],
+            recv_sem=recv_sems.at[0],
+            device_id=(store, scorer),
+            device_id_type=MESH,
+        ).start()
+        return carry
+
+    lax.fori_loop(1, pairs, ask, 0)
+    ask_in[me] = ask_ref[me]
+
+    def settle(ref, sem):
+        part = ref.at[pl.ds(0, pairs - 1)]
+        pltpu.make_async_copy(part, part, sem).wait()
+
+    settle(ask_in, recv_sems.at[0])
+    down = pltpu.make_async_copy(ask_in, ask_smem, local_sem)
+    down.start()
+    down.wait()
+
+    lane = lax.broadcasted_iota(jnp.int32, (per_pair, LANES), 1)
+    sub = lax.broadcasted_iota(jnp.int32, (per_pair, LANES), 0)
+
+    def collect(who):
+        for j in range(per_pair):
+            row = ask_smem[who, 0, j]
+            stage[pl.ds(j, 1), :] = store_scr[pl.ds(row, 1), :]
+            size_stage[pl.ds(j, 1), :] = size_scr[pl.ds(row, 1), :]
+        sizes = jnp.sum(jnp.where(lane == sub, size_stage[...], 0.0), axis=0, keepdims=True)
+        return stage[...].astype(BF), sizes
+
+    def answer(i, carry):
+        store, scorer = peer_of(i, stores, scorers)
+        who = store * scorers + scorer
+        rows, sizes = collect(who)
+        rows_send[who] = rows
+        sizes_send[who] = sizes
+        pltpu.make_async_remote_copy(
+            src_ref=rows_send.at[who],
+            dst_ref=rows_out.at[me],
+            send_sem=send_sems.at[1],
+            recv_sem=recv_sems.at[1],
+            device_id=(store, scorer),
+            device_id_type=MESH,
+        ).start()
+        pltpu.make_async_remote_copy(
+            src_ref=sizes_send.at[who],
+            dst_ref=sizes_out.at[me],
+            send_sem=send_sems.at[2],
+            recv_sem=recv_sems.at[2],
+            device_id=(store, scorer),
+            device_id_type=MESH,
+        ).start()
+        return carry
+
+    lax.fori_loop(1, pairs, answer, 0)
+    rows, sizes = collect(me)
+    rows_out[me] = rows
+    sizes_out[me] = sizes
+    settle(ask_in, send_sems.at[0])
+    settle(rows_send, send_sems.at[1])
+    settle(sizes_send, send_sems.at[2])
+    settle(rows_out, recv_sems.at[1])
+    settle(sizes_out, recv_sems.at[2])
+
+
+def exchange(ask, store_rows, logsize, stores, scorers, per_pair):
+    pairs = stores * scorers
     width = store_rows.shape[1]
     vm = pl.BlockSpec(memory_space=pltpu.VMEM)
     return pl.pallas_call(
-        functools.partial(serve_kernel, per_pair),
-        out_shape=jax.ShapeDtypeStruct((pairs * per_pair, width), BF),
-        in_specs=[pl.BlockSpec(memory_space=pltpu.SMEM), vm],
+        functools.partial(exchange_kernel, stores, scorers, per_pair),
+        out_shape=(
+            jax.ShapeDtypeStruct((pairs, per_pair, width), BF),
+            jax.ShapeDtypeStruct((pairs, 1, LANES), F32),
+        ),
+        in_specs=[vm, vm, vm],
+        out_specs=(vm, vm),
+        scratch_shapes=[
+            pltpu.VMEM((pairs, 1, LANES), jnp.int32),
+            pltpu.SMEM((pairs, 1, LANES), jnp.int32),
+            pltpu.VMEM(store_rows.shape, F32),
+            pltpu.VMEM((store_rows.shape[0], LANES), F32),
+            pltpu.VMEM((per_pair, width), F32),
+            pltpu.VMEM((per_pair, LANES), F32),
+            pltpu.VMEM((pairs, per_pair, width), BF),
+            pltpu.VMEM((pairs, 1, LANES), F32),
+            pltpu.SemaphoreType.DMA((3,)),
+            pltpu.SemaphoreType.DMA((3,)),
+            pltpu.SemaphoreType.DMA,
+        ],
+        compiler_params=pltpu.CompilerParams(
+            vmem_limit_bytes=VMEM_LIMIT, collective_id=0, has_side_effects=True
+        ),
+        name="exchange",
+    )(ask, store_rows, logsize)
+
+
+def gather_kernel(scorers, table_ref, out_ref, landed, send_sem, recv_sem):
+    part = out_ref.shape[0]
+    store = lax.axis_index("store")
+    me = lax.axis_index("scorer")
+    barrier = pltpu.get_barrier_semaphore()
+
+    def greet(i, carry):
+        pl.semaphore_signal(
+            barrier, inc=1, device_id=(store, lax.rem(me + i, scorers)), device_id_type=MESH
+        )
+        return carry
+
+    lax.fori_loop(1, scorers, greet, 0)
+    pl.semaphore_wait(barrier, scorers - 1)
+
+    def send(i, carry):
+        to = lax.rem(me + i, scorers)
+        pltpu.make_async_remote_copy(
+            src_ref=table_ref.at[to],
+            dst_ref=landed.at[i - 1],
+            send_sem=send_sem,
+            recv_sem=recv_sem,
+            device_id=(store, to),
+            device_id_type=MESH,
+        ).start()
+        return carry
+
+    lax.fori_loop(1, scorers, send, 0)
+    pltpu.make_async_copy(landed, landed, send_sem).wait()
+    pltpu.make_async_copy(landed, landed, recv_sem).wait()
+    out_ref[...] = table_ref[me] + jnp.sum(landed[...], axis=0)
+
+
+def gather_spans(table, scorers):
+    lines = table.shape[0] // scorers
+    vm = pl.BlockSpec(memory_space=pltpu.VMEM)
+    return pl.pallas_call(
+        functools.partial(gather_kernel, scorers),
+        out_shape=jax.ShapeDtypeStruct((lines, LANES), F32),
+        in_specs=[vm],
         out_specs=vm,
         scratch_shapes=[
-            pltpu.VMEM(store_rows.shape, F32),
-            pltpu.VMEM((4 * per_pair, width), F32),
+            pltpu.VMEM((scorers - 1, lines, LANES), F32),
+            pltpu.SemaphoreType.DMA,
+            pltpu.SemaphoreType.DMA,
         ],
-        compiler_params=pltpu.CompilerParams(vmem_limit_bytes=VMEM_LIMIT),
-        name="serve",
-    )(asked, store_rows)
+        compiler_params=pltpu.CompilerParams(collective_id=1, has_side_effects=True),
+        name="gather_spans",
+    )(table.reshape(scorers, lines, LANES))
 
 
 def score_kernel(
+    per_pair,
     pos_smem,
-    home_smem,
     valid_smem,
     count_smem,
-    home_ref,
+    pos_ref,
     sizes_ref,
     arrived_ref,
     cand_ref,
@@ -156,6 +313,7 @@
     per_req = slots // LANES
     head_size = width // HEADS
     step = 256
+    pair_shift = per_pair.bit_length() - 1
 
     @pl.when(r == 0)
     def _():
@@ -174,10 +332,9 @@
         col = lax.rem(b, LANES // unroll) * unroll
         for u in range(unroll):
             at = pos_smem[line, col + u]
-            home = home_smem[line, col + u]
             x_scr[pl.ds(b * unroll + u, 1), :] = arr_scr[pl.ds(at, 1), :]
             sz_scr[pl.ds(b * unroll + u, 1), :] = sizes_ref[
-                pl.ds(lax.shift_right_logical(home, 7), 1), :
+                pl.ds(lax.shift_right_logical(at, pair_shift), 1), :
             ]
         return carry
 
@@ -188,8 +345,8 @@
     values = jnp.dot(x, wv_ref[...], preferred_element_type=F32).astype(BF).astype(F32)
     sizes = []
     for t in range(per_req):
-        home_col = column_of(home_ref[0, t : t + 1, :])
-        size = lane_pick(sz_scr[t * LANES : (t + 1) * LANES, :], home_col & (LANES - 1))
+        pos_col = column_of(pos_ref[0, t : t + 1, :])
+        size = lane_pick(sz_scr[t * LANES : (t + 1) * LANES, :], pos_col & (per_pair - 1))
         slot = lax.broadcasted_iota(jnp.int32, (LANES, LANES), 0) + t * LANES
         sizes.append(jnp.where(slot < valid, size, -1e30))
     sizes = jnp.concatenate(sizes, axis=0)
@@ -247,7 +404,7 @@
         )
 
 
-def score(pos, home, valid, count, sizes, arrived, candidates, rows, weights, lines):
+def score(pos, per_pair, valid, count, sizes, arrived, candidates, rows, weights, lines):
     reqs, cands, width = candidates.shape
     slots = pos.size // reqs
     sm = pl.BlockSpec(memory_space=pltpu.SMEM)
@@ -255,14 +412,13 @@
     def whole(a):
         return pl.BlockSpec(a.shape, lambda r, n=a.ndim: (0,) * n)
 
-    home3 = home.reshape(reqs, slots // LANES, LANES)
+    pos3 = pos.reshape(reqs, slots // LANES, LANES)
     rows3 = rows.reshape(reqs, 1, cands)
     return pl.pallas_call(
-        score_kernel,
+        functools.partial(score_kernel, per_pair),
         grid=(reqs,),
         out_shape=jax.ShapeDtypeStruct((lines, LANES), F32),
         in_specs=[
-            sm,
             sm,
             sm,
             sm,
@@ -283,7 +439,7 @@
         ],
         compiler_params=pltpu.CompilerParams(vmem_limit_bytes=VMEM_LIMIT),
         name="score",
-    )(pos, home, valid, count, home3, sizes, arrived, candidates, rows3, *weights)
+    )(pos, valid, count, pos3, sizes, arrived, candidates, rows3, *weights)
 
 
 def on_device(
@@ -311,18 +467,19 @@
     slot_total = cluster_ids.size
     per_pair = slot_total // device_count
     reqs, cands = candidate_row.shape
-    sizes = lax.all_gather(cluster_logsize, AXES, tiled=True)
-    sizes = sizes.astype(F32).reshape(-1, LANES)
-    ask, pos, home = route(
+    ask, pos = route(
         cluster_ids.reshape(-1, LANES), cluster_home.reshape(-1, LANES), rows_dev, per_pair
     )
-    asked = lax.all_to_all(
-        ask[:device_count, :per_pair], AXES, split_axis=0, concat_axis=0, tiled=True
+    arrived, sizes = exchange(
+        ask.reshape(device_count, 1, LANES),
+        store_rows,
+        cluster_logsize.astype(F32).reshape(-1, LANES),
+        device_count // scorer_count,
+        scorer_count,
+        per_pair,
     )
-    found = serve(asked, store_rows, per_pair)
-    arrived = lax.all_to_all(
-        found.reshape(device_count, per_pair, width), AXES, split_axis=0, concat_axis=0, tiled=True
-    ).reshape(slot_total, width)
+    arrived = arrived.reshape(slot_total, width)
+    sizes = sizes.reshape(device_count, LANES)
     weights = (
         query_proj,
         key_proj,
@@ -336,11 +493,9 @@
     )
     lines = scorer_count * (reqs * cands // 2) // LANES
     table = score(
-        pos, home, valid_count, cand_count, sizes, arrived, candidates, candidate_row, weights, lines
+        pos, per_pair, valid_count, cand_count, sizes, arrived, candidates, candidate_row, weights, lines
     )
-    blocks = table.reshape(scorer_count, lines // scorer_count, LANES)
-    blocks = lax.all_to_all(blocks, "scorer", split_axis=0, concat_axis=0, tiled=True)
-    return jnp.sum(blocks, axis=0).reshape(-1)
+    return gather_spans(table, scorer_count).reshape(-1)
 
 
 def solution(mesh):

time: 197 us -> 142 us (0.72)
  blocking collectives: 104 us -> 0 us
  Pallas kernels: 72.6 us -> 124 us
  starting transfers between devices: 4.78 us -> 0 us
    all_gather x1 -> x0, blocking collectives: 71.5 us -> none  [on_device(): sizes = lax.all_gather(cluster_logsize, AXES, tiled=True)]
    pallas_call x2 -> x3, Pallas kernels: 62 us -> 114 us  [the longest x1 52.5 us: score(): pl.pallas_call(functools.partial(score_kernel, per_pair), grid=(reqs,), o...]
    all_to_all x2 -> x0, blocking collectives: 32.8 us -> none  [the longest x1 20.4 us: on_device(): lax.all_to_all(ask[:device_count, :per_pair], AXES, split_axis=0, concat_...]
    all_to_all x1 -> x0, starting transfers between devices: 4.78 us -> none  [on_device(): lax.all_to_all(found.reshape(device_count, per_pair, width), AXES, split_...]
    unnamed x36 -> x29, local copies, waits for them, and re-layouts: 11.7 us -> 12.7 us
  transfers between devices with their start and end apart: 1 -> 0, of which waited for: 0 -> 0; matrix products, arithmetic and copies ran while one was open for 0% -> 0% of each run, Pallas kernels for 0% -> 0%
where the time goes in v2:
time: 142 us; the launch traced here: 140 us
  Pallas kernels  124 us (87%)
  local copies, waits for them, and re-layouts  14.8 us (10%)
    pallas_call x1, Pallas kernels, score(): pl.pallas_call(functools.partial(score_kernel, per_pair), grid=(reqs,), o...  52.5 us
    pallas_call x1, Pallas kernels, exchange(): pl.pallas_call(functools.partial(exchange_kernel, stores, scorers, per_pa...  51.9 us
    unnamed x29, local copies, waits for them, and re-layouts  12.7 us
    pallas_call x1, Pallas kernels, route(): pl.pallas_call(functools.partial(route_kernel, rows_dev, per_pair), out_s...  10.5 us
    pallas_call x1, Pallas kernels, gather_spans(): pl.pallas_call(functools.partial(gather_kernel, scorers), out_shape=jax.S...  9.36 us

profile of v2, /device:TPU:0, one launch (start us, length us, event | category | flops | bytes accessed | tf_op | source)
XLA Modules:
  0.0 140.0 jit_solution(12585984085455268256)
XLA Ops:
  0.0 0.8 bitcast_convert_fusion.sizes_ref
  0.8 0.7 broadcast_in_dim.2.sp_ref
  1.5 0.7 reshape.40.ids_smem.ids_ref
  2.2 0.7 reshape.48.row_ref
  3.0 1.2 copy-done.1
  4.2 10.5 %route.1 = (s32[128,128]{1,0:T(8,128)S(1)}, s32[32,128]{1,0:T(8,128)S(1)}) custom-call(s32[32,128]{1,0:T(8,128)S(1)} %reshape.40.ids_smem.ids_ref, s32[32,128]{1,0:T(8,128)S(1)} %reshape.40.ids_smem.ids_ref, s32[2048,128]{1,0:T(8,128)S(1)} %bitcast.13), custom_call_target="tpu_custom_call" | custom-call | tf_op jit(solution)/shard_map/route/pallas_call | solution.py:76
  14.7 0.0 copy-start.2
  14.7 1.2 copy-done.2
  15.9 51.9 %exchange.1 = (bf16[128,32,256]{2,1,0:T(8,128)(2,1)S(1)}, f32[128,1,128]{2,1,0:T(1,128)S(1)}) custom-call(s32[128,1,128]{2,1,0:T(1,128)S(1)} %bitcast.17, bf16[2048,256]{1,0:T(8,128)(2,1)S(1)} %copy-done.2, f32[16,128]{1,0:T(8,128)S(1)} %bitcast_convert_fusion.sizes_ref), custom_call_target="tpu_custom_call" | custom-call | tf_op jit(solution)/shard_map/exchange/pallas_call | solution.py:205
  67.8 0.0 copy-start.3
  67.8 1.0 copy-done.3
  68.8 0.9 copy-done.5
  69.8 0.9 copy-done.6
  70.7 0.9 copy-done.7
  71.6 0.9 copy-done.8
  72.5 0.9 copy-done.9
  73.4 0.7 copy-done.10
  74.1 0.7 copy-done.11
  74.8 0.7 copy-done.12
  75.4 0.7 copy-done.13
  76.1 52.5 %score.1 = f32[256,128]{1,0:T(8,128)S(1)} custom-call(s32[32,128]{1,0:T(8,128)S(1)} %get-tuple-element.9.pos_smem, s32[8]{0:T(128)S(1)} %copy-done.12, s32[8]{0:T(128)S(1)} %copy-done.13, s32[8,4,128]{2,1,0:T(4,128)S(1)} %bitcast.16, f32[128,128]{1,0:T(8,128)S(1)} %bitcast.15, bf16[4096,256]{1,0:T(8,128)(2,1)S(1)} %bitcast.12, ...), custom_call_target="tpu_custom_call" | custom-call | tf_op jit(solution)/shard_map/score/pallas_call | solution.py:417
  128.6 0.6 copy-done.4
  129.3 9.4 %gather_spans.1 = f32[16,128]{1,0:T(8,128)} custom-call(f32[16,16,128]{2,1,0:T(8,128)} %bitcast.14), custom_call_target="tpu_custom_call" | custom-call | tf_op jit(solution)/shard_map/gather_spans/pallas_call | solution.py:269
  138.7 1.3 copy.19
  (13 shorter events, 0.0 us)
Async XLA Ops:
  0.0 67.8 %copy-start = (bf16[8,512,256]{2,1,0:T(8,128)(2,1)S(1)}, bf16[8,512,256]{2,1,0:T(8,128)(2,1)}, u32[]{:S(2)}) copy-start(bf16[8,512,256]{2,1,0:T(8,128)(2,1)} %cand_ref.1) | copy-start | bytes 6291460
  3.0 1.2 copy-start.1
  14.7 1.2 copy-start.2
  67.8 1.0 copy-start.3
  68.8 0.9 copy-start.5
  69.8 0.9 copy-start.6
  70.7 0.9 copy-start.7
  71.6 0.9 copy-start.8
  72.5 0.9 copy-start.9
  73.4 0.7 copy-start.10
  74.1 0.7 copy-start.11
  74.8 0.7 copy-start.12
  75.4 0.7 copy-start.13
  128.6 0.7 copy-start.4

commit v3 on v2

v3 whole, which is shorter than its diff:
```python
import functools

import jax
import jax.numpy as jnp
from jax import lax
from jax.experimental import pallas as pl
from jax.experimental.pallas import tpu as pltpu
from jax.sharding import PartitionSpec as P

HEADS = 4
CHUNK = 16
AXES = ("store", "scorer")
LANES = 128
NT = (((1,), (1,)), ((), ()))
TN = (((0,), (0,)), ((), ()))
BF = jnp.bfloat16
F32 = jnp.float32
VMEM_LIMIT = 48 * 1024 * 1024
MESH = pl.DeviceIdType.MESH


def lane_pick(rows, lane_index):
    return jnp.take_along_axis(rows, lane_index, axis=1)


def column_of(row):
    return jnp.broadcast_to(row, (LANES, LANES)).T


def route_kernel(rows_dev, per_pair, ids_smem, valid_smem, ids_ref, table_ref, ask_ref, plan_ref, rows_scr):
    reqs, slots = ids_ref.shape
    per_req = slots // LANES
    shift_rows = rows_dev.bit_length() - 1

    def fetch(r, carry):
        start = pl.multiple_of(r * slots, slots)
        for u in range(slots):
            c = ids_smem[r, u]
            rows_scr[pl.ds(start + u, 1), :] = table_ref[pl.ds(lax.shift_right_logical(c, 7), 1), :]
        return carry

    lax.fori_loop(0, reqs, fetch, 0)
    lane = lax.broadcasted_iota(jnp.int32, (LANES, LANES), 1)
    sub = lax.broadcasted_iota(jnp.int32, (LANES, LANES), 0)
    lower = jnp.where(sub >= lane, 1.0, 0.0).astype(BF)
    before = jnp.where(sub < lane, 1.0, 0.0).astype(BF)
    ones = jnp.ones((LANES, LANES), BF)
    base = jnp.zeros((1, LANES), F32)
    acc = jnp.zeros((LANES, 2 * LANES), F32)
    bases = []
    for t in range(reqs * per_req):
        r, q = t // per_req, t % per_req
        if q == 0:
            bases.append(base)
        ids_col = column_of(ids_ref[r : r + 1, q * LANES : (q + 1) * LANES])
        home = lane_pick(rows_scr[t * LANES : (t + 1) * LANES, :], ids_col & (LANES - 1))
        hot = lax.shift_right_logical(home, shift_rows) == lane
        hot = jnp.where(sub + q * LANES < valid_smem[r], jnp.where(hot, 1.0, 0.0), 0.0)
        hot_b = hot.astype(BF)
        incl = jnp.dot(lower, hot_b, preferred_element_type=F32)
        picked = (hot * (incl + (base - 1.0))).astype(BF)
        rank = jnp.dot(picked, ones, preferred_element_type=F32).astype(jnp.int32)
        base = base + incl[LANES - 1 : LANES, :]
        low = (home & 255).astype(F32)
        high = (lax.shift_right_logical(home, 8) & ((rows_dev >> 8) - 1)).astype(F32)
        at = rank == lane
        parts = jnp.concatenate(
            [jnp.where(at, low, 0.0), jnp.where(at, high, 0.0)], axis=1
        ).astype(BF)
        acc = acc + lax.dot_general(hot_b, parts, TN, preferred_element_type=F32)
    bases.append(base)
    ask_ref[...] = (acc[:, :LANES] + 256.0 * acc[:, LANES:]).astype(jnp.int32)
    starts = jnp.concatenate(bases[:reqs], axis=0)
    counts = jnp.concatenate(bases[1:], axis=0) - starts
    spots = jnp.dot(counts.astype(BF), before, preferred_element_type=F32)
    source = lax.broadcasted_iota(jnp.int32, (reqs, LANES), 1) * per_pair
    plan_ref[0:reqs, :] = source + starts.astype(jnp.int32)
    plan_ref[reqs : 2 * reqs, :] = spots.astype(jnp.int32)
    plan_ref[2 * reqs : 3 * reqs, :] = counts.astype(jnp.int32)
    most = jnp.max(counts, axis=1, keepdims=True)
    plan_ref[3 * reqs :, :] = jnp.broadcast_to(most, (reqs, LANES)).astype(jnp.int32)


def route(ids, valid, table, rows_dev, per_pair):
    reqs, slots = ids.shape
    sm = pl.BlockSpec(memory_space=pltpu.SMEM)
    vm = pl.BlockSpec(memory_space=pltpu.VMEM)
    return pl.pallas_call(
        functools.partial(route_kernel, rows_dev, per_pair),
        out_shape=(
            jax.ShapeDtypeStruct((LANES, LANES), jnp.int32),
            jax.ShapeDtypeStruct((4 * reqs, LANES), jnp.int32),
        ),
        in_specs=[sm, sm, vm, vm],
        out_specs=(vm, vm),
        scratch_shapes=[pltpu.VMEM((reqs * slots, LANES), jnp.int32)],
        compiler_params=pltpu.CompilerParams(vmem_limit_bytes=VMEM_LIMIT),
        name="route",
    )(ids, valid, ids, table)


def peer_of(step, stores, scorers):
    store = lax.rem(lax.axis_index("store") + step // scorers, stores)
    scorer = lax.rem(lax.axis_index("scorer") + lax.rem(step, scorers), scorers)
    return store, scorer


def exchange_kernel(
    stores,
    scorers,
    per_pair,
    ask_ref,
    store_ref,
    sizes_ref,
    rows_out,
    sizes_out,
    ask_in,
    ask_smem,
    left_scr,
    right_scr,
    size_scr,
    left,
    right,
    size_stage,
    rows_send,
    sizes_send,
    send_sems,
    recv_sems,
    local_sem,
):
    pairs = stores * scorers
    me = lax.axis_index("store") * scorers + lax.axis_index("scorer")
    barrier = pltpu.get_barrier_semaphore()

    def greet(i, carry):
        pl.semaphore_signal(barrier, inc=1, device_id=peer_of(i, stores, scorers), device_id_type=MESH)
        return carry

    lax.fori_loop(1, pairs, greet, 0)
    left_scr[...] = store_ref[:, :LANES].astype(F32)
    right_scr[...] = store_ref[:, LANES:].astype(F32)
    offsets = sizes_ref[...].astype(F32)
    for t in range(sizes_ref.shape[0]):
        size_scr[t * LANES : (t + 1) * LANES, :] = column_of(offsets[t : t + 1, :])
    pl.semaphore_wait(barrier, pairs - 1)

    def ask(i, carry):
        store, scorer = peer_of(i, stores, scorers)
        pltpu.make_async_remote_copy(
            src_ref=ask_ref.at[store * scorers + scorer],
            dst_ref=ask_in.at[me],
            send_sem=send_sems.at[0],
            recv_sem=recv_sems.at[0],
            device_id=(store, scorer),
            device_id_type=MESH,
        ).start()
        return carry

    lax.fori_loop(1, pairs, ask, 0)
    ask_in[me] = ask_ref[me]

    def settle(ref, sem):
        part = ref.at[pl.ds(0, pairs - 1)]
        pltpu.make_async_copy(part, part, sem).wait()

    settle(ask_in, recv_sems.at[0])
    down = pltpu.make_async_copy(ask_in, ask_smem, local_sem)
    down.start()
    down.wait()

    lane = lax.broadcasted_iota(jnp.int32, (per_pair, LANES), 1)
    sub = lax.broadcasted_iota(jnp.int32, (per_pair, LANES), 0)
    sub = sub + lax.rem(me, LANES // per_pair) * per_pair

    def collect(who):
        for j in range(per_pair):
            row = ask_smem[who, 0, j]
            left[pl.ds(j, 1), :] = left_scr[pl.ds(row, 1), :]
            right[pl.ds(j, 1), :] = right_scr[pl.ds(row, 1), :]
            size_stage[pl.ds(j, 1), :] = size_scr[pl.ds(row, 1), :]
        sizes = jnp.sum(jnp.where(lane == sub, size_stage[...], 0.0), axis=0, keepdims=True)
        return left[...].astype(BF), right[...].astype(BF), sizes

    def answer(i, carry):
        store, scorer = peer_of(i, stores, scorers)
        who = store * scorers + scorer
        rows_send[who, :, :LANES], rows_send[who, :, LANES:], sizes_send[who] = collect(who)
        pltpu.make_async_remote_copy(
            src_ref=rows_send.at[who],
            dst_ref=rows_out.at[me],
            send_sem=send_sems.at[1],
            recv_sem=recv_sems.at[1],
            device_id=(store, scorer),
            device_id_type=MESH,
        ).start()
        pltpu.make_async_remote_copy(
            src_ref=sizes_send.at[who],
            dst_ref=sizes_out.at[me],
            send_sem=send_sems.at[2],
            recv_sem=recv_sems.at[2],
            device_id=(store, scorer),
            device_id_type=MESH,
        ).start()
        return carry

    lax.fori_loop(1, pairs, answer, 0)
    rows_out[me, :, :LANES], rows_out[me, :, LANES:], sizes_out[me] = collect(me)
    settle(ask_in, send_sems.at[0])
    settle(rows_send, send_sems.at[1])
    settle(sizes_send, send_sems.at[2])
    settle(rows_out, recv_sems.at[1])
    settle(sizes_out, recv_sems.at[2])


def exchange(ask, store_rows, logsize, stores, scorers, per_pair):
    pairs = stores * scorers
    width = store_rows.shape[1]
    vm = pl.BlockSpec(memory_space=pltpu.VMEM)
    return pl.pallas_call(
        functools.partial(exchange_kernel, stores, scorers, per_pair),
        out_shape=(
            jax.ShapeDtypeStruct((pairs, per_pair, width), BF),
            jax.ShapeDtypeStruct((pairs, 1, LANES), F32),
        ),
        in_specs=[vm, vm, vm],
        out_specs=(vm, vm),
        scratch_shapes=[
            pltpu.VMEM((pairs, 1, LANES), jnp.int32),
            pltpu.SMEM((pairs, 1, LANES), jnp.int32),
            pltpu.VMEM((store_rows.shape[0], LANES), F32),
            pltpu.VMEM((store_rows.shape[0], LANES), F32),
            pltpu.VMEM((store_rows.shape[0], LANES), F32),
            pltpu.VMEM((per_pair, LANES), F32),
            pltpu.VMEM((per_pair, LANES), F32),
            pltpu.VMEM((per_pair, LANES), F32),
            pltpu.VMEM((pairs, per_pair, width), BF),
            pltpu.VMEM((pairs, 1, LANES), F32),
            pltpu.SemaphoreType.DMA((3,)),
            pltpu.SemaphoreType.DMA((3,)),
            pltpu.SemaphoreType.DMA,
        ],
        compiler_params=pltpu.CompilerParams(
            vmem_limit_bytes=VMEM_LIMIT, collective_id=0, has_side_effects=True
        ),
        name="exchange",
    )(ask, store_rows, logsize)


def gather_kernel(scorers, table_ref, out_ref, landed, send_sem, recv_sem):
    part = out_ref.shape[0]
    store = lax.axis_index("store")
    me = lax.axis_index("scorer")
    barrier = pltpu.get_barrier_semaphore()

    def greet(i, carry):
        pl.semaphore_signal(
            barrier, inc=1, device_id=(store, lax.rem(me + i, scorers)), device_id_type=MESH
        )
        return carry

    lax.fori_loop(1, scorers, greet, 0)
    pl.semaphore_wait(barrier, scorers - 1)

    def send(i, carry):
        to = lax.rem(me + i, scorers)
        pltpu.make_async_remote_copy(
            src_ref=table_ref.at[to],
            dst_ref=landed.at[i - 1],
            send_sem=send_sem,
            recv_sem=recv_sem,
            device_id=(store, to),
            device_id_type=MESH,
        ).start()
        return carry

    lax.fori_loop(1, scorers, send, 0)
    pltpu.make_async_copy(landed, landed, send_sem).wait()
    pltpu.make_async_copy(landed, landed, recv_sem).wait()
    out_ref[...] = table_ref[me] + jnp.sum(landed[...], axis=0)


def gather_spans(table, scorers):
    lines = table.shape[0] // scorers
    vm = pl.BlockSpec(memory_space=pltpu.VMEM)
    return pl.pallas_call(
        functools.partial(gather_kernel, scorers),
        out_shape=jax.ShapeDtypeStruct((lines, LANES), F32),
        in_specs=[vm],
        out_specs=vm,
        scratch_shapes=[
            pltpu.VMEM((scorers - 1, lines, LANES), F32),
            pltpu.SemaphoreType.DMA,
            pltpu.SemaphoreType.DMA,
        ],
        compiler_params=pltpu.CompilerParams(collective_id=1, has_side_effects=True),
        name="gather_spans",
    )(table.reshape(scorers, lines, LANES))


def score_kernel(
    per_pair,
    plan_smem,
    valid_smem,
    count_smem,
    sizes_ref,
    arrived_ref,
    cand_ref,
    row_ref,
    wq_ref,
    wk_ref,
    wv_ref,
    wo_ref,
    m1_ref,
    b1_ref,
    m2_ref,
    b2_ref,
    sp_ref,
    out_ref,
    left_scr,
    right_scr,
    size_scr,
    x_left,
    x_right,
    x_size,
    k_scr,
    v_scr,
    ctx_scr,
):
    r = pl.program_id(0)
    reqs = pl.num_programs(0)
    total_slots, width = arrived_ref.shape
    slots = ctx_scr.shape[0]
    cands = cand_ref.shape[1]
    pairs = sizes_ref.shape[0]
    head_size = width // HEADS
    copies = ((left_scr, x_left), (right_scr, x_right), (size_scr, x_size))

    @pl.when(r == 0)
    def _():
        left_scr[:total_slots, :] = arrived_ref[:, :LANES].astype(F32)
        right_scr[:total_slots, :] = arrived_ref[:, LANES:].astype(F32)
        group = LANES // per_pair
        one = lax.broadcasted_iota(jnp.int32, (pairs // group, pairs), 1) // group
        one = one == lax.broadcasted_iota(jnp.int32, (pairs // group, pairs), 0)
        packed = jnp.dot(
            jnp.where(one, 1.0, 0.0).astype(BF),
            sizes_ref[...].astype(BF),
            preferred_element_type=F32,
        )
        for t in range(pairs // group):
            size_scr[t * LANES : (t + 1) * LANES, :] = column_of(packed[t : t + 1, :])
        for held, taken in copies:
            held[total_slots:, :] = jnp.zeros((CHUNK, LANES), F32)
            taken[...] = jnp.zeros_like(taken)
        out_ref[...] = jnp.zeros_like(out_ref)

    valid = valid_smem[r]
    count = count_smem[r]

    for s in range(pairs):
        at = plan_smem[r, s]
        to = plan_smem[r + reqs, s]
        for held, taken in copies:
            taken[pl.ds(to, CHUNK), :] = held[pl.ds(at, CHUNK), :]

    @pl.when(plan_smem[r + 3 * reqs, 0] > CHUNK)
    def _():
        def rest(s, carry):
            at = plan_smem[r, s]
            to = plan_smem[r + reqs, s]
            left = plan_smem[r + 2 * reqs, s]
            sub = lax.broadcasted_iota(jnp.int32, (CHUNK, LANES), 0)

            @pl.when(left > CHUNK)
            def _():
                for held, taken in copies:
                    old = taken[pl.ds(to + CHUNK, CHUNK), :]
                    new = held[pl.ds(at + CHUNK, CHUNK), :]
                    taken[pl.ds(to + CHUNK, CHUNK), :] = jnp.where(sub < left - CHUNK, new, old)

            return carry

        lax.fori_loop(0, pairs, rest, 0)

    cand = cand_ref[0]
    query = jnp.dot(cand, wq_ref[...], preferred_element_type=F32)
    clane = lax.broadcasted_iota(jnp.int32, (cands, LANES), 1)
    queries = []
    for p in range(2):
        own = query[:, p * LANES : (p + 1) * LANES].astype(BF)
        other = query[:, (1 - p) * LANES : (2 - p) * LANES]
        other = jnp.where(clane == 0, 1.0, other).astype(BF)
        queries.append(jnp.concatenate([own, other] if p == 0 else [other, own], axis=1))

    def attend(live):
        x = jnp.concatenate([x_left[:live, :], x_right[:live, :]], axis=1).astype(BF)
        keys = jnp.dot(x, wk_ref[...], preferred_element_type=F32).astype(BF).astype(F32) * 0.125
        values = jnp.dot(x, wv_ref[...], preferred_element_type=F32).astype(BF).astype(F32)
        lane = lax.broadcasted_iota(jnp.int32, (live, LANES), 1)
        slot = lax.broadcasted_iota(jnp.int32, (live, LANES), 0)
        bias = jnp.where(slot < valid, x_size[:live, :], -1e30)
        bias = jnp.where(lane == 0, bias, 0.0).astype(BF)
        for h in range(HEADS):
            half = slice((h // 2) * LANES, (h // 2 + 1) * LANES)
            other = slice((1 - h // 2) * LANES, (2 - h // 2) * LANES)
            mine = (lane // head_size) == (h % 2)
            k_scr[h, :live, half] = jnp.where(mine, keys[:, half], 0.0).astype(BF)
            k_scr[h, :live, other] = bias
            v_scr[h, :live, :LANES] = jnp.where(mine, values[:, half], 0.0).astype(BF)
            v_scr[h, :live, LANES:] = jnp.where(mine, 1.0, 0.0).astype(BF)
        for p in range(2):
            total = None
            for h in (2 * p, 2 * p + 1):
                logits = lax.dot_general(
                    queries[p], k_scr[h, :live, :], NT, preferred_element_type=F32
                )
                top = jnp.max(logits, axis=1, keepdims=True)
                probs = jnp.exp(logits - top).astype(BF)
                part = jnp.dot(probs, v_scr[h, :live, :], preferred_element_type=F32)
                total = part if total is None else total + part
            ctx_scr[:, p * LANES : (p + 1) * LANES] = (
                total[:, :LANES] / total[:, LANES:]
            ).astype(BF)

    blocks = slots // LANES
    for n in range(1, blocks + 1):

        @pl.when(jnp.logical_and(valid <= n * LANES, valid > (n - 1) * LANES))
        def _(n=n):
            attend(n * LANES)

    attended = jnp.dot(ctx_scr[...], wo_ref[...], preferred_element_type=F32).astype(BF)
    hidden = jnp.dot(cand, m1_ref[:width, :], preferred_element_type=F32)
    hidden += jnp.dot(attended, m1_ref[width:, :], preferred_element_type=F32)
    hidden = jnp.maximum(hidden + b1_ref[...], 0.0).astype(BF)
    hidden = jnp.dot(hidden, m2_ref[...], preferred_element_type=F32)
    hidden = jnp.maximum(hidden + b2_ref[...], 0.0).astype(BF)
    weight = jnp.broadcast_to(sp_ref[...].astype(F32), (16, width)).astype(BF)
    score = lax.dot_general(weight, hidden, NT, preferred_element_type=F32)[0:1, :]
    slot = lax.broadcasted_iota(jnp.int32, (1, cands), 1)
    score = jnp.where(slot < count, score, 0.0)
    first = score.astype(BF).astype(F32)
    second = score - first
    row = row_ref[pl.ds(r, 1), :]
    lines = out_ref.shape[0]
    at_line = lax.broadcasted_iota(jnp.int32, (lines, cands), 0) == lax.shift_right_logical(row, 7)
    at_lane = lax.broadcasted_iota(jnp.int32, (LANES, cands), 0) == (row & (LANES - 1))
    at_lane = jnp.where(at_lane, 1.0, 0.0).astype(BF)
    out_ref[...] += lax.dot_general(
        jnp.where(at_line, first, 0.0).astype(BF), at_lane, NT, preferred_element_type=F32
    ) + lax.dot_general(
        jnp.where(at_line, second, 0.0).astype(BF), at_lane, NT, preferred_element_type=F32
    )


def score(plan, per_pair, valid, count, sizes, arrived, candidates, rows, weights, lines):
    reqs, cands, width = candidates.shape
    total_slots = arrived.shape[0]
    slots = total_slots // reqs
    sm = pl.BlockSpec(memory_space=pltpu.SMEM)

    def whole(a):
        return pl.BlockSpec(a.shape, lambda r, n=a.ndim: (0,) * n)

    held = pltpu.VMEM((total_slots + CHUNK, LANES), F32)
    taken = pltpu.VMEM((slots + 2 * CHUNK, LANES), F32)
    return pl.pallas_call(
        functools.partial(score_kernel, per_pair),
        grid=(reqs,),
        out_shape=jax.ShapeDtypeStruct((lines, LANES), F32),
        in_specs=[
            sm,
            sm,
            sm,
            whole(sizes),
            whole(arrived),
            pl.BlockSpec((1, cands, width), lambda r: (r, 0, 0)),
            whole(rows),
        ]
        + [whole(w) for w in weights],
        out_specs=pl.BlockSpec((lines, LANES), lambda r: (0, 0)),
        scratch_shapes=[
            held,
            held,
            held,
            taken,
            taken,
            taken,
            pltpu.VMEM((HEADS, slots, width), BF),
            pltpu.VMEM((HEADS, slots, width), BF),
            pltpu.VMEM((cands, width), BF),
        ],
        compiler_params=pltpu.CompilerParams(vmem_limit_bytes=VMEM_LIMIT),
        name="score",
    )(plan, valid, count, sizes, arrived, candidates, rows, *weights)


def on_device(
    store_rows,
    cluster_logsize,
    cluster_home,
    cluster_ids,
    valid_count,
    candidates,
    cand_count,
    candidate_row,
    query_proj,
    key_proj,
    value_proj,
    out_proj,
    mlp_first,
    bias_first,
    mlp_second,
    bias_second,
    score_proj,
):
    device_count = lax.axis_size(AXES)
    scorer_count = lax.axis_size("scorer")
    rows_dev, width = store_rows.shape
    slot_total = cluster_ids.size
    per_pair = slot_total // device_count
    reqs, cands = candidate_row.shape
    ask, plan = route(
        cluster_ids, valid_count, cluster_home.reshape(-1, LANES), rows_dev, per_pair
    )
    arrived, sizes = exchange(
        ask.reshape(device_count, 1, LANES),
        store_rows,
        cluster_logsize.reshape(-1, LANES),
        device_count // scorer_count,
        scorer_count,
        per_pair,
    )
    arrived = arrived.reshape(slot_total, width)
    sizes = sizes.reshape(device_count, LANES)
    weights = (
        query_proj,
        key_proj,
        value_proj,
        out_proj,
        mlp_first,
        bias_first.reshape(1, -1),
        mlp_second,
        bias_second.reshape(1, -1),
        score_proj.reshape(1, -1),
    )
    lines = scorer_count * (reqs * cands // 2) // LANES
    table = score(
        plan, per_pair, valid_count, cand_count, sizes, arrived, candidates, candidate_row, weights, lines
    )
    return gather_spans(table, scorer_count).reshape(-1)


def solution(mesh):
    split = P(AXES)
    in_specs = (
        P(AXES, None),
        split,
        P(),
        P(AXES, None),
        split,
        P(AXES, None, None),
        split,
        P(AXES, None),
    ) + (P(),) * 9
    return jax.shard_map(
        on_device, mesh=mesh, in_specs=in_specs, out_specs=split, check_vma=False
    )
```

time: 142 us -> 122 us (0.86); the launches traced: 140 us -> 122 us
  Pallas kernels: 124 us -> 106 us
    pallas_call x1, Pallas kernels: 52.5 us -> 33.2 us  [score(): pl.pallas_call(functools.partial(score_kernel, per_pair), grid=(reqs,), o...]
    unnamed x29 -> x35, local copies, waits for them, and re-layouts: 12.7 us -> 14.8 us
where the time goes in v3:
time: 122 us
  Pallas kernels  106 us (87%)
  local copies, waits for them, and re-layouts  15.6 us (13%)
    pallas_call x1, Pallas kernels, exchange(): pl.pallas_call(functools.partial(exchange_kernel, stores, scorers, per_pa...  51.8 us
    pallas_call x1, Pallas kernels, score(): pl.pallas_call(functools.partial(score_kernel, per_pair), grid=(reqs,), o...  33.2 us
    unnamed x35, local copies, waits for them, and re-layouts  14.8 us
    pallas_call x1, Pallas kernels, route(): pl.pallas_call(functools.partial(route_kernel, rows_dev, per_pair), out_s...  11.7 us
    pallas_call x1, Pallas kernels, gather_spans(): pl.pallas_call(functools.partial(gather_kernel, scorers), out_shape=jax.S...  9.36 us

profile of v3, /device:TPU:0, one launch (start us, length us, event | category | flops | bytes accessed | tf_op | source)
XLA Modules:
  0.0 121.6 jit_solution(21493070743772912)
XLA Ops:
  0.0 0.8 reshape.37.sp_ref
  0.8 1.2 %copy-done.1 = s32[262144]{0:T(1024)S(1)} copy-done((s32[262144]{0:T(1024)S(1)}, s32[262144]{0:T(1024)}, u32[]{:S(2)}) %copy-start.1) | copy-done | bytes 1048600
  2.0 0.7 copy-done.10
  2.8 0.7 copy-done.14
  3.4 11.7 %route.1 = (s32[128,128]{1,0:T(8,128)S(1)}, s32[32,128]{1,0:T(8,128)S(1)}) custom-call(s32[8,512]{1,0:T(8,128)S(1)} %copy-done.10, s32[8]{0:T(128)S(1)} %copy-done.14, s32[8,512]{1,0:T(8,128)S(1)} %copy-done.10, s32[2048,128]{1,0:T(8,128)S(1)} %bitcast.10), custom_call_target="tpu_custom_call" | custom-call | tf_op jit(solution)/shard_map/route/pallas_call | solution.py:88
  15.1 0.0 copy-start.2
  15.1 1.2 copy-done.2
  16.3 0.7 copy-done.12
  17.0 51.8 %exchange.1 = (bf16[128,32,256]{2,1,0:T(8,128)(2,1)S(1)}, f32[128,1,128]{2,1,0:T(1,128)S(1)}) custom-call(s32[128,1,128]{2,1,0:T(1,128)S(1)} %bitcast.13, bf16[2048,256]{1,0:T(8,128)(2,1)S(1)} %copy-done.2, bf16[16,128]{1,0:T(8,128)(2,1)S(1)} %bitcast.14), custom_call_target="tpu_custom_call" | custom-call | tf_op jit(solution)/shard_map/exchange/pallas_call | solution.py:219
  68.8 0.0 copy-start.4
  68.8 1.0 copy-done.4
  69.8 0.9 copy-done.5
  70.8 0.9 copy-done.6
  71.7 0.9 copy-done.7
  72.6 0.9 copy-done.8
  73.5 0.9 copy-done.9
  74.4 0.7 copy-done.11
  75.1 0.7 copy-done.13
  75.8 0.7 copy-done.15
  76.5 0.7 copy-done.16
  77.1 33.2 %score.1 = f32[256,128]{1,0:T(8,128)S(1)} custom-call(s32[32,128]{1,0:T(8,128)S(1)} %get-tuple-element.9.plan_smem, s32[8]{0:T(128)S(1)} %copy-done.14, s32[8]{0:T(128)S(1)} %copy-done.16, f32[128,128]{1,0:T(8,128)S(1)} %bitcast.12, bf16[4096,256]{1,0:T(8,128)(2,1)S(1)} %bitcast.9, bf16[8,512,256]{2,1,0:T(8,128)(2,1)S(1)} %copy-done, ...), custom_call_target="tpu_custom_call" | custom-call | tf_op jit(solution)/shard_map/score/pallas_call | solution.py:467
  110.3 0.7 copy-done.3
  111.0 9.4 %gather_spans.1 = f32[16,128]{1,0:T(8,128)} custom-call(f32[16,16,128]{2,1,0:T(8,128)} %bitcast.11), custom_call_target="tpu_custom_call" | custom-call | tf_op jit(solution)/shard_map/gather_spans/pallas_call | solution.py:285
  120.3 1.3 %copy.19 = f32[2048]{0:T(1024)} copy(f32[2048]{0:T(1024)} %bitcast.17) | data formatting | bytes 16384
  (16 shorter events, 0.0 us)
Async XLA Ops:
  0.0 68.8 %copy-start = (bf16[8,512,256]{2,1,0:T(8,128)(2,1)S(1)}, bf16[8,512,256]{2,1,0:T(8,128)(2,1)}, u32[]{:S(2)}) copy-start(bf16[8,512,256]{2,1,0:T(8,128)(2,1)} %cand_ref.1) | copy-start | bytes 6291460
  0.8 1.2 %copy-start.1 = (s32[262144]{0:T(1024)S(1)}, s32[262144]{0:T(1024)}, u32[]{:S(2)}) copy-start(s32[262144]{0:T(1024)} %param.19) | copy-start | bytes 3145732
  2.0 0.7 copy-start.10
  2.8 0.7 copy-start.14
  15.1 1.2 %copy-start.2 = (bf16[2048,256]{1,0:T(8,128)(2,1)S(1)}, bf16[2048,256]{1,0:T(8,128)(2,1)}, u32[]{:S(2)}) copy-start(bf16[2048,256]{1,0:T(8,128)(2,1)} %store_ref.1) | copy-start | bytes 3145732
  16.3 0.7 copy-start.12
  68.8 1.0 copy-start.4
  69.8 0.9 copy-start.5
  70.8 0.9 copy-start.6
  71.7 0.9 copy-start.7
  72.6 0.9 copy-start.8
  73.5 0.9 copy-start.9
  74.4 0.7 copy-start.11
  75.1 0.7 copy-start.13
  75.8 0.7 copy-start.15
  76.5 0.7 copy-start.16
  110.3 0.7 copy-start.3

commit v4 on v3

--- a/solution.py
+++ b/solution.py
@@ -9,6 +9,10 @@
 
 HEADS = 4
 CHUNK = 16
+AHEAD = 4
+TURN = 59
+FETCH_FLOPS = 40_000_000_000
+SCORE_FLOPS = 30_000_000_000
 AXES = ("store", "scorer")
 LANES = 128
 NT = (((1,), (1,)), ((), ()))
@@ -27,19 +31,91 @@
     return jnp.broadcast_to(row, (LANES, LANES)).T
 
 
-def route_kernel(rows_dev, per_pair, ids_smem, valid_smem, ids_ref, table_ref, ask_ref, plan_ref, rows_scr):
+def peer_of(step, pairs, scorers):
+    turn = lax.rem(step * TURN, pairs)
+    store = jnp.bitwise_xor(lax.axis_index("store"), turn // scorers)
+    scorer = jnp.bitwise_xor(lax.axis_index("scorer"), lax.rem(turn, scorers))
+    return store, scorer
+
+
+def fetch_kernel(
+    stores,
+    scorers,
+    per_pair,
+    ids_hbm,
+    valid_hbm,
+    table_hbm,
+    store_hbm,
+    sizes_hbm,
+    rows_out,
+    sizes_out,
+    plan_ref,
+    ids_smem,
+    valid_smem,
+    ids_ref,
+    table_ref,
+    store_ref,
+    sizes_ref,
+    homes,
+    ask_ref,
+    ask_in,
+    ask_smem,
+    left_scr,
+    right_scr,
+    size_scr,
+    left,
+    right,
+    size_stage,
+    rows_send,
+    sizes_send,
+    load_sems,
+    ask_sems,
+    down_sems,
+    send_sems,
+    recv_sems,
+):
+    pairs = stores * scorers
+    groups = ask_sems.shape[0]
+    group = pairs // groups
     reqs, slots = ids_ref.shape
     per_req = slots // LANES
+    rows_dev = store_ref.shape[0]
     shift_rows = rows_dev.bit_length() - 1
-
-    def fetch(r, carry):
+    me = lax.axis_index("store") * scorers + lax.axis_index("scorer")
+    barrier = pltpu.get_barrier_semaphore()
+
+    loads = [
+        pltpu.make_async_copy(src, dst, load_sems.at[n])
+        for n, (src, dst) in enumerate(
+            (
+                (ids_hbm, ids_smem),
+                (table_hbm, table_ref),
+                (ids_hbm, ids_ref),
+                (valid_hbm, valid_smem),
+                (store_hbm, store_ref),
+                (sizes_hbm, sizes_ref),
+            )
+        )
+    ]
+    for load in loads:
+        load.start()
+
+    def greet(i, carry):
+        pl.semaphore_signal(barrier, inc=1, device_id=peer_of(i, pairs, scorers), device_id_type=MESH)
+        return carry
+
+    lax.fori_loop(1, pairs, greet, 0)
+    for load in loads:
+        load.wait()
+
+    def look(r, carry):
         start = pl.multiple_of(r * slots, slots)
         for u in range(slots):
             c = ids_smem[r, u]
-            rows_scr[pl.ds(start + u, 1), :] = table_ref[pl.ds(lax.shift_right_logical(c, 7), 1), :]
+            homes[pl.ds(start + u, 1), :] = table_ref[pl.ds(lax.shift_right_logical(c, 7), 1), :]
         return carry
 
-    lax.fori_loop(0, reqs, fetch, 0)
+    lax.fori_loop(0, reqs, look, 0)
     lane = lax.broadcasted_iota(jnp.int32, (LANES, LANES), 1)
     sub = lax.broadcasted_iota(jnp.int32, (LANES, LANES), 0)
     lower = jnp.where(sub >= lane, 1.0, 0.0).astype(BF)
@@ -53,7 +129,7 @@
         if q == 0:
             bases.append(base)
         ids_col = column_of(ids_ref[r : r + 1, q * LANES : (q + 1) * LANES])
-        home = lane_pick(rows_scr[t * LANES : (t + 1) * LANES, :], ids_col & (LANES - 1))
+        home = lane_pick(homes[t * LANES : (t + 1) * LANES, :], ids_col & (LANES - 1))
         hot = lax.shift_right_logical(home, shift_rows) == lane
         hot = jnp.where(sub + q * LANES < valid_smem[r], jnp.where(hot, 1.0, 0.0), 0.0)
         hot_b = hot.astype(BF)
@@ -69,7 +145,8 @@
         ).astype(BF)
         acc = acc + lax.dot_general(hot_b, parts, TN, preferred_element_type=F32)
     bases.append(base)
-    ask_ref[...] = (acc[:, :LANES] + 256.0 * acc[:, LANES:]).astype(jnp.int32)
+    ask = (acc[:, :LANES] + 256.0 * acc[:, LANES:]).astype(jnp.int32)
+    ask_ref[...] = ask.reshape(pairs, 1, LANES)
     starts = jnp.concatenate(bases[:reqs], axis=0)
     counts = jnp.concatenate(bases[1:], axis=0) - starts
     spots = jnp.dot(counts.astype(BF), before, preferred_element_type=F32)
@@ -80,174 +157,156 @@
     most = jnp.max(counts, axis=1, keepdims=True)
     plan_ref[3 * reqs :, :] = jnp.broadcast_to(most, (reqs, LANES)).astype(jnp.int32)
 
-
-def route(ids, valid, table, rows_dev, per_pair):
-    reqs, slots = ids.shape
-    sm = pl.BlockSpec(memory_space=pltpu.SMEM)
-    vm = pl.BlockSpec(memory_space=pltpu.VMEM)
-    return pl.pallas_call(
-        functools.partial(route_kernel, rows_dev, per_pair),
-        out_shape=(
-            jax.ShapeDtypeStruct((LANES, LANES), jnp.int32),
-            jax.ShapeDtypeStruct((4 * reqs, LANES), jnp.int32),
-        ),
-        in_specs=[sm, sm, vm, vm],
-        out_specs=(vm, vm),
-        scratch_shapes=[pltpu.VMEM((reqs * slots, LANES), jnp.int32)],
-        compiler_params=pltpu.CompilerParams(vmem_limit_bytes=VMEM_LIMIT),
-        name="route",
-    )(ids, valid, ids, table)
-
-
-def peer_of(step, stores, scorers):
-    store = lax.rem(lax.axis_index("store") + step // scorers, stores)
-    scorer = lax.rem(lax.axis_index("scorer") + lax.rem(step, scorers), scorers)
-    return store, scorer
-
-
-def exchange_kernel(
-    stores,
-    scorers,
-    per_pair,
-    ask_ref,
-    store_ref,
-    sizes_ref,
-    rows_out,
-    sizes_out,
-    ask_in,
-    ask_smem,
-    left_scr,
-    right_scr,
-    size_scr,
-    left,
-    right,
-    size_stage,
-    rows_send,
-    sizes_send,
-    send_sems,
-    recv_sems,
-    local_sem,
-):
-    pairs = stores * scorers
-    me = lax.axis_index("store") * scorers + lax.axis_index("scorer")
-    barrier = pltpu.get_barrier_semaphore()
-
-    def greet(i, carry):
-        pl.semaphore_signal(barrier, inc=1, device_id=peer_of(i, stores, scorers), device_id_type=MESH)
-        return carry
-
-    lax.fori_loop(1, pairs, greet, 0)
+    pl.semaphore_wait(barrier, pairs - 1)
+
+    def ask_group(g, first):
+        def one(j, carry):
+            i = g * group + j
+            store, scorer = peer_of(i, pairs, scorers)
+            pltpu.make_async_remote_copy(
+                src_ref=ask_ref.at[store * scorers + scorer],
+                dst_ref=ask_in.at[i],
+                send_sem=send_sems.at[0],
+                recv_sem=ask_sems.at[g],
+                device_id=(store, scorer),
+                device_id_type=MESH,
+            ).start()
+            return carry
+
+        lax.fori_loop(first, group, one, 0)
+
+    ask_group(0, 1)
+    for g in range(1, AHEAD):
+        ask_group(g, 0)
+    ask_in[0] = ask_ref[me]
     left_scr[...] = store_ref[:, :LANES].astype(F32)
     right_scr[...] = store_ref[:, LANES:].astype(F32)
     offsets = sizes_ref[...].astype(F32)
     for t in range(sizes_ref.shape[0]):
         size_scr[t * LANES : (t + 1) * LANES, :] = column_of(offsets[t : t + 1, :])
-    pl.semaphore_wait(barrier, pairs - 1)
-
-    def ask(i, carry):
-        store, scorer = peer_of(i, stores, scorers)
+
+    def settle(ref, first, count, sem):
+        part = ref.at[pl.ds(first, count)]
+        pltpu.make_async_copy(part, part, sem).wait()
+
+    def down(g):
+        part = pl.ds(g * group, group)
+        return pltpu.make_async_copy(ask_in.at[part], ask_smem.at[part], down_sems.at[g])
+
+    settle(ask_in, 0, group - 1, ask_sems.at[0])
+    down(0).start()
+    plane = lax.broadcasted_iota(jnp.int32, (per_pair, LANES), 1)
+    place = lax.broadcasted_iota(jnp.int32, (per_pair, LANES), 0)
+    place = place + lax.rem(me, LANES // per_pair) * per_pair
+
+    def collect(i):
+        for j in range(per_pair):
+            row = ask_smem[i, 0, j] & (rows_dev - 1)
+            left[pl.ds(j, 1), :] = left_scr[pl.ds(row, 1), :]
+            right[pl.ds(j, 1), :] = right_scr[pl.ds(row, 1), :]
+            size_stage[pl.ds(j, 1), :] = size_scr[pl.ds(row, 1), :]
+        sizes = jnp.sum(jnp.where(plane == place, size_stage[...], 0.0), axis=0, keepdims=True)
+        return left[...].astype(BF), right[...].astype(BF), sizes
+
+    def answer(i, carry):
+        store, scorer = peer_of(i, pairs, scorers)
+        rows_send[i, :, :LANES], rows_send[i, :, LANES:], sizes_send[i] = collect(i)
         pltpu.make_async_remote_copy(
-            src_ref=ask_ref.at[store * scorers + scorer],
-            dst_ref=ask_in.at[me],
-            send_sem=send_sems.at[0],
+            src_ref=rows_send.at[i],
+            dst_ref=rows_out.at[me],
+            send_sem=send_sems.at[1],
             recv_sem=recv_sems.at[0],
             device_id=(store, scorer),
             device_id_type=MESH,
         ).start()
-        return carry
-
-    lax.fori_loop(1, pairs, ask, 0)
-    ask_in[me] = ask_ref[me]
-
-    def settle(ref, sem):
-        part = ref.at[pl.ds(0, pairs - 1)]
-        pltpu.make_async_copy(part, part, sem).wait()
-
-    settle(ask_in, recv_sems.at[0])
-    down = pltpu.make_async_copy(ask_in, ask_smem, local_sem)
-    down.start()
-    down.wait()
-
-    lane = lax.broadcasted_iota(jnp.int32, (per_pair, LANES), 1)
-    sub = lax.broadcasted_iota(jnp.int32, (per_pair, LANES), 0)
-    sub = sub + lax.rem(me, LANES // per_pair) * per_pair
-
-    def collect(who):
-        for j in range(per_pair):
-            row = ask_smem[who, 0, j]
-            left[pl.ds(j, 1), :] = left_scr[pl.ds(row, 1), :]
-            right[pl.ds(j, 1), :] = right_scr[pl.ds(row, 1), :]
-            size_stage[pl.ds(j, 1), :] = size_scr[pl.ds(row, 1), :]
-        sizes = jnp.sum(jnp.where(lane == sub, size_stage[...], 0.0), axis=0, keepdims=True)
-        return left[...].astype(BF), right[...].astype(BF), sizes
-
-    def answer(i, carry):
-        store, scorer = peer_of(i, stores, scorers)
-        who = store * scorers + scorer
-        rows_send[who, :, :LANES], rows_send[who, :, LANES:], sizes_send[who] = collect(who)
         pltpu.make_async_remote_copy(
-            src_ref=rows_send.at[who],
-            dst_ref=rows_out.at[me],
-            send_sem=send_sems.at[1],
+            src_ref=sizes_send.at[i],
+            dst_ref=sizes_out.at[me],
+            send_sem=send_sems.at[2],
             recv_sem=recv_sems.at[1],
             device_id=(store, scorer),
             device_id_type=MESH,
         ).start()
-        pltpu.make_async_remote_copy(
-            src_ref=sizes_send.at[who],
-            dst_ref=sizes_out.at[me],
-            send_sem=send_sems.at[2],
-            recv_sem=recv_sems.at[2],
-            device_id=(store, scorer),
-            device_id_type=MESH,
-        ).start()
         return carry
 
-    lax.fori_loop(1, pairs, answer, 0)
-    rows_out[me, :, :LANES], rows_out[me, :, LANES:], sizes_out[me] = collect(me)
-    settle(ask_in, send_sems.at[0])
-    settle(rows_send, send_sems.at[1])
-    settle(sizes_send, send_sems.at[2])
-    settle(rows_out, recv_sems.at[1])
-    settle(sizes_out, recv_sems.at[2])
-
-
-def exchange(ask, store_rows, logsize, stores, scorers, per_pair):
+    def serve(g, carry):
+        @pl.when(g + AHEAD < groups)
+        def _():
+            ask_group(g + AHEAD, 0)
+
+        down(g).wait()
+
+        @pl.when(g + 1 < groups)
+        def _():
+            settle(ask_in, 0, group, ask_sems.at[g + 1])
+            down(g + 1).start()
+
+        lax.fori_loop(jnp.where(g == 0, 1, g * group), (g + 1) * group, answer, 0)
+        return carry
+
+    lax.fori_loop(0, groups, serve, 0)
+    rows_out[me, :, :LANES], rows_out[me, :, LANES:], sizes_out[me] = collect(0)
+    settle(ask_in, 0, pairs - 1, send_sems.at[0])
+    settle(rows_send, 0, pairs - 1, send_sems.at[1])
+    settle(sizes_send, 0, pairs - 1, send_sems.at[2])
+    settle(rows_out, 0, pairs - 1, recv_sems.at[0])
+    settle(sizes_out, 0, pairs - 1, recv_sems.at[1])
+
+
+def fetch(ids, valid, table, store_rows, logsize, stores, scorers, per_pair):
     pairs = stores * scorers
-    width = store_rows.shape[1]
+    groups = 8
+    reqs, slots = ids.shape
+    rows_dev, width = store_rows.shape
     vm = pl.BlockSpec(memory_space=pltpu.VMEM)
+    hbm = pl.BlockSpec(memory_space=pltpu.HBM)
+    column = pltpu.VMEM((rows_dev, LANES), F32)
+    part = pltpu.VMEM((per_pair, LANES), F32)
     return pl.pallas_call(
-        functools.partial(exchange_kernel, stores, scorers, per_pair),
+        functools.partial(fetch_kernel, stores, scorers, per_pair),
         out_shape=(
             jax.ShapeDtypeStruct((pairs, per_pair, width), BF),
             jax.ShapeDtypeStruct((pairs, 1, LANES), F32),
+            jax.ShapeDtypeStruct((4 * reqs, LANES), jnp.int32),
         ),
-        in_specs=[vm, vm, vm],
-        out_specs=(vm, vm),
+        in_specs=[hbm] * 5,
+        out_specs=(vm, vm, vm),
         scratch_shapes=[
+            pltpu.SMEM(ids.shape, jnp.int32),
+            pltpu.SMEM(valid.shape, jnp.int32),
+            pltpu.VMEM(ids.shape, jnp.int32),
+            pltpu.VMEM(table.shape, jnp.int32),
+            pltpu.VMEM(store_rows.shape, BF),
+            pltpu.VMEM(logsize.shape, BF),
+            pltpu.VMEM((reqs * slots, LANES), jnp.int32),
+            pltpu.VMEM((pairs, 1, LANES), jnp.int32),
             pltpu.VMEM((pairs, 1, LANES), jnp.int32),
             pltpu.SMEM((pairs, 1, LANES), jnp.int32),
-            pltpu.VMEM((store_rows.shape[0], LANES), F32),
-            pltpu.VMEM((store_rows.shape[0], LANES), F32),
-            pltpu.VMEM((store_rows.shape[0], LANES), F32),
-            pltpu.VMEM((per_pair, LANES), F32),
-            pltpu.VMEM((per_pair, LANES), F32),
-            pltpu.VMEM((per_pair, LANES), F32),
+            column,
+            column,
+            column,
+            part,
+            part,
+            part,
             pltpu.VMEM((pairs, per_pair, width), BF),
             pltpu.VMEM((pairs, 1, LANES), F32),
+            pltpu.SemaphoreType.DMA((6,)),
+            pltpu.SemaphoreType.DMA((groups,)),
+            pltpu.SemaphoreType.DMA((groups,)),
             pltpu.SemaphoreType.DMA((3,)),
-            pltpu.SemaphoreType.DMA((3,)),
-            pltpu.SemaphoreType.DMA,
+            pltpu.SemaphoreType.DMA((2,)),
         ],
         compiler_params=pltpu.CompilerParams(
             vmem_limit_bytes=VMEM_LIMIT, collective_id=0, has_side_effects=True
         ),
-        name="exchange",
-    )(ask, store_rows, logsize)
-
-
-def gather_kernel(scorers, table_ref, out_ref, landed, send_sem, recv_sem):
-    part = out_ref.shape[0]
+        cost_estimate=pl.CostEstimate(
+            flops=FETCH_FLOPS, bytes_accessed=8 * 1024 * 1024, transcendentals=0
+        ),
+        name="fetch",
+    )(ids, valid, table, store_rows, logsize)
+
+
+def gather_kernel(scorers, table_ref, landed, send_sem, recv_sem):
     store = lax.axis_index("store")
     me = lax.axis_index("scorer")
     barrier = pltpu.get_barrier_semaphore()
@@ -265,7 +324,7 @@
         to = lax.rem(me + i, scorers)
         pltpu.make_async_remote_copy(
             src_ref=table_ref.at[to],
-            dst_ref=landed.at[i - 1],
+            dst_ref=landed.at[i],
             send_sem=send_sem,
             recv_sem=recv_sem,
             device_id=(store, to),
@@ -274,9 +333,10 @@
         return carry
 
     lax.fori_loop(1, scorers, send, 0)
-    pltpu.make_async_copy(landed, landed, send_sem).wait()
-    pltpu.make_async_copy(landed, landed, recv_sem).wait()
-    out_ref[...] = table_ref[me] + jnp.sum(landed[...], axis=0)
+    landed[0] = table_ref[me]
+    others = landed.at[pl.ds(1, scorers - 1)]
+    pltpu.make_async_copy(others, others, send_sem).wait()
+    pltpu.make_async_copy(others, others, recv_sem).wait()
 
 
 def gather_spans(table, scorers):
@@ -284,15 +344,13 @@
     vm = pl.BlockSpec(memory_space=pltpu.VMEM)
     return pl.pallas_call(
         functools.partial(gather_kernel, scorers),
-        out_shape=jax.ShapeDtypeStruct((lines, LANES), F32),
+        out_shape=jax.ShapeDtypeStruct((scorers, lines, LANES), F32),
         in_specs=[vm],
         out_specs=vm,
-        scratch_shapes=[
-            pltpu.VMEM((scorers - 1, lines, LANES), F32),
-            pltpu.SemaphoreType.DMA,
-            pltpu.SemaphoreType.DMA,
-        ],
-        compiler_params=pltpu.CompilerParams(collective_id=1, has_side_effects=True),
+        scratch_shapes=[pltpu.SemaphoreType.DMA, pltpu.SemaphoreType.DMA],
+        compiler_params=pltpu.CompilerParams(
+            vmem_limit_bytes=4 * 1024 * 1024, collective_id=1, has_side_effects=True
+        ),
         name="gather_spans",
     )(table.reshape(scorers, lines, LANES))
 
@@ -300,22 +358,27 @@
 def score_kernel(
     per_pair,
     plan_smem,
-    valid_smem,
-    count_smem,
     sizes_ref,
     arrived_ref,
     cand_ref,
-    row_ref,
-    wq_ref,
-    wk_ref,
-    wv_ref,
-    wo_ref,
-    m1_ref,
-    b1_ref,
-    m2_ref,
-    b2_ref,
-    sp_ref,
+    *rest,
+):
+    held_in_hbm, out_ref, rest = rest[:12], rest[12], rest[13:]
+    local_copies, rest = rest[:12], rest[12:]
+    score_body(
+        per_pair, plan_smem, sizes_ref, arrived_ref, cand_ref, out_ref, held_in_hbm, local_copies, *rest
+    )
+
+
+def score_body(
+    per_pair,
+    plan_smem,
+    sizes_ref,
+    arrived_ref,
+    cand_ref,
     out_ref,
+    held_in_hbm,
+    local_copies,
     left_scr,
     right_scr,
     size_scr,
@@ -325,7 +388,22 @@
     k_scr,
     v_scr,
     ctx_scr,
+    load_sems,
 ):
+    (
+        valid_smem,
+        count_smem,
+        row_ref,
+        wq_ref,
+        wk_ref,
+        wv_ref,
+        wo_ref,
+        m1_ref,
+        b1_ref,
+        m2_ref,
+        b2_ref,
+        sp_ref,
+    ) = local_copies
     r = pl.program_id(0)
     reqs = pl.num_programs(0)
     total_slots, width = arrived_ref.shape
@@ -337,6 +415,12 @@
 
     @pl.when(r == 0)
     def _():
+        loads = [
+            pltpu.make_async_copy(src, dst, load_sems.at[n])
+            for n, (src, dst) in enumerate(zip(held_in_hbm, local_copies))
+        ]
+        for load in loads:
+            load.start()
         left_scr[:total_slots, :] = arrived_ref[:, :LANES].astype(F32)
         right_scr[:total_slots, :] = arrived_ref[:, LANES:].astype(F32)
         group = LANES // per_pair
@@ -353,6 +437,8 @@
             held[total_slots:, :] = jnp.zeros((CHUNK, LANES), F32)
             taken[...] = jnp.zeros_like(taken)
         out_ref[...] = jnp.zeros_like(out_ref)
+        for load in loads:
+            load.wait()
 
     valid = valid_smem[r]
     count = count_smem[r]
@@ -458,6 +544,8 @@
     total_slots = arrived.shape[0]
     slots = total_slots // reqs
     sm = pl.BlockSpec(memory_space=pltpu.SMEM)
+    hbm = pl.BlockSpec(memory_space=pltpu.HBM)
+    loose = (valid, count, rows) + tuple(weights)
 
     def whole(a):
         return pl.BlockSpec(a.shape, lambda r, n=a.ndim: (0,) * n)
@@ -470,16 +558,18 @@
         out_shape=jax.ShapeDtypeStruct((lines, LANES), F32),
         in_specs=[
             sm,
-            sm,
-            sm,
             whole(sizes),
             whole(arrived),
             pl.BlockSpec((1, cands, width), lambda r: (r, 0, 0)),
-            whole(rows),
         ]
-        + [whole(w) for w in weights],
+        + [hbm] * len(loose),
         out_specs=pl.BlockSpec((lines, LANES), lambda r: (0, 0)),
         scratch_shapes=[
+            pltpu.SMEM(valid.shape, jnp.int32),
+            pltpu.SMEM(count.shape, jnp.int32),
+        ]
+        + [pltpu.VMEM(a.shape, a.dtype) for a in loose[2:]]
+        + [
             held,
             held,
             held,
@@ -489,10 +579,14 @@
             pltpu.VMEM((HEADS, slots, width), BF),
             pltpu.VMEM((HEADS, slots, width), BF),
             pltpu.VMEM((cands, width), BF),
+            pltpu.SemaphoreType.DMA((len(loose),)),
         ],
         compiler_params=pltpu.CompilerParams(vmem_limit_bytes=VMEM_LIMIT),
+        cost_estimate=pl.CostEstimate(
+            flops=SCORE_FLOPS, bytes_accessed=8 * 1024 * 1024, transcendentals=8 * 1024 * 1024
+        ),
         name="score",
-    )(plan, valid, count, sizes, arrived, candidates, rows, *weights)
+    )(plan, sizes, arrived, candidates, *loose)
 
 
 def on_device(
@@ -520,11 +614,10 @@
     slot_total = cluster_ids.size
     per_pair = slot_total // device_count
     reqs, cands = candidate_row.shape
-    ask, plan = route(
-        cluster_ids, valid_count, cluster_home.reshape(-1, LANES), rows_dev, per_pair
-    )
-    arrived, sizes = exchange(
-        ask.reshape(device_count, 1, LANES),
+    arrived, sizes, plan = fetch(
+        cluster_ids,
+        valid_count,
+        cluster_home.reshape(-1, LANES),
         store_rows,
         cluster_logsize.reshape(-1, LANES),
         device_count // scorer_count,
@@ -548,7 +641,7 @@
     table = score(
         plan, per_pair, valid_count, cand_count, sizes, arrived, candidates, candidate_row, weights, lines
     )
-    return gather_spans(table, scorer_count).reshape(-1)
+    return jnp.sum(gather_spans(table, scorer_count), axis=0).reshape(-1)
 
 
 def solution(mesh):

time: 122 us -> 100 us (0.82)
  Pallas kernels: 106 us -> 93.9 us
  local copies, waits for them, and re-layouts: 15.6 us -> 5.23 us
    pallas_call x2 -> x1, Pallas kernels: 63.4 us -> 52.8 us  [fetch(): pl.pallas_call(functools.partial(fetch_kernel, stores, scorers, per_pair)...]
    unnamed x35 -> x34, local copies, waits for them, and re-layouts: 14.8 us -> 4.57 us
    pallas_call x1, Pallas kernels: 9.36 us -> 8.06 us  [gather_spans(): pl.pallas_call(functools.partial(gather_kernel, scorers), out_shape=jax.S...]
where the time goes in v4:
time: 100 us; the launch traced here: 99.9 us
  Pallas kernels  93.9 us (94%)
  local copies, waits for them, and re-layouts  5.23 us (5%)
    pallas_call x1, Pallas kernels, fetch(): pl.pallas_call(functools.partial(fetch_kernel, stores, scorers, per_pair)...  52.8 us
    pallas_call x1, Pallas kernels, score(): pl.pallas_call(functools.partial(score_kernel, per_pair), grid=(reqs,), o...  33 us
    pallas_call x1, Pallas kernels, gather_spans(): pl.pallas_call(functools.partial(gather_kernel, scorers), out_shape=jax.S...  8.06 us
    unnamed x34, local copies, waits for them, and re-layouts  4.57 us

profile of v4, /device:TPU:0, one launch (start us, length us, event | category | flops | bytes accessed | tf_op | source)
XLA Modules:
  0.0 99.9 jit_solution(10922514023976885214)
XLA Ops:
  0.0 0.7 reshape.33.rest_11_
  0.7 1.2 %copy-done.1 = s32[262144]{0:T(1024)S(1)} copy-done((s32[262144]{0:T(1024)S(1)}, s32[262144]{0:T(1024)}, u32[]{:S(2)}) %copy-start.1) | copy-done | bytes 1048600
  1.9 1.2 %copy-done.2 = bf16[2048,256]{1,0:T(8,128)(2,1)S(1)} copy-done((bf16[2048,256]{1,0:T(8,128)(2,1)S(1)}, bf16[2048,256]{1,0:T(8,128)(2,1)}, u32[]{:S(2)}) %copy-start.2) | copy-done | bytes 1048600
  3.1 0.7 copy-done.9
  3.8 0.7 copy-done.11
  4.5 0.7 copy-done.14
  5.2 0.0 copy-start.6
  5.2 0.0 copy-start.7
  5.2 0.0 copy-start.8
  5.2 0.0 copy-start.10
  5.2 0.0 copy-start.12
  5.2 0.0 copy-start.13
  5.3 0.0 copy-start.16
  5.3 52.8 %fetch.1 = (bf16[128,32,256]{2,1,0:T(8,128)(2,1)S(1)}, f32[128,1,128]{2,1,0:T(1,128)S(1)}, s32[32,128]{1,0:T(8,128)S(1)}) custom-call(s32[8,512]{1,0:T(8,128)S(1)} %copy-done.9, s32[8]{0:T(128)S(1)} %copy-done.14, s32[2048,128]{1,0:T(8,128)S(1)} %bitcast.9, bf16[2048,256]{1,0:T(8,128)(2,1)S(1)} %copy-done.2, bf16[16,128]{1,0:T(8,128)(2,1)S(1)} %bitcast.10), custom_call_target="tpu_custom_call" | custom-call | flops 40000000000 | bytes 8388608 | tf_op jit(solution)/shard_map/fetch/pallas_call | solution.py:265
  58.1 0.0 copy-done
  58.1 0.0 copy-done.3
  58.1 0.0 copy-done.4
  58.1 0.0 copy-done.5
  58.1 0.0 copy-done.6
  58.1 0.0 copy-done.7
  58.2 0.0 copy-done.8
  58.2 33.0 %score.1 = f32[256,128]{1,0:T(8,128)S(1)} custom-call(s32[32,128]{1,0:T(8,128)S(1)} %get-tuple-element.8.plan_smem, f32[128,128]{1,0:T(8,128)S(1)} %bitcast.14, bf16[4096,256]{1,0:T(8,128)(2,1)S(1)} %bitcast.13, bf16[8,512,256]{2,1,0:T(8,128)(2,1)S(1)} %copy-done, s32[8]{0:T(128)S(1)} %copy-done.15, s32[8]{0:T(128)S(1)} %copy-done.16, ...), custom_call_target="tpu_custom_call" | custom-call | flops 30000001024 | bytes 8388608 | tf_op jit(solution)/shard_map/score/pallas_call | solution.py:555
  91.3 8.1 %gather_spans.1 = f32[16,16,128]{2,1,0:T(8,128)S(1)} custom-call(f32[16,16,128]{2,1,0:T(8,128)S(1)} %bitcast.8), custom_call_target="tpu_custom_call" | custom-call | tf_op jit(solution)/shard_map/gather_spans/pallas_call | solution.py:345
  99.3 0.6 reduce_sum.9
  (15 shorter events, 0.0 us)
Async XLA Ops:
  0.7 1.2 %copy-start.1 = (s32[262144]{0:T(1024)S(1)}, s32[262144]{0:T(1024)}, u32[]{:S(2)}) copy-start(s32[262144]{0:T(1024)} %param.19) | copy-start | bytes 3145732
  1.9 1.2 %copy-start.2 = (bf16[2048,256]{1,0:T(8,128)(2,1)S(1)}, bf16[2048,256]{1,0:T(8,128)(2,1)}, u32[]{:S(2)}) copy-start(bf16[2048,256]{1,0:T(8,128)(2,1)} %store_hbm.1) | copy-start | bytes 3145732
  3.1 0.7 copy-start.9
  3.8 0.7 copy-start.11
  4.5 0.7 copy-start.14
  5.2 52.9 %copy-start = (bf16[8,512,256]{2,1,0:T(8,128)(2,1)S(1)}, bf16[8,512,256]{2,1,0:T(8,128)(2,1)}, u32[]{:S(2)}) copy-start(bf16[8,512,256]{2,1,0:T(8,128)(2,1)} %cand_ref.1) | copy-start | bytes 6291460
  5.2 52.9 %copy-start.3 = (bf16[512,512]{1,0:T(8,128)(2,1)S(1)}, bf16[512,512]{1,0:T(8,128)(2,1)}, u32[]{:S(2)}) copy-start(bf16[512,512]{1,0:T(8,128)(2,1)} %rest_7_.1) | copy-start | bytes 1572868
  5.2 52.9 %copy-start.4 = (bf16[512,256]{1,0:T(8,128)(2,1)S(1)}, bf16[512,256]{1,0:T(8,128)(2,1)}, u32[]{:S(2)}) copy-start(bf16[512,256]{1,0:T(8,128)(2,1)} %rest_9_.1) | copy-start | bytes 786436
  5.2 53.0 %copy-start.5 = (bf16[256,256]{1,0:T(8,128)(2,1)S(1)}, bf16[256,256]{1,0:T(8,128)(2,1)}, u32[]{:S(2)}) copy-start(bf16[256,256]{1,0:T(8,128)(2,1)} %rest_3_.1) | copy-start | bytes 393220
  5.2 53.0 %copy-start.6 = (bf16[256,256]{1,0:T(8,128)(2,1)S(1)}, bf16[256,256]{1,0:T(8,128)(2,1)}, u32[]{:S(2)}) copy-start(bf16[256,256]{1,0:T(8,128)(2,1)} %rest_4_.1) | copy-start | bytes 393220
  5.2 53.0 %copy-start.7 = (bf16[256,256]{1,0:T(8,128)(2,1)S(1)}, bf16[256,256]{1,0:T(8,128)(2,1)}, u32[]{:S(2)}) copy-start(bf16[256,256]{1,0:T(8,128)(2,1)} %rest_5_.1) | copy-start | bytes 393220
  5.2 53.0 %copy-start.8 = (bf16[256,256]{1,0:T(8,128)(2,1)S(1)}, bf16[256,256]{1,0:T(8,128)(2,1)}, u32[]{:S(2)}) copy-start(bf16[256,256]{1,0:T(8,128)(2,1)} %rest_6_.1) | copy-start | bytes 393220
  5.2 53.0 %copy-start.10 = (s32[8,512]{1,0:T(8,128)S(1)}, s32[8,512]{1,0:T(8,128)}, u32[]{:S(2)}) copy-start(s32[8,512]{1,0:T(8,128)} %rest_2_.1) | copy-start | bytes 49156
  5.2 53.0 %copy-start.12 = (f32[512]{0:T(512)S(1)}, f32[512]{0:T(512)}, u32[]{:S(2)}) copy-start(f32[512]{0:T(512)} %param.30) | copy-start | bytes 6148
  5.2 52.9 %copy-start.13 = (f32[256]{0:T(256)S(1)}, f32[256]{0:T(256)}, u32[]{:S(2)}) copy-start(f32[256]{0:T(256)} %param.32) | copy-start | bytes 3076
  5.3 52.9 %copy-start.15 = (s32[8]{0:T(128)S(1)}, s32[8]{0:T(128)}, u32[]{:S(2)}) copy-start(s32[8]{0:T(128)} %rest_0_.1) | copy-start | bytes 100
  5.3 52.9 %copy-start.16 = (s32[8]{0:T(128)S(1)}, s32[8]{0:T(128)}, u32[]{:S(2)}) copy-start(s32[8]{0:T(128)} %rest_1_.1) | copy-start | bytes 100

commit v5 on v4

--- a/solution.py
+++ b/solution.py
@@ -19,7 +19,7 @@
 TN = (((0,), (0,)), ((), ()))
 BF = jnp.bfloat16
 F32 = jnp.float32
-VMEM_LIMIT = 48 * 1024 * 1024
+VMEM_LIMIT = 60 * 1024 * 1024
 MESH = pl.DeviceIdType.MESH
 
 
@@ -36,6 +36,79 @@
     store = jnp.bitwise_xor(lax.axis_index("store"), turn // scorers)
     scorer = jnp.bitwise_xor(lax.axis_index("scorer"), lax.rem(turn, scorers))
     return store, scorer
+
+
+def plan_asks(
+    per_pair, rows_dev, ids_smem, valid_smem, ids_ref, table_ref, ask_ref, plan_ref, even, odd, starts
+):
+    reqs, slots = ids_ref.shape
+    shift_rows = rows_dev.bit_length() - 1
+    lane = lax.broadcasted_iota(jnp.int32, (LANES, LANES), 1)
+    sub = lax.broadcasted_iota(jnp.int32, (LANES, LANES), 0)
+    lower = jnp.where(sub >= lane, 1.0, 0.0).astype(BF)
+    before = jnp.where(sub < lane, 1.0, 0.0).astype(BF)
+    ones = jnp.ones((LANES, LANES), BF)
+    wide = lax.broadcasted_iota(jnp.int32, (slots, LANES), 1)
+
+    def look(r, into):
+        for u in range(slots):
+            c = ids_smem[r, u]
+            into[u : u + 1, :] = table_ref[pl.ds(lax.shift_right_logical(c, 7), 1), :]
+
+    def rank(r, held, base, acc):
+        starts[pl.ds(r, 1), :] = base
+        ids = ids_ref[pl.ds(r, 1), :]
+        valid = valid_smem[r]
+        homes, hots = [], []
+        for t in range(0, slots, LANES):
+            home = lane_pick(held[t : t + LANES, :], column_of(ids[:, t : t + LANES]) & (LANES - 1))
+            hot = lax.shift_right_logical(home, shift_rows) == lane
+            homes.append(home)
+            hots.append(jnp.where(sub + t < valid, jnp.where(hot, 1.0, 0.0), 0.0))
+        picked = []
+        for t in range(0, len(hots), 2):
+            two = jnp.concatenate(hots[t : t + 2], axis=1).astype(BF)
+            incl = jnp.dot(lower, two, preferred_element_type=F32)
+            for n in range(2):
+                part = incl[:, n * LANES : (n + 1) * LANES]
+                picked.append(hots[t + n] * (part + (base - 1.0)))
+                base = base + part[LANES - 1 : LANES, :]
+        picked = jnp.concatenate(picked, axis=0).astype(BF)
+        place = jnp.dot(picked, ones, preferred_element_type=F32).astype(jnp.int32)
+        home = jnp.concatenate(homes, axis=0)
+        low = (home & 255).astype(F32)
+        high = (lax.shift_right_logical(home, 8) & ((rows_dev >> 8) - 1)).astype(F32)
+        at = place == wide
+        parts = jnp.concatenate(
+            [jnp.where(at, low, 0.0), jnp.where(at, high, 0.0)], axis=1
+        ).astype(BF)
+        hot = jnp.concatenate(hots, axis=0).astype(BF)
+        acc = acc + lax.dot_general(hot, parts, TN, preferred_element_type=F32)
+        return base, acc
+
+    look(0, even)
+
+    def both(n, carry):
+        base, acc = rank(2 * n, even, *carry)
+        look(2 * n + 1, odd)
+        base, acc = rank(2 * n + 1, odd, base, acc)
+        look(lax.rem(2 * n + 2, reqs), even)
+        return base, acc
+
+    base, acc = lax.fori_loop(
+        0, reqs // 2, both, (jnp.zeros((1, LANES), F32), jnp.zeros((LANES, 2 * LANES), F32))
+    )
+    ask = (acc[:, :LANES] + 256.0 * acc[:, LANES:]).astype(jnp.int32)
+    ask_ref[...] = ask.reshape(ask_ref.shape)
+    first = starts[...]
+    counts = jnp.concatenate([first[1:], base], axis=0) - first
+    spots = jnp.dot(counts.astype(BF), before, preferred_element_type=F32)
+    source = lax.broadcasted_iota(jnp.int32, (reqs, LANES), 1) * per_pair
+    plan_ref[0:reqs, :] = source + first.astype(jnp.int32)
+    plan_ref[reqs : 2 * reqs, :] = spots.astype(jnp.int32)
+    plan_ref[2 * reqs : 3 * reqs, :] = counts.astype(jnp.int32)
+    most = jnp.max(counts, axis=1, keepdims=True)
+    plan_ref[3 * reqs :, :] = jnp.broadcast_to(most, (reqs, LANES)).astype(jnp.int32)
 
 
 def fetch_kernel(
@@ -49,6 +122,7 @@
     sizes_hbm,
     rows_out,
     sizes_out,
+    plan_hbm,
     plan_ref,
     ids_smem,
     valid_smem,
@@ -56,7 +130,9 @@
     table_ref,
     store_ref,
     sizes_ref,
-    homes,
+    even,
+    odd,
+    starts,
     ask_ref,
     ask_in,
     ask_smem,
@@ -77,10 +153,7 @@
     pairs = stores * scorers
     groups = ask_sems.shape[0]
     group = pairs // groups
-    reqs, slots = ids_ref.shape
-    per_req = slots // LANES
     rows_dev = store_ref.shape[0]
-    shift_rows = rows_dev.bit_length() - 1
     me = lax.axis_index("store") * scorers + lax.axis_index("scorer")
     barrier = pltpu.get_barrier_semaphore()
 
@@ -108,55 +181,11 @@
     for load in loads:
         load.wait()
 
-    def look(r, carry):
-        start = pl.multiple_of(r * slots, slots)
-        for u in range(slots):
-            c = ids_smem[r, u]
-            homes[pl.ds(start + u, 1), :] = table_ref[pl.ds(lax.shift_right_logical(c, 7), 1), :]
-        return carry
-
-    lax.fori_loop(0, reqs, look, 0)
-    lane = lax.broadcasted_iota(jnp.int32, (LANES, LANES), 1)
-    sub = lax.broadcasted_iota(jnp.int32, (LANES, LANES), 0)
-    lower = jnp.where(sub >= lane, 1.0, 0.0).astype(BF)
-    before = jnp.where(sub < lane, 1.0, 0.0).astype(BF)
-    ones = jnp.ones((LANES, LANES), BF)
-    base = jnp.zeros((1, LANES), F32)
-    acc = jnp.zeros((LANES, 2 * LANES), F32)
-    bases = []
-    for t in range(reqs * per_req):
-        r, q = t // per_req, t % per_req
-        if q == 0:
-            bases.append(base)
-        ids_col = column_of(ids_ref[r : r + 1, q * LANES : (q + 1) * LANES])
-        home = lane_pick(homes[t * LANES : (t + 1) * LANES, :], ids_col & (LANES - 1))
-        hot = lax.shift_right_logical(home, shift_rows) == lane
-        hot = jnp.where(sub + q * LANES < valid_smem[r], jnp.where(hot, 1.0, 0.0), 0.0)
-        hot_b = hot.astype(BF)
-        incl = jnp.dot(lower, hot_b, preferred_element_type=F32)
-        picked = (hot * (incl + (base - 1.0))).astype(BF)
-        rank = jnp.dot(picked, ones, preferred_element_type=F32).astype(jnp.int32)
-        base = base + incl[LANES - 1 : LANES, :]
-        low = (home & 255).astype(F32)
-        high = (lax.shift_right_logical(home, 8) & ((rows_dev >> 8) - 1)).astype(F32)
-        at = rank == lane
-        parts = jnp.concatenate(
-            [jnp.where(at, low, 0.0), jnp.where(at, high, 0.0)], axis=1
-        ).astype(BF)
-        acc = acc + lax.dot_general(hot_b, parts, TN, preferred_element_type=F32)
-    bases.append(base)
-    ask = (acc[:, :LANES] + 256.0 * acc[:, LANES:]).astype(jnp.int32)
-    ask_ref[...] = ask.reshape(pairs, 1, LANES)
-    starts = jnp.concatenate(bases[:reqs], axis=0)
-    counts = jnp.concatenate(bases[1:], axis=0) - starts
-    spots = jnp.dot(counts.astype(BF), before, preferred_element_type=F32)
-    source = lax.broadcasted_iota(jnp.int32, (reqs, LANES), 1) * per_pair
-    plan_ref[0:reqs, :] = source + starts.astype(jnp.int32)
-    plan_ref[reqs : 2 * reqs, :] = spots.astype(jnp.int32)
-    plan_ref[2 * reqs : 3 * reqs, :] = counts.astype(jnp.int32)
-    most = jnp.max(counts, axis=1, keepdims=True)
-    plan_ref[3 * reqs :, :] = jnp.broadcast_to(most, (reqs, LANES)).astype(jnp.int32)
-
+    plan_asks(
+        per_pair, rows_dev, ids_smem, valid_smem, ids_ref, table_ref, ask_ref, plan_ref, even, odd, starts
+    )
+    plan_out = pltpu.make_async_copy(plan_ref, plan_hbm, load_sems.at[0])
+    plan_out.start()
     pl.semaphore_wait(barrier, pairs - 1)
 
     def ask_group(g, first):
@@ -245,7 +274,14 @@
         return carry
 
     lax.fori_loop(0, groups, serve, 0)
-    rows_out[me, :, :LANES], rows_out[me, :, LANES:], sizes_out[me] = collect(0)
+    rows_send[0, :, :LANES], rows_send[0, :, LANES:], sizes_send[0] = collect(0)
+    own_rows = pltpu.make_async_copy(rows_send.at[0], rows_out.at[me], load_sems.at[1])
+    own_sizes = pltpu.make_async_copy(sizes_send.at[0], sizes_out.at[me], load_sems.at[2])
+    own_rows.start()
+    own_sizes.start()
+    own_rows.wait()
+    own_sizes.wait()
+    plan_out.wait()
     settle(ask_in, 0, pairs - 1, send_sems.at[0])
     settle(rows_send, 0, pairs - 1, send_sems.at[1])
     settle(sizes_send, 0, pairs - 1, send_sems.at[2])
@@ -258,7 +294,6 @@
     groups = 8
     reqs, slots = ids.shape
     rows_dev, width = store_rows.shape
-    vm = pl.BlockSpec(memory_space=pltpu.VMEM)
     hbm = pl.BlockSpec(memory_space=pltpu.HBM)
     column = pltpu.VMEM((rows_dev, LANES), F32)
     part = pltpu.VMEM((per_pair, LANES), F32)
@@ -270,15 +305,18 @@
             jax.ShapeDtypeStruct((4 * reqs, LANES), jnp.int32),
         ),
         in_specs=[hbm] * 5,
-        out_specs=(vm, vm, vm),
+        out_specs=(hbm, hbm, hbm),
         scratch_shapes=[
+            pltpu.VMEM((4 * reqs, LANES), jnp.int32),
             pltpu.SMEM(ids.shape, jnp.int32),
             pltpu.SMEM(valid.shape, jnp.int32),
             pltpu.VMEM(ids.shape, jnp.int32),
             pltpu.VMEM(table.shape, jnp.int32),
             pltpu.VMEM(store_rows.shape, BF),
             pltpu.VMEM(logsize.shape, BF),
-            pltpu.VMEM((reqs * slots, LANES), jnp.int32),
+            pltpu.VMEM((slots, LANES), jnp.int32),
+            pltpu.VMEM((slots, LANES), jnp.int32),
+            pltpu.VMEM((reqs, LANES), F32),
             pltpu.VMEM((pairs, 1, LANES), jnp.int32),
             pltpu.VMEM((pairs, 1, LANES), jnp.int32),
             pltpu.SMEM((pairs, 1, LANES), jnp.int32),
@@ -306,7 +344,7 @@
     )(ids, valid, table, store_rows, logsize)
 
 
-def gather_kernel(scorers, table_ref, landed, send_sem, recv_sem):
+def gather_kernel(scorers, table_ref, landed, send_sem, recv_sem, own_sem):
     store = lax.axis_index("store")
     me = lax.axis_index("scorer")
     barrier = pltpu.get_barrier_semaphore()
@@ -333,7 +371,9 @@
         return carry
 
     lax.fori_loop(1, scorers, send, 0)
-    landed[0] = table_ref[me]
+    own = pltpu.make_async_copy(table_ref.at[me], landed.at[0], own_sem)
+    own.start()
+    own.wait()
     others = landed.at[pl.ds(1, scorers - 1)]
     pltpu.make_async_copy(others, others, send_sem).wait()
     pltpu.make_async_copy(others, others, recv_sem).wait()
@@ -345,11 +385,11 @@
     return pl.pallas_call(
         functools.partial(gather_kernel, scorers),
         out_shape=jax.ShapeDtypeStruct((scorers, lines, LANES), F32),
-        in_specs=[vm],
+        in_specs=[pl.BlockSpec(memory_space=pltpu.HBM)],
         out_specs=vm,
-        scratch_shapes=[pltpu.SemaphoreType.DMA, pltpu.SemaphoreType.DMA],
+        scratch_shapes=[pltpu.SemaphoreType.DMA] * 3,
         compiler_params=pltpu.CompilerParams(
-            vmem_limit_bytes=4 * 1024 * 1024, collective_id=1, has_side_effects=True
+            vmem_limit_bytes=VMEM_LIMIT, collective_id=1, has_side_effects=True
         ),
         name="gather_spans",
     )(table.reshape(scorers, lines, LANES))
@@ -357,28 +397,23 @@
 
 def score_kernel(
     per_pair,
-    plan_smem,
-    sizes_ref,
-    arrived_ref,
     cand_ref,
+    arrived_hbm,
     *rest,
 ):
-    held_in_hbm, out_ref, rest = rest[:12], rest[12], rest[13:]
-    local_copies, rest = rest[:12], rest[12:]
-    score_body(
-        per_pair, plan_smem, sizes_ref, arrived_ref, cand_ref, out_ref, held_in_hbm, local_copies, *rest
-    )
+    held_in_hbm, out_ref, rest = rest[:14], rest[14], rest[15:]
+    local_copies, rest = rest[:14], rest[14:]
+    score_body(per_pair, cand_ref, arrived_hbm, out_ref, held_in_hbm, local_copies, *rest)
 
 
 def score_body(
     per_pair,
-    plan_smem,
-    sizes_ref,
-    arrived_ref,
     cand_ref,
+    arrived_hbm,
     out_ref,
     held_in_hbm,
     local_copies,
+    arrived_ref,
     left_scr,
     right_scr,
     size_scr,
@@ -388,9 +423,12 @@
     k_scr,
     v_scr,
     ctx_scr,
+    wkt_scr,
     load_sems,
 ):
     (
+        plan_smem,
+        sizes_ref,
         valid_smem,
         count_smem,
         row_ref,
@@ -421,8 +459,28 @@
         ]
         for load in loads:
             load.start()
-        left_scr[:total_slots, :] = arrived_ref[:, :LANES].astype(F32)
-        right_scr[:total_slots, :] = arrived_ref[:, LANES:].astype(F32)
+        quarter = total_slots // 4
+        blocks = [
+            pltpu.make_async_copy(
+                arrived_hbm.at[pl.ds(n * quarter, quarter)],
+                arrived_ref.at[pl.ds(n * quarter, quarter)],
+                load_sems.at[len(loads) + n],
+            )
+            for n in range(4)
+        ]
+        for block in blocks:
+            block.start()
+        k_scr[...] = jnp.zeros_like(k_scr)
+        ones_lane = lax.broadcasted_iota(jnp.int32, (slots, LANES), 1) // head_size
+        for h in range(HEADS):
+            v_scr[h, :, LANES:] = jnp.where(ones_lane == h % 2, 1.0, 0.0).astype(BF)
+        for held, taken in copies:
+            held[total_slots:, :] = jnp.zeros((CHUNK, LANES), F32)
+            taken[...] = jnp.zeros_like(taken)
+        out_ref[...] = jnp.zeros_like(out_ref)
+        for load in loads:
+            load.wait()
+        wkt_scr[...] = wk_ref[...].astype(F32).T.astype(BF)
         group = LANES // per_pair
         one = lax.broadcasted_iota(jnp.int32, (pairs // group, pairs), 1) // group
         one = one == lax.broadcasted_iota(jnp.int32, (pairs // group, pairs), 0)
@@ -433,12 +491,11 @@
         )
         for t in range(pairs // group):
             size_scr[t * LANES : (t + 1) * LANES, :] = column_of(packed[t : t + 1, :])
-        for held, taken in copies:
-            held[total_slots:, :] = jnp.zeros((CHUNK, LANES), F32)
-            taken[...] = jnp.zeros_like(taken)
-        out_ref[...] = jnp.zeros_like(out_ref)
-        for load in loads:
-            load.wait()
+        for n, block in enumerate(blocks):
+            block.wait()
+            part = slice(n * quarter, (n + 1) * quarter)
+            left_scr[part, :] = arrived_ref[part, :LANES].astype(F32)
+            right_scr[part, :] = arrived_ref[part, LANES:].astype(F32)
 
     valid = valid_smem[r]
     count = count_smem[r]
@@ -480,26 +537,29 @@
 
     def attend(live):
         x = jnp.concatenate([x_left[:live, :], x_right[:live, :]], axis=1).astype(BF)
-        keys = jnp.dot(x, wk_ref[...], preferred_element_type=F32).astype(BF).astype(F32) * 0.125
-        values = jnp.dot(x, wv_ref[...], preferred_element_type=F32).astype(BF).astype(F32)
+        keys = lax.dot_general(wkt_scr[...], x, NT, preferred_element_type=F32)
+        keys = (keys.astype(BF).astype(F32) * 0.125).astype(BF)
+        values = jnp.dot(x, wv_ref[...], preferred_element_type=F32)
+        bias = jnp.concatenate(
+            [x_size[t : t + LANES, :].T[0:16, :] for t in range(0, live, LANES)], axis=1
+        )
+        slot = lax.broadcasted_iota(jnp.int32, (16, live), 1)
+        sub = lax.broadcasted_iota(jnp.int32, (16, live), 0)
+        bias = jnp.where(slot < valid, bias, -1e30)
+        bias = jnp.where(sub == 0, bias, 0.0).astype(BF)
         lane = lax.broadcasted_iota(jnp.int32, (live, LANES), 1)
-        slot = lax.broadcasted_iota(jnp.int32, (live, LANES), 0)
-        bias = jnp.where(slot < valid, x_size[:live, :], -1e30)
-        bias = jnp.where(lane == 0, bias, 0.0).astype(BF)
         for h in range(HEADS):
             half = slice((h // 2) * LANES, (h // 2 + 1) * LANES)
-            other = slice((1 - h // 2) * LANES, (2 - h // 2) * LANES)
+            own = slice(h * head_size, (h + 1) * head_size)
+            other = (1 - h // 2) * LANES
             mine = (lane // head_size) == (h % 2)
-            k_scr[h, :live, half] = jnp.where(mine, keys[:, half], 0.0).astype(BF)
-            k_scr[h, :live, other] = bias
+            k_scr[h, own, :live] = keys[own, :]
+            k_scr[h, other : other + 16, :live] = bias
             v_scr[h, :live, :LANES] = jnp.where(mine, values[:, half], 0.0).astype(BF)
-            v_scr[h, :live, LANES:] = jnp.where(mine, 1.0, 0.0).astype(BF)
         for p in range(2):
             total = None
             for h in (2 * p, 2 * p + 1):
-                logits = lax.dot_general(
-                    queries[p], k_scr[h, :live, :], NT, preferred_element_type=F32
-                )
+                logits = jnp.dot(queries[p], k_scr[h, :, :live], preferred_element_type=F32)
                 top = jnp.max(logits, axis=1, keepdims=True)
                 probs = jnp.exp(logits - top).astype(BF)
                 part = jnp.dot(probs, v_scr[h, :live, :], preferred_element_type=F32)
@@ -521,7 +581,9 @@
     hidden = jnp.maximum(hidden + b1_ref[...], 0.0).astype(BF)
     hidden = jnp.dot(hidden, m2_ref[...], preferred_element_type=F32)
     hidden = jnp.maximum(hidden + b2_ref[...], 0.0).astype(BF)
-    weight = jnp.broadcast_to(sp_ref[...].astype(F32), (16, width)).astype(BF)
+    weight = sp_ref[...].astype(F32)
+    weight = jnp.concatenate([weight[n : n + 1, :] for n in range(width // LANES)], axis=1)
+    weight = jnp.broadcast_to(weight, (16, width)).astype(BF)
     score = lax.dot_general(weight, hidden, NT, preferred_element_type=F32)[0:1, :]
     slot = lax.broadcasted_iota(jnp.int32, (1, cands), 1)
     score = jnp.where(slot < count, score, 0.0)
@@ -543,50 +605,43 @@
     reqs, cands, width = candidates.shape
     total_slots = arrived.shape[0]
     slots = total_slots // reqs
-    sm = pl.BlockSpec(memory_space=pltpu.SMEM)
     hbm = pl.BlockSpec(memory_space=pltpu.HBM)
-    loose = (valid, count, rows) + tuple(weights)
-
-    def whole(a):
-        return pl.BlockSpec(a.shape, lambda r, n=a.ndim: (0,) * n)
-
+    loose = (plan, sizes, valid, count, rows) + tuple(weights)
     held = pltpu.VMEM((total_slots + CHUNK, LANES), F32)
     taken = pltpu.VMEM((slots + 2 * CHUNK, LANES), F32)
     return pl.pallas_call(
         functools.partial(score_kernel, per_pair),
         grid=(reqs,),
         out_shape=jax.ShapeDtypeStruct((lines, LANES), F32),
-        in_specs=[
-            sm,
-            whole(sizes),
-            whole(arrived),
-            pl.BlockSpec((1, cands, width), lambda r: (r, 0, 0)),
-        ]
-        + [hbm] * len(loose),
+        in_specs=[pl.BlockSpec((1, cands, width), lambda r: (r, 0, 0)), hbm] + [hbm] * len(loose),
         out_specs=pl.BlockSpec((lines, LANES), lambda r: (0, 0)),
         scratch_shapes=[
+            pltpu.SMEM(plan.shape, jnp.int32),
+            pltpu.VMEM(sizes.shape, F32),
             pltpu.SMEM(valid.shape, jnp.int32),
             pltpu.SMEM(count.shape, jnp.int32),
         ]
-        + [pltpu.VMEM(a.shape, a.dtype) for a in loose[2:]]
+        + [pltpu.VMEM(a.shape, a.dtype) for a in loose[4:]]
         + [
+            pltpu.VMEM(arrived.shape, BF),
             held,
             held,
             held,
             taken,
             taken,
             taken,
-            pltpu.VMEM((HEADS, slots, width), BF),
+            pltpu.VMEM((HEADS, width, slots), BF),
             pltpu.VMEM((HEADS, slots, width), BF),
             pltpu.VMEM((cands, width), BF),
-            pltpu.SemaphoreType.DMA((len(loose),)),
+            pltpu.VMEM((width, width), BF),
+            pltpu.SemaphoreType.DMA((len(loose) + 4,)),
         ],
         compiler_params=pltpu.CompilerParams(vmem_limit_bytes=VMEM_LIMIT),
         cost_estimate=pl.CostEstimate(
             flops=SCORE_FLOPS, bytes_accessed=8 * 1024 * 1024, transcendentals=8 * 1024 * 1024
         ),
         name="score",
-    )(plan, sizes, arrived, candidates, *loose)
+    )(candidates, arrived, *loose)
 
 
 def on_device(
@@ -635,7 +690,7 @@
         bias_first.reshape(1, -1),
         mlp_second,
         bias_second.reshape(1, -1),
-        score_proj.reshape(1, -1),
+        score_proj.reshape(-1, LANES),
     )
     lines = scorer_count * (reqs * cands // 2) // LANES
     table = score(

time: 100 us -> 99 us (0.990)
  local copies, waits for them, and re-layouts: 5.23 us -> 0 us
  Pallas kernels: 93.9 us -> 96.8 us
    unnamed x34 -> x0, local copies, waits for them, and re-layouts: 4.57 us -> none
    pallas_call x1, Pallas kernels: 8.06 us -> 12.4 us  [gather_spans(): pl.pallas_call(functools.partial(gather_kernel, scorers), out_shape=jax.S...]
    pallas_call x1, Pallas kernels: 52.8 us -> 51.2 us  [fetch(): pl.pallas_call(functools.partial(fetch_kernel, stores, scorers, per_pair)...]
where the time goes in v5:
time: 99 us; the launch traced here: 98.4 us
  Pallas kernels  96.8 us (98%)
  other arithmetic  1.52 us (2%)
    pallas_call x1, Pallas kernels, fetch(): pl.pallas_call(functools.partial(fetch_kernel, stores, scorers, per_pair)...  51.2 us
    pallas_call x1, Pallas kernels, score(): pl.pallas_call(functools.partial(score_kernel, per_pair), grid=(reqs,), o...  33.3 us
    pallas_call x1, Pallas kernels, gather_spans(): pl.pallas_call(functools.partial(gather_kernel, scorers), out_shape=jax.S...  12.4 us

profile of v5, /device:TPU:0, one launch (start us, length us, event | category | flops | bytes accessed | tf_op | source)
XLA Modules:
  0.0 98.4 jit_solution(16106879270521176039)
XLA Ops:
  0.0 51.2 %fetch.1 = (bf16[128,32,256]{2,1,0:T(8,128)(2,1)}, f32[128,1,128]{2,1,0:T(1,128)}, s32[32,128]{1,0:T(8,128)}) custom-call(s32[8,512]{1,0:T(8,128)} %ids_hbm.1, s32[8]{0:T(128)} %rest_2_.1, s32[2048,128]{1,0:T(8,128)} %bitcast.10, bf16[2048,256]{1,0:T(8,128)(2,1)} %store_hbm.1, bf16[16,128]{1,0:T(8,128)(2,1)} %bitcast.11), custom_call_target="tpu_custom_call" | custom-call | flops 40000000000 | bytes 8388608 | tf_op jit(solution)/shard_map/fetch/pallas_call | solution.py:300
  51.2 33.3 %score.1 = f32[256,128]{1,0:T(8,128)} custom-call(bf16[8,512,256]{2,1,0:T(8,128)(2,1)} %cand_ref.1, bf16[4096,256]{1,0:T(8,128)(2,1)} %bitcast.15, s32[32,128]{1,0:T(8,128)} %get-tuple-element.9.rest_0_, f32[128,128]{1,0:T(8,128)} %bitcast.16, s32[8]{0:T(128)} %rest_2_.1, s32[8]{0:T(128)} %rest_3_.1, s32[8,512]{1,0:T(8,128)} %rest_4_.1, ...), custom_call_target="tpu_custom_call" | custom-call | flops 30000001024 | bytes 8388608 | tf_op jit(solution)/shard_map/score/pallas_call | solution.py:612
  84.4 12.4 %gather_spans.1 = f32[16,16,128]{2,1,0:T(8,128)} custom-call(f32[16,16,128]{2,1,0:T(8,128)} %bitcast.9), custom_call_target="tpu_custom_call" | custom-call | tf_op jit(solution)/shard_map/gather_spans/pallas_call | solution.py:385
  96.9 1.5 %reduce_sum.9 = f32[16,128]{1,0:T(8,128)} reduce(f32[16,16,128]{2,1,0:T(8,128)} %gather_spans.1, f32[]{:T(128)} %constant.0.clone.1), dimensions={0}, to_apply=%region_0.0 | reduce | flops 30720 | bytes 139268 | tf_op jit(solution)/shard_map/reduce_sum | solution.py:699

commit v6 on v5

--- a/solution.py
+++ b/solution.py
@@ -39,7 +39,7 @@
 
 
 def plan_asks(
-    per_pair, rows_dev, ids_smem, valid_smem, ids_ref, table_ref, ask_ref, plan_ref, even, odd, starts
+    per_pair, rows_dev, lines_smem, valid_smem, ids_ref, table_ref, ask_ref, plan_ref, even, odd, starts
 ):
     reqs, slots = ids_ref.shape
     shift_rows = rows_dev.bit_length() - 1
@@ -52,8 +52,8 @@
 
     def look(r, into):
         for u in range(slots):
-            c = ids_smem[r, u]
-            into[u : u + 1, :] = table_ref[pl.ds(lax.shift_right_logical(c, 7), 1), :]
+            c = lines_smem[r, u]
+            into[u : u + 1, :] = table_ref[pl.ds(c, 1), :]
 
     def rank(r, held, base, acc):
         starts[pl.ds(r, 1), :] = base
@@ -120,13 +120,26 @@
     table_hbm,
     store_hbm,
     sizes_hbm,
+    cand_hbm,
+    wq_hbm,
+    m1_hbm,
+    b1_hbm,
     rows_out,
     sizes_out,
     plan_hbm,
+    query_hbm,
+    hidden_hbm,
     plan_ref,
-    ids_smem,
+    lines_smem,
     valid_smem,
     ids_ref,
+    lines_ref,
+    cand_ref,
+    wq_ref,
+    m1_ref,
+    b1_ref,
+    query_scr,
+    hidden_scr,
     table_ref,
     store_ref,
     sizes_ref,
@@ -161,28 +174,52 @@
         pltpu.make_async_copy(src, dst, load_sems.at[n])
         for n, (src, dst) in enumerate(
             (
-                (ids_hbm, ids_smem),
-                (table_hbm, table_ref),
                 (ids_hbm, ids_ref),
-                (valid_hbm, valid_smem),
                 (store_hbm, store_ref),
                 (sizes_hbm, sizes_ref),
+                (table_hbm, table_ref),
+                (valid_hbm, valid_smem),
+                (cand_hbm, cand_ref),
+                (wq_hbm, wq_ref),
+                (m1_hbm.at[pl.ds(0, m1_ref.shape[0])], m1_ref),
+                (b1_hbm, b1_ref),
             )
         )
     ]
     for load in loads:
         load.start()
 
-    def greet(i, carry):
+    def greet(i):
         pl.semaphore_signal(barrier, inc=1, device_id=peer_of(i, pairs, scorers), device_id_type=MESH)
+
+    def greet_one(i, carry):
+        greet(i)
         return carry
 
-    lax.fori_loop(1, pairs, greet, 0)
-    for load in loads:
+    loads[0].wait()
+    lines_ref[...] = lax.shift_right_logical(ids_ref[...], 7)
+    lines_load = pltpu.make_async_copy(lines_ref, lines_smem, load_sems.at[0])
+    lines_load.start()
+    half = pairs // 2
+    lax.fori_loop(1, half, greet_one, 0)
+    for load in loads[1:5]:
         load.wait()
-
+    portion = rows_dev // half
+
+    def greet_and_widen(i, carry):
+        greet(half + i)
+        part = pl.ds(pl.multiple_of(i * portion, portion), portion)
+        left_scr[part, :] = store_ref[part, :LANES].astype(F32)
+        right_scr[part, :] = store_ref[part, LANES:].astype(F32)
+        return carry
+
+    lax.fori_loop(0, half, greet_and_widen, 0)
+    offsets = sizes_ref[...].astype(F32)
+    for t in range(sizes_ref.shape[0]):
+        size_scr[t * LANES : (t + 1) * LANES, :] = column_of(offsets[t : t + 1, :])
+    lines_load.wait()
     plan_asks(
-        per_pair, rows_dev, ids_smem, valid_smem, ids_ref, table_ref, ask_ref, plan_ref, even, odd, starts
+        per_pair, rows_dev, lines_smem, valid_smem, ids_ref, table_ref, ask_ref, plan_ref, even, odd, starts
     )
     plan_out = pltpu.make_async_copy(plan_ref, plan_hbm, load_sems.at[0])
     plan_out.start()
@@ -208,11 +245,6 @@
     for g in range(1, AHEAD):
         ask_group(g, 0)
     ask_in[0] = ask_ref[me]
-    left_scr[...] = store_ref[:, :LANES].astype(F32)
-    right_scr[...] = store_ref[:, LANES:].astype(F32)
-    offsets = sizes_ref[...].astype(F32)
-    for t in range(sizes_ref.shape[0]):
-        size_scr[t * LANES : (t + 1) * LANES, :] = column_of(offsets[t : t + 1, :])
 
     def settle(ref, first, count, sem):
         part = ref.at[pl.ds(first, count)]
@@ -279,6 +311,20 @@
     own_sizes = pltpu.make_async_copy(sizes_send.at[0], sizes_out.at[me], load_sems.at[2])
     own_rows.start()
     own_sizes.start()
+    for load in loads[5:]:
+        load.wait()
+
+    def project(r, carry):
+        cand = cand_ref[r]
+        query_scr[r] = jnp.dot(cand, wq_ref[...], preferred_element_type=F32).astype(BF)
+        hidden_scr[r] = jnp.dot(cand, m1_ref[...], preferred_element_type=F32) + b1_ref[...]
+        pltpu.make_async_copy(query_scr.at[r], query_hbm.at[r], load_sems.at[3]).start()
+        pltpu.make_async_copy(hidden_scr.at[r], hidden_hbm.at[r], load_sems.at[4]).start()
+        return carry
+
+    lax.fori_loop(0, cand_ref.shape[0], project, 0)
+    pltpu.make_async_copy(query_scr, query_hbm, load_sems.at[3]).wait()
+    pltpu.make_async_copy(hidden_scr, hidden_hbm, load_sems.at[4]).wait()
     own_rows.wait()
     own_sizes.wait()
     plan_out.wait()
@@ -289,9 +335,11 @@
     settle(sizes_out, 0, pairs - 1, recv_sems.at[1])
 
 
-def fetch(ids, valid, table, store_rows, logsize, stores, scorers, per_pair):
+def fetch(
+    ids, valid, table, store_rows, logsize, candidates, wq, m1, b1, stores, scorers, per_pair
+):
     pairs = stores * scorers
-    groups = 8
+    groups = 4
     reqs, slots = ids.shape
     rows_dev, width = store_rows.shape
     hbm = pl.BlockSpec(memory_space=pltpu.HBM)
@@ -303,14 +351,23 @@
             jax.ShapeDtypeStruct((pairs, per_pair, width), BF),
             jax.ShapeDtypeStruct((pairs, 1, LANES), F32),
             jax.ShapeDtypeStruct((4 * reqs, LANES), jnp.int32),
+            jax.ShapeDtypeStruct(candidates.shape, BF),
+            jax.ShapeDtypeStruct(candidates.shape[:2] + m1.shape[1:], F32),
         ),
-        in_specs=[hbm] * 5,
-        out_specs=(hbm, hbm, hbm),
+        in_specs=[hbm] * 9,
+        out_specs=(hbm,) * 5,
         scratch_shapes=[
             pltpu.VMEM((4 * reqs, LANES), jnp.int32),
             pltpu.SMEM(ids.shape, jnp.int32),
             pltpu.SMEM(valid.shape, jnp.int32),
             pltpu.VMEM(ids.shape, jnp.int32),
+            pltpu.VMEM(ids.shape, jnp.int32),
+            pltpu.VMEM(candidates.shape, BF),
+            pltpu.VMEM(wq.shape, BF),
+            pltpu.VMEM((width, m1.shape[1]), BF),
+            pltpu.VMEM(b1.shape, F32),
+            pltpu.VMEM(candidates.shape, BF),
+            pltpu.VMEM(candidates.shape[:2] + m1.shape[1:], F32),
             pltpu.VMEM(table.shape, jnp.int32),
             pltpu.VMEM(store_rows.shape, BF),
             pltpu.VMEM(logsize.shape, BF),
@@ -328,7 +385,7 @@
             part,
             pltpu.VMEM((pairs, per_pair, width), BF),
             pltpu.VMEM((pairs, 1, LANES), F32),
-            pltpu.SemaphoreType.DMA((6,)),
+            pltpu.SemaphoreType.DMA((9,)),
             pltpu.SemaphoreType.DMA((groups,)),
             pltpu.SemaphoreType.DMA((groups,)),
             pltpu.SemaphoreType.DMA((3,)),
@@ -341,7 +398,7 @@
             flops=FETCH_FLOPS, bytes_accessed=8 * 1024 * 1024, transcendentals=0
         ),
         name="fetch",
-    )(ids, valid, table, store_rows, logsize)
+    )(ids, valid, table, store_rows, logsize, candidates, wq, m1, b1)
 
 
 def gather_kernel(scorers, table_ref, landed, send_sem, recv_sem, own_sem):
@@ -389,7 +446,7 @@
         out_specs=vm,
         scratch_shapes=[pltpu.SemaphoreType.DMA] * 3,
         compiler_params=pltpu.CompilerParams(
-            vmem_limit_bytes=VMEM_LIMIT, collective_id=1, has_side_effects=True
+            vmem_limit_bytes=4 * 1024 * 1024, collective_id=1, has_side_effects=True
         ),
         name="gather_spans",
     )(table.reshape(scorers, lines, LANES))
@@ -397,18 +454,20 @@
 
 def score_kernel(
     per_pair,
-    cand_ref,
+    query_ref,
+    hidden_ref,
     arrived_hbm,
     *rest,
 ):
-    held_in_hbm, out_ref, rest = rest[:14], rest[14], rest[15:]
-    local_copies, rest = rest[:14], rest[14:]
-    score_body(per_pair, cand_ref, arrived_hbm, out_ref, held_in_hbm, local_copies, *rest)
+    held_in_hbm, out_ref, rest = rest[:12], rest[12], rest[13:]
+    local_copies, rest = rest[:12], rest[12:]
+    score_body(per_pair, query_ref, hidden_ref, arrived_hbm, out_ref, held_in_hbm, local_copies, *rest)
 
 
 def score_body(
     per_pair,
-    cand_ref,
+    query_ref,
+    hidden_ref,
     arrived_hbm,
     out_ref,
     held_in_hbm,
@@ -432,12 +491,10 @@
         valid_smem,
         count_smem,
         row_ref,
-        wq_ref,
         wk_ref,
         wv_ref,
         wo_ref,
         m1_ref,
-        b1_ref,
         m2_ref,
         b2_ref,
         sp_ref,
@@ -446,10 +503,17 @@
     reqs = pl.num_programs(0)
     total_slots, width = arrived_ref.shape
     slots = ctx_scr.shape[0]
-    cands = cand_ref.shape[1]
+    cands = query_ref.shape[1]
     pairs = sizes_ref.shape[0]
     head_size = width // HEADS
     copies = ((left_scr, x_left), (right_scr, x_right), (size_scr, x_size))
+
+    def group_rows(req):
+        for s in range(pairs):
+            at = plan_smem[req, s]
+            to = plan_smem[req + reqs, s]
+            for held, taken in copies:
+                taken[pl.ds(to, CHUNK), :] = held[pl.ds(at, CHUNK), :]
 
     @pl.when(r == 0)
     def _():
@@ -496,15 +560,10 @@
             part = slice(n * quarter, (n + 1) * quarter)
             left_scr[part, :] = arrived_ref[part, :LANES].astype(F32)
             right_scr[part, :] = arrived_ref[part, LANES:].astype(F32)
+        group_rows(0)
 
     valid = valid_smem[r]
     count = count_smem[r]
-
-    for s in range(pairs):
-        at = plan_smem[r, s]
-        to = plan_smem[r + reqs, s]
-        for held, taken in copies:
-            taken[pl.ds(to, CHUNK), :] = held[pl.ds(at, CHUNK), :]
 
     @pl.when(plan_smem[r + 3 * reqs, 0] > CHUNK)
     def _():
@@ -525,13 +584,12 @@
 
         lax.fori_loop(0, pairs, rest, 0)
 
-    cand = cand_ref[0]
-    query = jnp.dot(cand, wq_ref[...], preferred_element_type=F32)
+    query = query_ref[0]
     clane = lax.broadcasted_iota(jnp.int32, (cands, LANES), 1)
     queries = []
     for p in range(2):
-        own = query[:, p * LANES : (p + 1) * LANES].astype(BF)
-        other = query[:, (1 - p) * LANES : (2 - p) * LANES]
+        own = query[:, p * LANES : (p + 1) * LANES]
+        other = query[:, (1 - p) * LANES : (2 - p) * LANES].astype(F32)
         other = jnp.where(clane == 0, 1.0, other).astype(BF)
         queries.append(jnp.concatenate([own, other] if p == 0 else [other, own], axis=1))
 
@@ -575,10 +633,10 @@
         def _(n=n):
             attend(n * LANES)
 
+    group_rows(jnp.minimum(r + 1, reqs - 1))
     attended = jnp.dot(ctx_scr[...], wo_ref[...], preferred_element_type=F32).astype(BF)
-    hidden = jnp.dot(cand, m1_ref[:width, :], preferred_element_type=F32)
-    hidden += jnp.dot(attended, m1_ref[width:, :], preferred_element_type=F32)
-    hidden = jnp.maximum(hidden + b1_ref[...], 0.0).astype(BF)
+    hidden = hidden_ref[0] + jnp.dot(attended, m1_ref[width:, :], preferred_element_type=F32)
+    hidden = jnp.maximum(hidden, 0.0).astype(BF)
     hidden = jnp.dot(hidden, m2_ref[...], preferred_element_type=F32)
     hidden = jnp.maximum(hidden + b2_ref[...], 0.0).astype(BF)
     weight = sp_ref[...].astype(F32)
@@ -601,8 +659,8 @@
     )
 
 
-def score(plan, per_pair, valid, count, sizes, arrived, candidates, rows, weights, lines):
-    reqs, cands, width = candidates.shape
+def score(plan, per_pair, valid, count, sizes, arrived, queries, hidden, rows, weights, lines):
+    reqs, cands, width = queries.shape
     total_slots = arrived.shape[0]
     slots = total_slots // reqs
     hbm = pl.BlockSpec(memory_space=pltpu.HBM)
@@ -613,7 +671,12 @@
         functools.partial(score_kernel, per_pair),
         grid=(reqs,),
         out_shape=jax.ShapeDtypeStruct((lines, LANES), F32),
-        in_specs=[pl.BlockSpec((1, cands, width), lambda r: (r, 0, 0)), hbm] + [hbm] * len(loose),
+        in_specs=[
+            pl.BlockSpec((1, cands, width), lambda r: (r, 0, 0)),
+            pl.BlockSpec((1,) + hidden.shape[1:], lambda r: (r, 0, 0)),
+            hbm,
+        ]
+        + [hbm] * len(loose),
         out_specs=pl.BlockSpec((lines, LANES), lambda r: (0, 0)),
         scratch_shapes=[
             pltpu.SMEM(plan.shape, jnp.int32),
@@ -641,7 +704,7 @@
             flops=SCORE_FLOPS, bytes_accessed=8 * 1024 * 1024, transcendentals=8 * 1024 * 1024
         ),
         name="score",
-    )(candidates, arrived, *loose)
+    )(queries, hidden, arrived, *loose)
 
 
 def on_device(
@@ -669,12 +732,16 @@
     slot_total = cluster_ids.size
     per_pair = slot_total // device_count
     reqs, cands = candidate_row.shape
-    arrived, sizes, plan = fetch(
+    arrived, sizes, plan, queries, hidden = fetch(
         cluster_ids,
         valid_count,
         cluster_home.reshape(-1, LANES),
         store_rows,
         cluster_logsize.reshape(-1, LANES),
+        candidates,
+        query_proj,
+        mlp_first,
+        bias_first.reshape(1, -1),
         device_count // scorer_count,
         scorer_count,
         per_pair,
@@ -682,19 +749,17 @@
     arrived = arrived.reshape(slot_total, width)
     sizes = sizes.reshape(device_count, LANES)
     weights = (
-        query_proj,
         key_proj,
         value_proj,
         out_proj,
         mlp_first,
-        bias_first.reshape(1, -1),
         mlp_second,
         bias_second.reshape(1, -1),
         score_proj.reshape(-1, LANES),
     )
     lines = scorer_count * (reqs * cands // 2) // LANES
     table = score(
-        plan, per_pair, valid_count, cand_count, sizes, arrived, candidates, candidate_row, weights, lines
+        plan, per_pair, valid_count, cand_count, sizes, arrived, queries, hidden, candidate_row, weights, lines
     )
     return jnp.sum(gather_spans(table, scorer_count), axis=0).reshape(-1)
 

time: 99 us -> 89.3 us (0.902)
  Pallas kernels: 96.8 us -> 87.6 us
    pallas_call x1, Pallas kernels: 33.3 us -> 25.3 us  [score(): pl.pallas_call(functools.partial(score_kernel, per_pair), grid=(reqs,), o...]
    pallas_call x1, Pallas kernels: 51.2 us -> 49.8 us  [fetch(): pl.pallas_call(functools.partial(fetch_kernel, stores, scorers, per_pair)...]
where the time goes in v6:
time: 89.3 us; the launch traced here: 89.1 us
  Pallas kernels  87.6 us (98%)
  local copies, waits for them, and re-layouts  0.9 us (1%)
    pallas_call x1, Pallas kernels, fetch(): pl.pallas_call(functools.partial(fetch_kernel, stores, scorers, per_pair)...  49.8 us
    pallas_call x1, Pallas kernels, score(): pl.pallas_call(functools.partial(score_kernel, per_pair), grid=(reqs,), o...  25.3 us
    pallas_call x1, Pallas kernels, gather_spans(): pl.pallas_call(functools.partial(gather_kernel, scorers), out_shape=jax.S...  12.4 us

profile of v6, /device:TPU:0, one launch (start us, length us, event | category | flops | bytes accessed | tf_op | source)
XLA Modules:
  0.0 89.1 jit_solution(16776924519634958762)
XLA Ops:
  0.0 49.8 %fetch.1 = (bf16[128,32,256]{2,1,0:T(8,128)(2,1)}, f32[128,1,128]{2,1,0:T(1,128)}, s32[32,128]{1,0:T(8,128)}, bf16[8,512,256]{2,1,0:T(8,128)(2,1)}, f32[8,512,512]{2,1,0:T(8,128)}) custom-call(s32[8,512]{1,0:T(8,128)} %ids_hbm.1, s32[8]{0:T(128)} %rest_2_.1, s32[2048,128]{1,0:T(8,128)} %bitcast.10, bf16[2048,256]{1,0:T(8,128)(2,1)} %store_hbm.1, ...), custom_call_target="tpu_custom_call" | custom-call | flops 40000000000 | bytes 8388608 | tf_op jit(solution)/shard_map/fetch/pallas_call | solution.py:348
  49.8 25.3 %score.1 = f32[256,128]{1,0:T(8,128)} custom-call(bf16[8,512,256]{2,1,0:T(8,128)(2,1)} %get-tuple-element.10.query_ref, f32[8,512,512]{2,1,0:T(8,128)} %get-tuple-element.11.hidden_ref, bf16[4096,256]{1,0:T(8,128)(2,1)} %bitcast.15, s32[32,128]{1,0:T(8,128)} %get-tuple-element.13.rest_0_, f32[128,128]{1,0:T(8,128)} %bitcast.16, s32[8]{0:T(128)} %rest_2_.1, ...), custom_call_target="tpu_custom_call" | custom-call | flops 30000001024 | bytes 8388608 | tf_op jit(solution)/shard_map/score/pallas_call | solution.py:670
  75.2 0.0 copy-start
  75.2 0.9 %copy-done = f32[256,128]{1,0:T(8,128)S(1)} copy-done((f32[256,128]{1,0:T(8,128)S(1)}, f32[256,128]{1,0:T(8,128)}, u32[]{:S(2)}) %copy-start) | copy-done | bytes 131096
  76.1 12.4 %gather_spans.1 = f32[16,16,128]{2,1,0:T(8,128)S(1)} custom-call(f32[16,16,128]{2,1,0:T(8,128)S(1)} %bitcast.9), custom_call_target="tpu_custom_call" | custom-call | tf_op jit(solution)/shard_map/gather_spans/pallas_call | solution.py:442
  88.5 0.6 reduce_sum.9
Async XLA Ops:
  75.2 0.9 %copy-start = (f32[256,128]{1,0:T(8,128)S(1)}, f32[256,128]{1,0:T(8,128)}, u32[]{:S(2)}) copy-start(f32[256,128]{1,0:T(8,128)} %score.1) | copy-start | bytes 393220

commit v7 on v6

--- a/solution.py
+++ b/solution.py
@@ -535,9 +535,6 @@
         for block in blocks:
             block.start()
         k_scr[...] = jnp.zeros_like(k_scr)
-        ones_lane = lax.broadcasted_iota(jnp.int32, (slots, LANES), 1) // head_size
-        for h in range(HEADS):
-            v_scr[h, :, LANES:] = jnp.where(ones_lane == h % 2, 1.0, 0.0).astype(BF)
         for held, taken in copies:
             held[total_slots:, :] = jnp.zeros((CHUNK, LANES), F32)
             taken[...] = jnp.zeros_like(taken)
@@ -606,22 +603,29 @@
         bias = jnp.where(slot < valid, bias, -1e30)
         bias = jnp.where(sub == 0, bias, 0.0).astype(BF)
         lane = lax.broadcasted_iota(jnp.int32, (live, LANES), 1)
+        blank = jnp.zeros((head_size, live), BF)
         for h in range(HEADS):
-            half = slice((h // 2) * LANES, (h // 2 + 1) * LANES)
-            own = slice(h * head_size, (h + 1) * head_size)
-            other = (1 - h // 2) * LANES
-            mine = (lane // head_size) == (h % 2)
-            k_scr[h, own, :live] = keys[own, :]
-            k_scr[h, other : other + 16, :live] = bias
-            v_scr[h, :live, :LANES] = jnp.where(mine, values[:, half], 0.0).astype(BF)
+            p, side = h // 2, h % 2
+            half = slice(p * LANES, (p + 1) * LANES)
+            own = keys[h * head_size : (h + 1) * head_size, :]
+            other = (1 - p) * LANES
+            span = slice(side * live, (side + 1) * live)
+            mine = (lane // head_size) == side
+            k_scr[p, half, span] = jnp.concatenate(
+                [own, blank] if side == 0 else [blank, own], axis=0
+            )
+            k_scr[p, other : other + 16, span] = bias
+            v_scr[p, span, :LANES] = jnp.where(mine, values[:, half], 0.0).astype(BF)
+            v_scr[p, span, LANES:] = jnp.where(mine, 1.0, 0.0).astype(BF)
         for p in range(2):
-            total = None
-            for h in (2 * p, 2 * p + 1):
-                logits = jnp.dot(queries[p], k_scr[h, :, :live], preferred_element_type=F32)
-                top = jnp.max(logits, axis=1, keepdims=True)
-                probs = jnp.exp(logits - top).astype(BF)
-                part = jnp.dot(probs, v_scr[h, :live, :], preferred_element_type=F32)
-                total = part if total is None else total + part
+            logits = jnp.dot(queries[p], k_scr[p, :, : 2 * live], preferred_element_type=F32)
+            probs = []
+            for side in range(2):
+                part = logits[:, side * live : (side + 1) * live]
+                top = jnp.max(part, axis=1, keepdims=True)
+                probs.append(jnp.exp(part - top).astype(BF))
+            probs = jnp.concatenate(probs, axis=1)
+            total = jnp.dot(probs, v_scr[p, : 2 * live, :], preferred_element_type=F32)
             ctx_scr[:, p * LANES : (p + 1) * LANES] = (
                 total[:, :LANES] / total[:, LANES:]
             ).astype(BF)
@@ -629,34 +633,42 @@
     blocks = slots // LANES
     for n in range(1, blocks + 1):
 
-        @pl.when(jnp.logical_and(valid <= n * LANES, valid > (n - 1) * LANES))
+        @pl.when(jnp.logical_and(count > 0, (valid + LANES - 1) // LANES == n))
         def _(n=n):
             attend(n * LANES)
 
-    group_rows(jnp.minimum(r + 1, reqs - 1))
-    attended = jnp.dot(ctx_scr[...], wo_ref[...], preferred_element_type=F32).astype(BF)
-    hidden = hidden_ref[0] + jnp.dot(attended, m1_ref[width:, :], preferred_element_type=F32)
-    hidden = jnp.maximum(hidden, 0.0).astype(BF)
-    hidden = jnp.dot(hidden, m2_ref[...], preferred_element_type=F32)
-    hidden = jnp.maximum(hidden + b2_ref[...], 0.0).astype(BF)
-    weight = sp_ref[...].astype(F32)
-    weight = jnp.concatenate([weight[n : n + 1, :] for n in range(width // LANES)], axis=1)
-    weight = jnp.broadcast_to(weight, (16, width)).astype(BF)
-    score = lax.dot_general(weight, hidden, NT, preferred_element_type=F32)[0:1, :]
-    slot = lax.broadcasted_iota(jnp.int32, (1, cands), 1)
-    score = jnp.where(slot < count, score, 0.0)
-    first = score.astype(BF).astype(F32)
-    second = score - first
-    row = row_ref[pl.ds(r, 1), :]
-    lines = out_ref.shape[0]
-    at_line = lax.broadcasted_iota(jnp.int32, (lines, cands), 0) == lax.shift_right_logical(row, 7)
-    at_lane = lax.broadcasted_iota(jnp.int32, (LANES, cands), 0) == (row & (LANES - 1))
-    at_lane = jnp.where(at_lane, 1.0, 0.0).astype(BF)
-    out_ref[...] += lax.dot_general(
-        jnp.where(at_line, first, 0.0).astype(BF), at_lane, NT, preferred_element_type=F32
-    ) + lax.dot_general(
-        jnp.where(at_line, second, 0.0).astype(BF), at_lane, NT, preferred_element_type=F32
-    )
+    following = jnp.minimum(r + 1, reqs - 1)
+
+    @pl.when(count <= 0)
+    def _():
+        group_rows(following)
+
+    @pl.when(count > 0)
+    def _():
+        group_rows(following)
+        attended = jnp.dot(ctx_scr[...], wo_ref[...], preferred_element_type=F32).astype(BF)
+        hidden = hidden_ref[0] + jnp.dot(attended, m1_ref[width:, :], preferred_element_type=F32)
+        hidden = jnp.maximum(hidden, 0.0).astype(BF)
+        hidden = jnp.dot(hidden, m2_ref[...], preferred_element_type=F32)
+        hidden = jnp.maximum(hidden + b2_ref[...], 0.0).astype(BF)
+        weight = sp_ref[...].astype(F32)
+        weight = jnp.concatenate([weight[n : n + 1, :] for n in range(width // LANES)], axis=1)
+        weight = jnp.broadcast_to(weight, (16, width)).astype(BF)
+        score = lax.dot_general(weight, hidden, NT, preferred_element_type=F32)[0:1, :]
+        slot = lax.broadcasted_iota(jnp.int32, (1, cands), 1)
+        score = jnp.where(slot < count, score, 0.0)
+        first = score.astype(BF).astype(F32)
+        second = score - first
+        row = row_ref[pl.ds(r, 1), :]
+        lines = out_ref.shape[0]
+        at_line = lax.broadcasted_iota(jnp.int32, (lines, cands), 0) == lax.shift_right_logical(row, 7)
+        at_lane = lax.broadcasted_iota(jnp.int32, (LANES, cands), 0) == (row & (LANES - 1))
+        at_lane = jnp.where(at_lane, 1.0, 0.0).astype(BF)
+        out_ref[...] += lax.dot_general(
+            jnp.where(at_line, first, 0.0).astype(BF), at_lane, NT, preferred_element_type=F32
+        ) + lax.dot_general(
+            jnp.where(at_line, second, 0.0).astype(BF), at_lane, NT, preferred_element_type=F32
+        )
 
 
 def score(plan, per_pair, valid, count, sizes, arrived, queries, hidden, rows, weights, lines):
@@ -693,8 +705,8 @@
             taken,
             taken,
             taken,
-            pltpu.VMEM((HEADS, width, slots), BF),
-            pltpu.VMEM((HEADS, slots, width), BF),
+            pltpu.VMEM((2, width, 2 * slots), BF),
+            pltpu.VMEM((2, 2 * slots, width), BF),
             pltpu.VMEM((cands, width), BF),
             pltpu.VMEM((width, width), BF),
             pltpu.SemaphoreType.DMA((len(loose) + 4,)),

time: 89.3 us -> 86.9 us (0.973)
  the two profiles are of different devices: /device:TPU:0 before, /device:TPU:1 now
where the time goes in v7:
time: 86.9 us; the launch traced here: 86.7 us
  Pallas kernels  85.1 us (98%)
  local copies, waits for them, and re-layouts  0.9 us (1%)
    pallas_call x1, Pallas kernels, fetch(): pl.pallas_call(functools.partial(fetch_kernel, stores, scorers, per_pair)...  50.7 us
    pallas_call x1, Pallas kernels, score(): pl.pallas_call(functools.partial(score_kernel, per_pair), grid=(reqs,), o...  21 us
    pallas_call x1, Pallas kernels, gather_spans(): pl.pallas_call(functools.partial(gather_kernel, scorers), out_shape=jax.S...  13.4 us

profile of v7, /device:TPU:1, one launch (start us, length us, event | category | flops | bytes accessed | tf_op | source)
XLA Modules:
  0.0 86.7 jit_solution(7923471378369472035)
XLA Ops:
  0.0 50.7 %fetch.1 = (bf16[128,32,256]{2,1,0:T(8,128)(2,1)}, f32[128,1,128]{2,1,0:T(1,128)}, s32[32,128]{1,0:T(8,128)}, bf16[8,512,256]{2,1,0:T(8,128)(2,1)}, f32[8,512,512]{2,1,0:T(8,128)}) custom-call(s32[8,512]{1,0:T(8,128)} %ids_hbm.1, s32[8]{0:T(128)} %rest_2_.1, s32[2048,128]{1,0:T(8,128)} %bitcast.10, bf16[2048,256]{1,0:T(8,128)(2,1)} %store_hbm.1, ...), custom_call_target="tpu_custom_call" | custom-call | flops 40000000000 | bytes 8388608 | tf_op jit(solution)/shard_map/fetch/pallas_call | solution.py:348
  50.8 21.0 %score.1 = f32[256,128]{1,0:T(8,128)} custom-call(bf16[8,512,256]{2,1,0:T(8,128)(2,1)} %get-tuple-element.10.query_ref, f32[8,512,512]{2,1,0:T(8,128)} %get-tuple-element.11.hidden_ref, bf16[4096,256]{1,0:T(8,128)(2,1)} %bitcast.15, s32[32,128]{1,0:T(8,128)} %get-tuple-element.13.rest_0_, f32[128,128]{1,0:T(8,128)} %bitcast.16, s32[8]{0:T(128)} %rest_2_.1, ...), custom_call_target="tpu_custom_call" | custom-call | flops 30000001024 | bytes 8388608 | tf_op jit(solution)/shard_map/score/pallas_call | solution.py:682
  71.8 0.0 copy-start
  71.8 0.9 %copy-done = f32[256,128]{1,0:T(8,128)S(1)} copy-done((f32[256,128]{1,0:T(8,128)S(1)}, f32[256,128]{1,0:T(8,128)}, u32[]{:S(2)}) %copy-start) | copy-done | bytes 131096
  72.7 13.4 %gather_spans.1 = f32[16,16,128]{2,1,0:T(8,128)S(1)} custom-call(f32[16,16,128]{2,1,0:T(8,128)S(1)} %bitcast.9), custom_call_target="tpu_custom_call" | custom-call | tf_op jit(solution)/shard_map/gather_spans/pallas_call | solution.py:442
  86.1 0.6 reduce_sum.9
Async XLA Ops:
  71.8 0.9 %copy-start = (f32[256,128]{1,0:T(8,128)S(1)}, f32[256,128]{1,0:T(8,128)}, u32[]{:S(2)}) copy-start(f32[256,128]{1,0:T(8,128)} %score.1) | copy-start | bytes 393220

commit v8 on v6

--- a/solution.py
+++ b/solution.py
@@ -454,20 +454,20 @@
 
 def score_kernel(
     per_pair,
-    query_ref,
-    hidden_ref,
+    query_hbm,
+    hidden_hbm,
     arrived_hbm,
     *rest,
 ):
     held_in_hbm, out_ref, rest = rest[:12], rest[12], rest[13:]
     local_copies, rest = rest[:12], rest[12:]
-    score_body(per_pair, query_ref, hidden_ref, arrived_hbm, out_ref, held_in_hbm, local_copies, *rest)
+    score_body(per_pair, query_hbm, hidden_hbm, arrived_hbm, out_ref, held_in_hbm, local_copies, *rest)
 
 
 def score_body(
     per_pair,
-    query_ref,
-    hidden_ref,
+    query_hbm,
+    hidden_hbm,
     arrived_hbm,
     out_ref,
     held_in_hbm,
@@ -483,7 +483,10 @@
     v_scr,
     ctx_scr,
     wkt_scr,
+    query_ref,
+    hidden_ref,
     load_sems,
+    step_sems,
 ):
     (
         plan_smem,
@@ -499,8 +502,7 @@
         b2_ref,
         sp_ref,
     ) = local_copies
-    r = pl.program_id(0)
-    reqs = pl.num_programs(0)
+    reqs = query_ref.shape[0]
     total_slots, width = arrived_ref.shape
     slots = ctx_scr.shape[0]
     cands = query_ref.shape[1]
@@ -515,148 +517,179 @@
             for held, taken in copies:
                 taken[pl.ds(to, CHUNK), :] = held[pl.ds(at, CHUNK), :]
 
-    @pl.when(r == 0)
-    def _():
-        loads = [
-            pltpu.make_async_copy(src, dst, load_sems.at[n])
-            for n, (src, dst) in enumerate(zip(held_in_hbm, local_copies))
-        ]
-        for load in loads:
-            load.start()
-        quarter = total_slots // 4
-        blocks = [
-            pltpu.make_async_copy(
-                arrived_hbm.at[pl.ds(n * quarter, quarter)],
-                arrived_ref.at[pl.ds(n * quarter, quarter)],
-                load_sems.at[len(loads) + n],
+    loads = [
+        pltpu.make_async_copy(src, dst, load_sems.at[n])
+        for n, (src, dst) in enumerate(zip(held_in_hbm, local_copies))
+    ]
+    for load in loads:
+        load.start()
+    quarter = total_slots // 4
+    blocks = [
+        pltpu.make_async_copy(
+            arrived_hbm.at[pl.ds(n * quarter, quarter)],
+            arrived_ref.at[pl.ds(n * quarter, quarter)],
+            load_sems.at[len(loads) + n],
+        )
+        for n in range(4)
+    ]
+    for block in blocks:
+        block.start()
+
+    def step_loads(r):
+        return (
+            pltpu.make_async_copy(query_hbm.at[r], query_ref.at[r], step_sems.at[0, r]),
+            pltpu.make_async_copy(hidden_hbm.at[r], hidden_ref.at[r], step_sems.at[1, r]),
+        )
+
+    for load in step_loads(0):
+        load.start()
+    k_scr[...] = jnp.zeros_like(k_scr)
+    for held, taken in copies:
+        held[total_slots:, :] = jnp.zeros((CHUNK, LANES), F32)
+        taken[...] = jnp.zeros_like(taken)
+    out_ref[...] = jnp.zeros_like(out_ref)
+    for load in loads:
+        load.wait()
+    wkt_scr[...] = wk_ref[...].astype(F32).T.astype(BF)
+    group = LANES // per_pair
+    one = lax.broadcasted_iota(jnp.int32, (pairs // group, pairs), 1) // group
+    one = one == lax.broadcasted_iota(jnp.int32, (pairs // group, pairs), 0)
+    packed = jnp.dot(
+        jnp.where(one, 1.0, 0.0).astype(BF),
+        sizes_ref[...].astype(BF),
+        preferred_element_type=F32,
+    )
+    for t in range(pairs // group):
+        size_scr[t * LANES : (t + 1) * LANES, :] = column_of(packed[t : t + 1, :])
+    for n, block in enumerate(blocks):
+        block.wait()
+        part = slice(n * quarter, (n + 1) * quarter)
+        left_scr[part, :] = arrived_ref[part, :LANES].astype(F32)
+        right_scr[part, :] = arrived_ref[part, LANES:].astype(F32)
+    group_rows(0)
+
+    def one_request(r, carry):
+        for load in step_loads(r):
+            load.wait()
+
+        @pl.when(r + 1 < reqs)
+        def _():
+            for load in step_loads(r + 1):
+                load.start()
+
+        valid = valid_smem[r]
+        count = count_smem[r]
+
+        @pl.when(plan_smem[r + 3 * reqs, 0] > CHUNK)
+        def _():
+            def rest(s, carry):
+                at = plan_smem[r, s]
+                to = plan_smem[r + reqs, s]
+                left = plan_smem[r + 2 * reqs, s]
+                sub = lax.broadcasted_iota(jnp.int32, (CHUNK, LANES), 0)
+
+                @pl.when(left > CHUNK)
+                def _():
+                    for held, taken in copies:
+                        old = taken[pl.ds(to + CHUNK, CHUNK), :]
+                        new = held[pl.ds(at + CHUNK, CHUNK), :]
+                        taken[pl.ds(to + CHUNK, CHUNK), :] = jnp.where(sub < left - CHUNK, new, old)
+
+                return carry
+
+            lax.fori_loop(0, pairs, rest, 0)
+
+        query = query_ref[r]
+        clane = lax.broadcasted_iota(jnp.int32, (cands, LANES), 1)
+        queries = []
+        for p in range(2):
+            own = query[:, p * LANES : (p + 1) * LANES]
+            other = query[:, (1 - p) * LANES : (2 - p) * LANES].astype(F32)
+            other = jnp.where(clane == 0, 1.0, other).astype(BF)
+            queries.append(jnp.concatenate([own, other] if p == 0 else [other, own], axis=1))
+
+        def attend(live):
+            x = jnp.concatenate([x_left[:live, :], x_right[:live, :]], axis=1).astype(BF)
+            keys = lax.dot_general(wkt_scr[...], x, NT, preferred_element_type=F32)
+            keys = (keys.astype(BF).astype(F32) * 0.125).astype(BF)
+            values = jnp.dot(x, wv_ref[...], preferred_element_type=F32)
+            bias = jnp.concatenate(
+                [x_size[t : t + LANES, :].T[0:16, :] for t in range(0, live, LANES)], axis=1
             )
-            for n in range(4)
-        ]
-        for block in blocks:
-            block.start()
-        k_scr[...] = jnp.zeros_like(k_scr)
-        ones_lane = lax.broadcasted_iota(jnp.int32, (slots, LANES), 1) // head_size
-        for h in range(HEADS):
-            v_scr[h, :, LANES:] = jnp.where(ones_lane == h % 2, 1.0, 0.0).astype(BF)
-        for held, taken in copies:
-            held[total_slots:, :] = jnp.zeros((CHUNK, LANES), F32)
-            taken[...] = jnp.zeros_like(taken)
-        out_ref[...] = jnp.zeros_like(out_ref)
-        for load in loads:
-            load.wait()
-        wkt_scr[...] = wk_ref[...].astype(F32).T.astype(BF)
-        group = LANES // per_pair
-        one = lax.broadcasted_iota(jnp.int32, (pairs // group, pairs), 1) // group
-        one = one == lax.broadcasted_iota(jnp.int32, (pairs // group, pairs), 0)
-        packed = jnp.dot(
-            jnp.where(one, 1.0, 0.0).astype(BF),
-            sizes_ref[...].astype(BF),
-            preferred_element_type=F32,
-        )
-        for t in range(pairs // group):
-            size_scr[t * LANES : (t + 1) * LANES, :] = column_of(packed[t : t + 1, :])
-        for n, block in enumerate(blocks):
-            block.wait()
-            part = slice(n * quarter, (n + 1) * quarter)
-            left_scr[part, :] = arrived_ref[part, :LANES].astype(F32)
-            right_scr[part, :] = arrived_ref[part, LANES:].astype(F32)
-        group_rows(0)
-
-    valid = valid_smem[r]
-    count = count_smem[r]
-
-    @pl.when(plan_smem[r + 3 * reqs, 0] > CHUNK)
-    def _():
-        def rest(s, carry):
-            at = plan_smem[r, s]
-            to = plan_smem[r + reqs, s]
-            left = plan_smem[r + 2 * reqs, s]
-            sub = lax.broadcasted_iota(jnp.int32, (CHUNK, LANES), 0)
-
-            @pl.when(left > CHUNK)
-            def _():
-                for held, taken in copies:
-                    old = taken[pl.ds(to + CHUNK, CHUNK), :]
-                    new = held[pl.ds(at + CHUNK, CHUNK), :]
-                    taken[pl.ds(to + CHUNK, CHUNK), :] = jnp.where(sub < left - CHUNK, new, old)
-
-            return carry
-
-        lax.fori_loop(0, pairs, rest, 0)
-
-    query = query_ref[0]
-    clane = lax.broadcasted_iota(jnp.int32, (cands, LANES), 1)
-    queries = []
-    for p in range(2):
-        own = query[:, p * LANES : (p + 1) * LANES]
-        other = query[:, (1 - p) * LANES : (2 - p) * LANES].astype(F32)
-        other = jnp.where(clane == 0, 1.0, other).astype(BF)
-        queries.append(jnp.concatenate([own, other] if p == 0 else [other, own], axis=1))
-
-    def attend(live):
-        x = jnp.concatenate([x_left[:live, :], x_right[:live, :]], axis=1).astype(BF)
-        keys = lax.dot_general(wkt_scr[...], x, NT, preferred_element_type=F32)
-        keys = (keys.astype(BF).astype(F32) * 0.125).astype(BF)
-        values = jnp.dot(x, wv_ref[...], preferred_element_type=F32)
-        bias = jnp.concatenate(
-            [x_size[t : t + LANES, :].T[0:16, :] for t in range(0, live, LANES)], axis=1
-        )
-        slot = lax.broadcasted_iota(jnp.int32, (16, live), 1)
-        sub = lax.broadcasted_iota(jnp.int32, (16, live), 0)
-        bias = jnp.where(slot < valid, bias, -1e30)
-        bias = jnp.where(sub == 0, bias, 0.0).astype(BF)
-        lane = lax.broadcasted_iota(jnp.int32, (live, LANES), 1)
-        for h in range(HEADS):
-            half = slice((h // 2) * LANES, (h // 2 + 1) * LANES)
-            own = slice(h * head_size, (h + 1) * head_size)
-            other = (1 - h // 2) * LANES
-            mine = (lane // head_size) == (h % 2)
-            k_scr[h, own, :live] = keys[own, :]
-            k_scr[h, other : other + 16, :live] = bias
-            v_scr[h, :live, :LANES] = jnp.where(mine, values[:, half], 0.0).astype(BF)
-        for p in range(2):
-            total = None
-            for h in (2 * p, 2 * p + 1):
-                logits = jnp.dot(queries[p], k_scr[h, :, :live], preferred_element_type=F32)
-                top = jnp.max(logits, axis=1, keepdims=True)
-                probs = jnp.exp(logits - top).astype(BF)
-                part = jnp.dot(probs, v_scr[h, :live, :], preferred_element_type=F32)
-                total = part if total is None else total + part
-            ctx_scr[:, p * LANES : (p + 1) * LANES] = (
-                total[:, :LANES] / total[:, LANES:]
-            ).astype(BF)
-
-    blocks = slots // LANES
-    for n in range(1, blocks + 1):
-
-        @pl.when(jnp.logical_and(valid <= n * LANES, valid > (n - 1) * LANES))
-        def _(n=n):
-            attend(n * LANES)
-
-    group_rows(jnp.minimum(r + 1, reqs - 1))
-    attended = jnp.dot(ctx_scr[...], wo_ref[...], preferred_element_type=F32).astype(BF)
-    hidden = hidden_ref[0] + jnp.dot(attended, m1_ref[width:, :], preferred_element_type=F32)
-    hidden = jnp.maximum(hidden, 0.0).astype(BF)
-    hidden = jnp.dot(hidden, m2_ref[...], preferred_element_type=F32)
-    hidden = jnp.maximum(hidden + b2_ref[...], 0.0).astype(BF)
-    weight = sp_ref[...].astype(F32)
-    weight = jnp.concatenate([weight[n : n + 1, :] for n in range(width // LANES)], axis=1)
-    weight = jnp.broadcast_to(weight, (16, width)).astype(BF)
-    score = lax.dot_general(weight, hidden, NT, preferred_element_type=F32)[0:1, :]
-    slot = lax.broadcasted_iota(jnp.int32, (1, cands), 1)
-    score = jnp.where(slot < count, score, 0.0)
-    first = score.astype(BF).astype(F32)
-    second = score - first
-    row = row_ref[pl.ds(r, 1), :]
-    lines = out_ref.shape[0]
-    at_line = lax.broadcasted_iota(jnp.int32, (lines, cands), 0) == lax.shift_right_logical(row, 7)
-    at_lane = lax.broadcasted_iota(jnp.int32, (LANES, cands), 0) == (row & (LANES - 1))
-    at_lane = jnp.where(at_lane, 1.0, 0.0).astype(BF)
-    out_ref[...] += lax.dot_general(
-        jnp.where(at_line, first, 0.0).astype(BF), at_lane, NT, preferred_element_type=F32
-    ) + lax.dot_general(
-        jnp.where(at_line, second, 0.0).astype(BF), at_lane, NT, preferred_element_type=F32
-    )
+            slot = lax.broadcasted_iota(jnp.int32, (16, live), 1)
+            sub = lax.broadcasted_iota(jnp.int32, (16, live), 0)
+            bias = jnp.where(slot < valid, bias, -1e30)
+            bias = jnp.where(sub == 0, bias, 0.0).astype(BF)
+            lane = lax.broadcasted_iota(jnp.int32, (live, LANES), 1)
+            blank = jnp.zeros((head_size, live), BF)
+            for h in range(HEADS):
+                p, side = h // 2, h % 2
+                half = slice(p * LANES, (p + 1) * LANES)
+                own = keys[h * head_size : (h + 1) * head_size, :]
+                other = (1 - p) * LANES
+                span = slice(side * live, (side + 1) * live)
+                mine = (lane // head_size) == side
+                k_scr[p, half, span] = jnp.concatenate(
+                    [own, blank] if side == 0 else [blank, own], axis=0
+                )
+                k_scr[p, other : other + 16, span] = bias
+                v_scr[p, span, :LANES] = jnp.where(mine, values[:, half], 0.0).astype(BF)
+                v_scr[p, span, LANES:] = jnp.where(mine, 1.0, 0.0).astype(BF)
+            for p in range(2):
+                logits = jnp.dot(queries[p], k_scr[p, :, : 2 * live], preferred_element_type=F32)
+                probs = []
+                for side in range(2):
+                    part = logits[:, side * live : (side + 1) * live]
+                    top = jnp.max(part, axis=1, keepdims=True)
+                    probs.append(jnp.exp(part - top).astype(BF))
+                probs = jnp.concatenate(probs, axis=1)
+                total = jnp.dot(probs, v_scr[p, : 2 * live, :], preferred_element_type=F32)
+                ctx_scr[:, p * LANES : (p + 1) * LANES] = (
+                    total[:, :LANES] / total[:, LANES:]
+                ).astype(BF)
+
+        blocks = slots // LANES
+        for n in range(1, blocks + 1):
+
+            @pl.when(jnp.logical_and(count > 0, (valid + LANES - 1) // LANES == n))
+            def _(n=n):
+                attend(n * LANES)
+
+        following = jnp.minimum(r + 1, reqs - 1)
+
+        @pl.when(count <= 0)
+        def _():
+            group_rows(following)
+
+        @pl.when(count > 0)
+        def _():
+            group_rows(following)
+            attended = jnp.dot(ctx_scr[...], wo_ref[...], preferred_element_type=F32).astype(BF)
+            hidden = hidden_ref[r] + jnp.dot(attended, m1_ref[width:, :], preferred_element_type=F32)
+            hidden = jnp.maximum(hidden, 0.0).astype(BF)
+            hidden = jnp.dot(hidden, m2_ref[...], preferred_element_type=F32)
+            hidden = jnp.maximum(hidden + b2_ref[...], 0.0).astype(BF)
+            weight = sp_ref[...].astype(F32)
+            weight = jnp.concatenate([weight[n : n + 1, :] for n in range(width // LANES)], axis=1)
+            weight = jnp.broadcast_to(weight, (16, width)).astype(BF)
+            score = lax.dot_general(weight, hidden, NT, preferred_element_type=F32)[0:1, :]
+            slot = lax.broadcasted_iota(jnp.int32, (1, cands), 1)
+            score = jnp.where(slot < count, score, 0.0)
+            first = score.astype(BF).astype(F32)
+            second = score - first
+            row = row_ref[pl.ds(r, 1), :]
+            lines = out_ref.shape[0]
+            at_line = lax.broadcasted_iota(jnp.int32, (lines, cands), 0) == lax.shift_right_logical(row, 7)
+            at_lane = lax.broadcasted_iota(jnp.int32, (LANES, cands), 0) == (row & (LANES - 1))
+            at_lane = jnp.where(at_lane, 1.0, 0.0).astype(BF)
+            out_ref[...] += lax.dot_general(
+                jnp.where(at_line, first, 0.0).astype(BF), at_lane, NT, preferred_element_type=F32
+            ) + lax.dot_general(
+                jnp.where(at_line, second, 0.0).astype(BF), at_lane, NT, preferred_element_type=F32
+            )
+        return carry
+
+    lax.fori_loop(0, reqs, one_request, 0)
 
 
 def score(plan, per_pair, valid, count, sizes, arrived, queries, hidden, rows, weights, lines):
@@ -669,15 +702,9 @@
     taken = pltpu.VMEM((slots + 2 * CHUNK, LANES), F32)
     return pl.pallas_call(
         functools.partial(score_kernel, per_pair),
-        grid=(reqs,),
         out_shape=jax.ShapeDtypeStruct((lines, LANES), F32),
-        in_specs=[
-            pl.BlockSpec((1, cands, width), lambda r: (r, 0, 0)),
-            pl.BlockSpec((1,) + hidden.shape[1:], lambda r: (r, 0, 0)),
-            hbm,
-        ]
-        + [hbm] * len(loose),
-        out_specs=pl.BlockSpec((lines, LANES), lambda r: (0, 0)),
+        in_specs=[hbm] * (3 + len(loose)),
+        out_specs=pl.BlockSpec(memory_space=pltpu.VMEM),
         scratch_shapes=[
             pltpu.SMEM(plan.shape, jnp.int32),
             pltpu.VMEM(sizes.shape, F32),
@@ -693,11 +720,14 @@
             taken,
             taken,
             taken,
-            pltpu.VMEM((HEADS, width, slots), BF),
-            pltpu.VMEM((HEADS, slots, width), BF),
+            pltpu.VMEM((2, width, 2 * slots), BF),
+            pltpu.VMEM((2, 2 * slots, width), BF),
             pltpu.VMEM((cands, width), BF),
             pltpu.VMEM((width, width), BF),
+            pltpu.VMEM(queries.shape, BF),
+            pltpu.VMEM(hidden.shape, F32),
             pltpu.SemaphoreType.DMA((len(loose) + 4,)),
+            pltpu.SemaphoreType.DMA((2, reqs)),
         ],
         compiler_params=pltpu.CompilerParams(vmem_limit_bytes=VMEM_LIMIT),
         cost_estimate=pl.CostEstimate(

time: 89.3 us -> 85.4 us (0.956)
  Pallas kernels: 87.6 us -> 84.4 us
    pallas_call x1, Pallas kernels: 25.3 us -> 15.1 us  [score(): pl.pallas_call(functools.partial(score_kernel, per_pair), out_shape=jax.S...]
    pallas_call x1, Pallas kernels: 12.4 us -> 19.5 us  [gather_spans(): pl.pallas_call(functools.partial(gather_kernel, scorers), out_shape=jax.S...]
where the time goes in v8:
time: 85.4 us; the launch traced here: 86 us
  Pallas kernels  84.4 us (99%)
  local copies, waits for them, and re-layouts  0.9 us (1%)
    pallas_call x1, Pallas kernels, fetch(): pl.pallas_call(functools.partial(fetch_kernel, stores, scorers, per_pair)...  49.8 us
    pallas_call x1, Pallas kernels, gather_spans(): pl.pallas_call(functools.partial(gather_kernel, scorers), out_shape=jax.S...  19.5 us
    pallas_call x1, Pallas kernels, score(): pl.pallas_call(functools.partial(score_kernel, per_pair), out_shape=jax.S...  15.1 us

profile of v8, /device:TPU:0, one launch (start us, length us, event | category | flops | bytes accessed | tf_op | source)
XLA Modules:
  0.0 86.0 jit_solution(5061214727324030211)
XLA Ops:
  0.0 49.8 %fetch.1 = (bf16[128,32,256]{2,1,0:T(8,128)(2,1)}, f32[128,1,128]{2,1,0:T(1,128)}, s32[32,128]{1,0:T(8,128)}, bf16[8,512,256]{2,1,0:T(8,128)(2,1)}, f32[8,512,512]{2,1,0:T(8,128)}) custom-call(s32[8,512]{1,0:T(8,128)} %ids_hbm.1, s32[8]{0:T(128)} %rest_2_.1, s32[2048,128]{1,0:T(8,128)} %bitcast.10, bf16[2048,256]{1,0:T(8,128)(2,1)} %store_hbm.1, ...), custom_call_target="tpu_custom_call" | custom-call | flops 40000000000 | bytes 8388608 | tf_op jit(solution)/shard_map/fetch/pallas_call | solution.py:348
  49.8 15.1 %score.1 = f32[256,128]{1,0:T(8,128)} custom-call(bf16[8,512,256]{2,1,0:T(8,128)(2,1)} %get-tuple-element.10.query_hbm, f32[8,512,512]{2,1,0:T(8,128)} %get-tuple-element.11.hidden_hbm, bf16[4096,256]{1,0:T(8,128)(2,1)} %bitcast.15, s32[32,128]{1,0:T(8,128)} %get-tuple-element.13.rest_0_, f32[128,128]{1,0:T(8,128)} %bitcast.16, s32[8]{0:T(128)} %rest_2_.1, ...), custom_call_target="tpu_custom_call" | custom-call | flops 30000001024 | bytes 8388608 | tf_op jit(solution)/shard_map/score/pallas_call | solution.py:703
  64.9 0.0 copy-start
  64.9 0.9 %copy-done = f32[256,128]{1,0:T(8,128)S(1)} copy-done((f32[256,128]{1,0:T(8,128)S(1)}, f32[256,128]{1,0:T(8,128)}, u32[]{:S(2)}) %copy-start) | copy-done | bytes 131096
  65.8 19.5 %gather_spans.1 = f32[16,16,128]{2,1,0:T(8,128)S(1)} custom-call(f32[16,16,128]{2,1,0:T(8,128)S(1)} %bitcast.9), custom_call_target="tpu_custom_call" | custom-call | tf_op jit(solution)/shard_map/gather_spans/pallas_call | solution.py:442
  85.4 0.6 reduce_sum.9
Async XLA Ops:
  64.9 0.9 %copy-start = (f32[256,128]{1,0:T(8,128)S(1)}, f32[256,128]{1,0:T(8,128)}, u32[]{:S(2)}) copy-start(f32[256,128]{1,0:T(8,128)} %score.1) | copy-start | bytes 393220
